TPU v7x, 512 devices: a whole 4x4x16 slice. The times are simulated.
512 devices in a mesh: leaf: 64 (over z, y), front: 8 (over x, core).
Axes of the slice: x: 4, y: 4, z: 16, core: 2. Of those that a mesh axis runs over, the one named last changes fastest.
Arguments:
- top_factor: float32 [1408, 2816], P('front', 'leaf'), may hold values from -1 to 3
- panel_two: float32 [1408, 5632], P('front', 'leaf'), may hold values from -0.109375 to 0.109375
- panel_three: float32 [1408, 11264], P('front', 'leaf'), may hold values from -0.109375 to 0.109375
- panel_four: float32 [1408, 22528], P('front', 'leaf'), may hold values from -0.109375 to 0.109375
- factor_two: float32 [1408, 5632], P('front', 'leaf'), may hold values from -1 to 3
- factor_three: float32 [1408, 11264], P('front', 'leaf'), may hold values from -1 to 3
- factor_four: float32 [1408, 22528], P('front', 'leaf'), may hold values from -1 to 3
Outputs:
- cov_one: float32 [1408, 2816], P('front', 'leaf')
- cross_two: float32 [1408, 5632], P('front', 'leaf')
- cov_two: float32 [1408, 5632], P('front', 'leaf')
- cross_three: float32 [1408, 11264], P('front', 'leaf')
- cov_three: float32 [1408, 11264], P('front', 'leaf')
- cross_four: float32 [1408, 22528], P('front', 'leaf')
- cov_four: float32 [1408, 22528], P('front', 'leaf')
All inputs are finite; a program needn't handle non-finite values.
Results may differ from a plain program's by a relative error of at most 0.000088.
Values sent between devices are 32-bit elements; how exact they have to be, the bound alone decides.
No kernel may reach another device: no remote copies, remote signals or barrier semaphores. Data moves between devices by JAX's collectives and lax.ppermute only.
A program may use at most 64 MiB of HBM per device.

v0:
```python
import functools

import jax
import jax.numpy as jnp
from jax import lax
from jax.experimental import pallas as pl
from jax.experimental.pallas import tpu as pltpu
from jax.sharding import PartitionSpec as P

Y = 4
XS = 4
CORES = 2
VMEM_BYTES = 48 * 1024 * 1024


def split(value):
    high = value.astype(jnp.bfloat16)
    low = (value - high.astype(jnp.float32)).astype(jnp.bfloat16)
    return high, low


def product(first, second):
    (fh, fl), (sh, sl) = first, second
    run = functools.partial(jnp.dot, preferred_element_type=jnp.float32)
    return run(fh, sh) + (run(fh, sl) + run(fl, sh))


def join(where_ref, own_ref, got_ref, p4_ref, f4_ref, f1_ref, rows_ref, p2_ref, columns_ref):
    z = where_ref[2]
    pieces = []
    for plane in range(8):
        distance = plane ^ z
        at, far = ((distance >> 1) & 1) * 3 + 2, (distance >> 2) == 1
        both = jnp.where((distance & 1) == 0, own_ref[at], got_ref[at])
        pieces.append(jnp.where(far, both[44:], both[:44]))
    f1_ref[...] = jnp.concatenate(pieces, 0).T
    for which in range(2):
        pieces = []
        for plane in range(4):
            distance = plane ^ (z % 4)
            at = (distance >> 1) * 3 + which
            pieces.append(jnp.where((distance & 1) == 0, own_ref[at], got_ref[at]))
        tile = jnp.concatenate(pieces, 0).T
        rows_ref[which] = tile
        if which == 0:
            p2_ref[...] = tile
    for which in range(2):
        pieces = []
        for plane in range(2):
            near = plane == (z % 2)
            for at in (6 + 2 * which, 7 + 2 * which):
                pieces.append(jnp.where(near, own_ref[at], got_ref[at]))
        tile = jnp.concatenate(pieces, 0).T
        rows_ref[2 + which] = tile
        if which == 0:
            columns_ref[0] = tile
    rows_ref[4] = p4_ref[...]
    rows_ref[5] = f4_ref[...]
    columns_ref[1] = p4_ref[...]


def share_terms(where_ref, planes, tiles, factors, other_ref, mine_ref):
    x, core = where_ref[0], where_ref[1]
    width = factors[0][0].shape[1] // planes
    step = min(width, 176)
    for y in range(Y):
        total = None
        for tile, factor in zip(tiles, factors):
            term = product(split(tile(y).T), factor)
            total = term if total is None else total + term
        for plane in range(planes):
            for part in range(0, width, step):
                column = (plane * Y + y) * width + part
                block, offset = column // 176, column % 176
                value = total[plane * width + part : plane * width + part + step]
                at = (block // CORES - x) % XS
                same = core == (block % CORES)

                @pl.when(same)
                def _():
                    mine_ref[at, offset : offset + step, :] = value

                @pl.when(jnp.logical_not(same))
                def _():
                    other_ref[at, offset : offset + step, :] = value


def top_terms(where_ref, rows_ref, own_ref, other_ref, mine_ref):
    factors = [split(own_ref[...])]
    share_terms(where_ref, 8, [lambda y: rows_ref[y]], factors, other_ref, mine_ref)


def level_terms(planes, where_ref, parent_ref, *refs):
    *column_refs, rows_ref, own_ref, cross_ref, other_ref, mine_ref = refs
    x, core = where_ref[0], where_ref[1]
    parts, width = planes * 2, own_ref.shape[-1] // (planes * 2)

    def columns(start, count):
        block, offset = start // 176, start % 176
        if len(column_refs) == 1:
            return column_refs[0][block, 0, offset : offset + count, :]
        step = (block // CORES - x) % XS
        same = core == (block % CORES)
        mine = column_refs[0][step, offset : offset + count, :]
        theirs = column_refs[1][step, offset : offset + count, :]
        return jnp.where(same, mine, theirs)

    total = None
    for y in range(Y):
        rows = [columns((p * Y + y) * width, width) for p in range(parts)]
        term = product(split(parent_ref[y]), split(jnp.concatenate(rows, 0)))
        total = term if total is None else total + term
    cross_ref[...] = -total
    tiles = [lambda y: rows_ref[y, 0], lambda y: rows_ref[y, 1]]
    factors = [split(total), split(own_ref[0])]
    share_terms(where_ref, planes, tiles, factors, other_ref, mine_ref)


def add_pieces(mine_ref, got_ref, *out_refs):
    for step, out_ref in enumerate(out_refs):
        out_ref[...] = mine_ref[step] + got_ref[step]


def local(top_factor, panel_two, panel_three, panel_four, factor_two, factor_three, factor_four):
    leaves = lax.axis_size("leaf")
    fronts = lax.axis_size("front")
    share = top_factor.shape[0]
    width = panel_four.shape[1]
    leaf = lax.axis_index("leaf")
    front = lax.axis_index("front")
    z, x, core = leaf // Y, front // CORES, front % CORES
    where = jnp.stack([x, core, z % 8]).astype(jnp.int32)
    y_groups = [list(range(i, i + Y)) for i in range(0, leaves, Y)]

    def from_plane(value, distance):
        pairs = [(i, ((i // Y) ^ distance) * Y + i % Y) for i in range(leaves)]
        return lax.ppermute(value, "leaf", pairs)

    def from_core(value):
        return lax.ppermute(value, "front", [(i, i ^ 1) for i in range(fronts)])

    def shift_x(value, distance):
        pairs = [
            (i, (i // CORES + distance) % XS * CORES + i % CORES) for i in range(fronts)
        ]
        return lax.ppermute(value, "front", pairs)

    def y_gather(value):
        return lax.all_gather(value, "leaf", axis=0, axis_index_groups=y_groups)

    tile = jax.ShapeDtypeStruct((share, width), jnp.float32)
    tiles = jax.ShapeDtypeStruct((XS, share, width), jnp.float32)
    scalars = pl.BlockSpec(memory_space=pltpu.SMEM)

    def full(value):
        return pl.BlockSpec(value.shape, lambda i: (0,) * len(value.shape))

    def call(kernel, out_shape, in_specs, flops, *args):
        many = isinstance(out_shape, (tuple, list))
        specs = [full(o) for o in (out_shape if many else [out_shape])]
        return pl.pallas_call(
            kernel,
            out_shape=out_shape,
            grid=(1,),
            in_specs=in_specs,
            out_specs=specs if many else specs[0],
            compiler_params=pltpu.CompilerParams(vmem_limit_bytes=VMEM_BYTES),
            cost_estimate=pl.CostEstimate(
                flops=flops, bytes_accessed=8_000_000, transcendentals=0
            ),
        )(*args)

    def front_total(other, mine):
        got = from_core(other)
        pieces = call(add_pieces, [tile] * XS, [full(tiles)] * 2, 1_000_000, mine, got)
        total = pieces[0]
        for distance in (1, 3, 2):
            total = total + shift_x(pieces[distance], distance)
        return total

    half = share // 2
    first = top_factor.T
    stack = functools.partial(jax.ShapeDtypeStruct, dtype=jnp.float32)

    def turn(p2_ref, f2_ref, p3_ref, f3_ref, own_ref, got_ref, two_ref, three_ref):
        two_ref[0] = p2_ref[...].T
        two_ref[1] = f2_ref[...].T
        two_ref[2] = jnp.concatenate([own_ref[...], got_ref[...]], 0)
        for which, ref in enumerate((p3_ref, f3_ref)):
            turned = ref[...].T
            for part in range(2):
                three_ref[2 * which + part] = turned[part * half : (part + 1) * half]

    raw = [panel_two, factor_two, panel_three, factor_three, first, from_plane(first, 4)]
    two, three = call(
        turn,
        [stack((3, half, share)), stack((4, half, share))],
        [full(v) for v in raw],
        1_000_000,
        *raw,
    )
    near = jnp.concatenate([two, from_plane(two, 2), three], 0)
    got = from_plane(near, 1)
    f1, deep, p2, columns_in = call(
        join,
        [tile, stack((6, share, width)), tile, stack((2, share, width))],
        [scalars, full(near), full(got), full(tile), full(tile)],
        1_000_000,
        where,
        near,
        got,
        panel_four,
        factor_four,
    )
    rows = y_gather(deep)
    panels = lax.all_gather(columns_in, "front", axis=0)
    near = jnp.stack([p2] + [shift_x(p2, (XS - d) % XS) for d in range(1, XS)])
    far = from_core(near)

    work = 6 * share * share * XS * width
    other, mine = call(
        top_terms,
        [tiles, tiles],
        [scalars, full(tiles), full(tile)],
        2 * work,
        where,
        y_gather(f1),
        f1,
    )
    parent = front_total(other, mine)

    def own(value, planes):
        part = width // planes
        return lax.dynamic_slice_in_dim(value, (z % planes) * part, part, 1)

    results = [own(parent, 8)]
    for level, planes in enumerate((4, 2, 1)):
        row_spec = pl.BlockSpec((Y, 2, share, width), lambda i, n=level: (0, n, 0, 0))
        own_spec = pl.BlockSpec((1, share, width), lambda i, n=level: (2 * n + 1, 0, 0))
        if level == 0:
            columns, column_specs = [near, far], [full(tiles)] * 2
        else:
            columns = [panels]
            column_specs = [
                pl.BlockSpec((fronts, 1, share, width), lambda i, n=level: (0, n - 1, 0, 0))
            ]
        cross, other, mine = call(
            functools.partial(level_terms, planes),
            [tile, tiles, tiles],
            [scalars, full(tiles), *column_specs, row_spec, own_spec],
            4 * work,
            where,
            y_gather(parent),
            *columns,
            rows,
            deep,
        )
        parent = front_total(other, mine)
        results.append(own(cross, planes))
        results.append(own(parent, planes))
    return tuple(results)


def solution(mesh):
    spec = P("front", "leaf")
    return jax.shard_map(
        local, mesh=mesh, in_specs=(spec,) * 7, out_specs=(spec,) * 7, check_vma=False
    )
```

profile of v0, /device:TPU:6, one launch (start us, length us, event | category | flops | bytes accessed | tf_op | source)
XLA Modules:
  0.0 284.2 jit_solution(3387843636070888087)
XLA Ops:
  7.2 9.1 %collective-permute-start = (f32[44,176]{1,0:T(8,128)}, f32[44,176]{1,0:T(8,128)S(1)}, u32[]{:S(2)}, u32[]{:S(2)}) collective-permute-start(f32[44,176]{1,0:T(8,128)} %bitcast.19), channel_id=1, source_target_pairs={{0,128},{8,136},{16,144},{24,152},{32,160},{40,168},{48,176},{56,1... | collective-permute-start | bytes 92936 | tf_op jit(solution)/shard_map/ppermute | solution.py:137
  16.3 2.3 collective-permute-done.got_ref
  18.6 0.9 copy-done.2
  19.5 0.9 copy-done.3
  20.4 0.9 copy-done.4
  21.3 0.9 copy-done.5
  22.2 0.8 copy-done.6
  23.0 0.3 shard_map.126
  23.3 5.6 %collective-permute-start.1 = (f32[3,88,176]{2,1,0:T(8,128)S(1)}, f32[3,88,176]{2,1,0:T(8,128)S(1)}, u32[]{:S(2)}, u32[]{:S(2)}) collective-permute-start(f32[3,88,176]{2,1,0:T(8,128)S(1)} %get-tuple-element.40), channel_id=1, source_target_pairs={{0,64},{8,72},{16,80},{24,88},{32,96},{40,104},{48,112},{56,120},{... | collective-permute-start | bytes 557576 | tf_op jit(solution)/shard_map/ppermute | solution.py:137
  28.9 12.4 %collective-permute-done.1 = f32[3,88,176]{2,1,0:T(8,128)S(1)} collective-permute-done((f32[3,88,176]{2,1,0:T(8,128)S(1)}, f32[3,88,176]{2,1,0:T(8,128)S(1)}, u32[]{:S(2)}, u32[]{:S(2)}) %collective-permute-start.1) | collective-permute-done | bytes 185888 | tf_op jit(solution)/shard_map/ppermute | solution.py:137
  41.4 2.6 collective-permute-start.2
  44.1 20.5 %collective-permute-done.2.got_ref = f32[10,88,176]{2,1,0:T(8,128)S(1)} collective-permute-done((f32[10,88,176]{2,1,0:T(8,128)S(1)}, f32[10,88,176]{2,1,0:T(8,128)S(1)}, u32[]{:S(2)}, u32[]{:S(2)}) %collective-permute-start.2) | collective-permute-done | bytes 619552 | tf_op jit(solution)/shard_map/ppermute | solution.py:137
  64.6 2.5 shard_map.127
  67.2 0.7 all-gather.11.cloned.1.call-update
  67.9 15.1 %all-gather = f32[704,352]{1,0:T(8,128)S(1)} all-gather(f32[176,352]{1,0:T(8,128)S(1)} %get-tuple-element.42.own_ref), channel_id=2, replica_groups={{0,8,16,24},{32,40,48,56},{64,72,80,88},{96,104,112,120},{128,136,144,1..., dimensions={0}, use_global_device_ids=true | all-gather | bytes 1239040 | tf_op jit(solution)/shard_map/all_gather | solution.py:149
  83.1 2.9 %shard_map.128 = (f32[4,176,352]{2,1,0:T(8,128)S(1)}, f32[4,176,352]{2,1,0:T(8,128)S(1)}) custom-call(s32[3]{0:T(128)S(1)} %pad_add_fusion.where_ref, f32[4,176,352]{2,1,0:T(8,128)S(1)} %bitcast.17, f32[176,352]{1,0:T(8,128)S(1)} %get-tuple-element.42.own_ref), custom_call_target="tpu_custom_call" | custom-call | flops 523370496 | bytes 8000000 | tf_op jit(solution)/shard_map/pallas_call | solution.py:161
  85.9 1.9 collective-permute-start.3
  87.9 2.4 collective-permute-start.9
  90.3 4.3 %collective-permute-start.8 = (f32[176,352]{1,0:T(8,128)S(1)}, f32[176,352]{1,0:T(8,128)S(1)}, u32[]{:S(2)}, u32[]{:S(2)}) collective-permute-start(f32[176,352]{1,0:T(8,128)S(1)} %get-tuple-element.49), channel_id=1, source_target_pairs={{0,4},{1,5},{2,6},{3,7},{4,0},{5,1},{6,2},{7,3},{8,12},{9,13},{10,... | collective-permute-start | bytes 743432 | tf_op jit(solution)/shard_map/ppermute | solution.py:146
  94.6 1.9 collective-permute-start.7
  96.5 2.5 collective-permute-done.9
  99.0 3.9 %collective-permute-done.8 = f32[176,352]{1,0:T(8,128)S(1)} collective-permute-done((f32[176,352]{1,0:T(8,128)S(1)}, f32[176,352]{1,0:T(8,128)S(1)}, u32[]{:S(2)}, u32[]{:S(2)}) %collective-permute-start.8) | collective-permute-done | bytes 247840 | tf_op jit(solution)/shard_map/ppermute | solution.py:146
  103.0 5.1 %collective-permute-done.7 = f32[176,352]{1,0:T(8,128)S(1)} collective-permute-done((f32[176,352]{1,0:T(8,128)S(1)}, f32[176,352]{1,0:T(8,128)S(1)}, u32[]{:S(2)}, u32[]{:S(2)}) %collective-permute-start.7) | collective-permute-done | bytes 247840 | tf_op jit(solution)/shard_map/ppermute | solution.py:146
  108.1 2.0 collective-permute-start.10
  110.3 4.4 %collective-permute-start.6 = (f32[176,352]{1,0:T(8,128)S(1)}, f32[176,352]{1,0:T(8,128)S(1)}, u32[]{:S(2)}, u32[]{:S(2)}) collective-permute-start(f32[176,352]{1,0:T(8,128)S(1)} %get-tuple-element.48), channel_id=1, source_target_pairs={{0,4},{1,5},{2,6},{3,7},{4,0},{5,1},{6,2},{7,3},{8,12},{9,13},{10,... | collective-permute-start | bytes 743432 | tf_op jit(solution)/shard_map/ppermute | solution.py:146
  114.7 1.9 collective-permute-start.5
  116.6 5.1 %collective-permute-start.4 = (f32[176,352]{1,0:T(8,128)S(1)}, f32[176,352]{1,0:T(8,128)S(1)}, u32[]{:S(2)}, u32[]{:S(2)}) collective-permute-start(f32[176,352]{1,0:T(8,128)S(1)} %get-tuple-element.46), channel_id=1, source_target_pairs={{0,2},{1,3},{2,4},{3,5},{4,6},{5,7},{6,0},{7,1},{8,10},{9,11},{10,... | collective-permute-start | bytes 743432 | tf_op jit(solution)/shard_map/ppermute | solution.py:146
  121.7 1.3 collective-permute-done.6
  123.0 5.2 %collective-permute-done.5 = f32[176,352]{1,0:T(8,128)S(1)} collective-permute-done((f32[176,352]{1,0:T(8,128)S(1)}, f32[176,352]{1,0:T(8,128)S(1)}, u32[]{:S(2)}, u32[]{:S(2)}) %collective-permute-start.5) | collective-permute-done | bytes 247840 | tf_op jit(solution)/shard_map/ppermute | solution.py:146
  128.4 22.5 %all-gather.1 = f32[704,352]{1,0:T(8,128)S(1)} all-gather(f32[176,352]{1,0:T(8,128)S(1)} %add_add_fusion.3), channel_id=3, replica_groups={{0,8,16,24},{32,40,48,56},{64,72,80,88},{96,104,112,120},{128,136,144,1..., dimensions={0}, use_global_device_ids=true | all-gather | bytes 1239040 | tf_op jit(solution)/shard_map/all_gather | solution.py:149
  150.8 0.6 all-gather.9.cloned.1.call-done
  151.4 6.2 %shard_map.130 = (f32[176,352]{1,0:T(8,128)S(1)}, f32[4,176,352]{2,1,0:T(8,128)S(1)}, f32[4,176,352]{2,1,0:T(8,128)S(1)}) custom-call(s32[3]{0:T(128)S(1)} %pad_add_fusion.where_ref, f32[4,176,352]{2,1,0:T(8,128)S(1)} %bitcast.14, f32[4,176,352]{2,1,0:T(8,128)S(1)} %pad_maximum_fusion.refs_0_, f32[4,176,352]{2,1,0:T(8,128)S(1)} %collective-permute-done.10.refs_1_, ...), custom_call_target="tpu_custom_call" | custom-call | flops 1046740992 | bytes 8000000 | tf_op jit(solution)/shard_map/pallas_call | solution.py:161
  157.6 1.9 collective-permute-start.11
  159.5 2.7 collective-permute-done.11.got_ref
  162.4 3.1 %collective-permute-start.14 = (f32[176,352]{1,0:T(8,128)S(1)}, f32[176,352]{1,0:T(8,128)S(1)}, u32[]{:S(2)}, u32[]{:S(2)}) collective-permute-start(f32[176,352]{1,0:T(8,128)S(1)} %get-tuple-element.57), channel_id=1, source_target_pairs={{0,4},{1,5},{2,6},{3,7},{4,0},{5,1},{6,2},{7,3},{8,12},{9,13},{10,... | collective-permute-start | bytes 743432 | tf_op jit(solution)/shard_map/ppermute | solution.py:146
  165.4 1.9 collective-permute-start.13
  167.4 5.1 %collective-permute-start.12 = (f32[176,352]{1,0:T(8,128)S(1)}, f32[176,352]{1,0:T(8,128)S(1)}, u32[]{:S(2)}, u32[]{:S(2)}) collective-permute-start(f32[176,352]{1,0:T(8,128)S(1)} %get-tuple-element.55), channel_id=1, source_target_pairs={{0,2},{1,3},{2,4},{3,5},{4,6},{5,7},{6,0},{7,1},{8,10},{9,11},{10,... | collective-permute-start | bytes 743432 | tf_op jit(solution)/shard_map/ppermute | solution.py:146
  172.5 3.0 %collective-permute-done.14 = f32[176,352]{1,0:T(8,128)S(1)} collective-permute-done((f32[176,352]{1,0:T(8,128)S(1)}, f32[176,352]{1,0:T(8,128)S(1)}, u32[]{:S(2)}, u32[]{:S(2)}) %collective-permute-start.14) | collective-permute-done | bytes 247840 | tf_op jit(solution)/shard_map/ppermute | solution.py:146
  175.5 10.1 %collective-permute-done.13 = f32[176,352]{1,0:T(8,128)S(1)} collective-permute-done((f32[176,352]{1,0:T(8,128)S(1)}, f32[176,352]{1,0:T(8,128)S(1)}, u32[]{:S(2)}, u32[]{:S(2)}) %collective-permute-start.13) | collective-permute-done | bytes 247840 | tf_op jit(solution)/shard_map/ppermute | solution.py:146
  185.7 14.8 %all-gather.3 = f32[704,352]{1,0:T(8,128)S(1)} all-gather(f32[176,352]{1,0:T(8,128)S(1)} %add_add_fusion.2), channel_id=5, replica_groups={{0,8,16,24},{32,40,48,56},{64,72,80,88},{96,104,112,120},{128,136,144,1..., dimensions={0}, use_global_device_ids=true | all-gather | bytes 1239040 | tf_op jit(solution)/shard_map/all_gather | solution.py:149
  200.5 6.9 %shard_map.132 = (f32[176,352]{1,0:T(8,128)S(1)}, f32[4,176,352]{2,1,0:T(8,128)S(1)}, f32[4,176,352]{2,1,0:T(8,128)S(1)}) custom-call(s32[3]{0:T(128)S(1)} %pad_add_fusion.where_ref, f32[4,176,352]{2,1,0:T(8,128)S(1)} %bitcast.15, f32[8,2,176,352]{3,2,1,0:T(8,128)} %bitcast.24, f32[4,6,176,352]{3,2,1,0:T(8,128)} %bitcast.22, ...), custom_call_target="tpu_custom_call" | custom-call | flops 1046740992 | bytes 8000000 | tf_op jit(solution)/shard_map/pallas_call | solution.py:161
  207.4 1.9 collective-permute-start.15
  209.4 2.7 collective-permute-done.15.got_ref
  212.2 5.1 %collective-permute-start.18 = (f32[176,352]{1,0:T(8,128)S(1)}, f32[176,352]{1,0:T(8,128)S(1)}, u32[]{:S(2)}, u32[]{:S(2)}) collective-permute-start(f32[176,352]{1,0:T(8,128)S(1)} %get-tuple-element.65), channel_id=1, source_target_pairs={{0,4},{1,5},{2,6},{3,7},{4,0},{5,1},{6,2},{7,3},{8,12},{9,13},{10,... | collective-permute-start | bytes 743432 | tf_op jit(solution)/shard_map/ppermute | solution.py:146
  217.3 2.4 collective-permute-start.17
  219.7 4.7 %collective-permute-start.16 = (f32[176,352]{1,0:T(8,128)S(1)}, f32[176,352]{1,0:T(8,128)S(1)}, u32[]{:S(2)}, u32[]{:S(2)}) collective-permute-start(f32[176,352]{1,0:T(8,128)S(1)} %get-tuple-element.63), channel_id=1, source_target_pairs={{0,2},{1,3},{2,4},{3,5},{4,6},{5,7},{6,0},{7,1},{8,10},{9,11},{10,... | collective-permute-start | bytes 743432 | tf_op jit(solution)/shard_map/ppermute | solution.py:146
  224.4 0.5 collective-permute-done.18
  224.9 5.0 %collective-permute-done.17 = f32[176,352]{1,0:T(8,128)S(1)} collective-permute-done((f32[176,352]{1,0:T(8,128)S(1)}, f32[176,352]{1,0:T(8,128)S(1)}, u32[]{:S(2)}, u32[]{:S(2)}) %collective-permute-start.17) | collective-permute-done | bytes 247840 | tf_op jit(solution)/shard_map/ppermute | solution.py:146
  230.2 15.0 %all-gather.5 = f32[704,352]{1,0:T(8,128)S(1)} all-gather(f32[176,352]{1,0:T(8,128)S(1)} %add_add_fusion.1), channel_id=7, replica_groups={{0,8,16,24},{32,40,48,56},{64,72,80,88},{96,104,112,120},{128,136,144,1..., dimensions={0}, use_global_device_ids=true | all-gather | bytes 1239040 | tf_op jit(solution)/shard_map/all_gather | solution.py:149
  245.2 7.8 %shard_map.134 = (f32[176,352]{1,0:T(8,128)}, f32[4,176,352]{2,1,0:T(8,128)}, f32[4,176,352]{2,1,0:T(8,128)S(1)}) custom-call(s32[3]{0:T(128)S(1)} %pad_add_fusion.where_ref, f32[4,176,352]{2,1,0:T(8,128)S(1)} %bitcast.16, f32[8,2,176,352]{3,2,1,0:T(8,128)} %bitcast.25, f32[4,6,176,352]{3,2,1,0:T(8,128)} %bitcast.23, ...), custom_call_target="tpu_custom_call" | custom-call | flops 1046740992 | bytes 8000000 | tf_op jit(solution)/shard_map/pallas_call | solution.py:161
  252.9 1.9 collective-permute-start.19
  254.9 1.0 constant_dynamic-slice_fusion.4
  255.9 0.7 copy.15
  256.6 0.7 constant_dynamic-slice_fusion.3
  257.4 0.4 collective-permute-done.19.got_ref
  257.9 5.4 %collective-permute-start.22 = (f32[176,352]{1,0:T(8,128)S(1)}, f32[176,352]{1,0:T(8,128)S(1)}, u32[]{:S(2)}, u32[]{:S(2)}) collective-permute-start(f32[176,352]{1,0:T(8,128)S(1)} %get-tuple-element.72), channel_id=1, source_target_pairs={{0,4},{1,5},{2,6},{3,7},{4,0},{5,1},{6,2},{7,3},{8,12},{9,13},{10,... | collective-permute-start | bytes 743432 | tf_op jit(solution)/shard_map/ppermute | solution.py:146
  263.3 2.9 %collective-permute-start.21 = (f32[176,352]{1,0:T(8,128)S(1)}, f32[176,352]{1,0:T(8,128)S(1)}, u32[]{:S(2)}, u32[]{:S(2)}) collective-permute-start(f32[176,352]{1,0:T(8,128)S(1)} %get-tuple-element.71), channel_id=1, source_target_pairs={{0,6},{1,7},{2,0},{3,1},{4,2},{5,3},{6,4},{7,5},{8,14},{9,15},{10,... | collective-permute-start | bytes 743432 | tf_op jit(solution)/shard_map/ppermute | solution.py:146
  266.2 4.1 %collective-permute-start.20 = (f32[176,352]{1,0:T(8,128)S(1)}, f32[176,352]{1,0:T(8,128)S(1)}, u32[]{:S(2)}, u32[]{:S(2)}) collective-permute-start(f32[176,352]{1,0:T(8,128)S(1)} %get-tuple-element.70), channel_id=1, source_target_pairs={{0,2},{1,3},{2,4},{3,5},{4,6},{5,7},{6,0},{7,1},{8,10},{9,11},{10,... | collective-permute-start | bytes 743432 | tf_op jit(solution)/shard_map/ppermute | solution.py:146
  270.3 0.7 constant_dynamic-slice_fusion.2
  271.1 0.8 constant_dynamic-slice_fusion.1
  271.9 0.8 constant_dynamic-slice_fusion
  272.7 3.2 %collective-permute-done.21 = f32[176,352]{1,0:T(8,128)S(1)} collective-permute-done((f32[176,352]{1,0:T(8,128)S(1)}, f32[176,352]{1,0:T(8,128)S(1)}, u32[]{:S(2)}, u32[]{:S(2)}) %collective-permute-start.21) | collective-permute-done | bytes 247840 | tf_op jit(solution)/shard_map/ppermute | solution.py:146
  275.8 0.7 collective-permute-done.20
  276.6 0.8 add_add_fusion
  (33 shorter events, 1.3 us)
Async XLA Ops:
  7.2 144.3 %all-gather.9.cloned.1.call-start = ((), (), s32[]{:S(2)}) async-start(), calls=%async_computation | async-start | bytes 8110080 | tf_op jit(solution)/shard_map/all_gather | solution.py:149
  7.2 11.4 %collective-permute-start = (f32[44,176]{1,0:T(8,128)}, f32[44,176]{1,0:T(8,128)S(1)}, u32[]{:S(2)}, u32[]{:S(2)}) collective-permute-start(f32[44,176]{1,0:T(8,128)} %bitcast.19), channel_id=1, source_target_pairs={{0,128},{8,136},{16,144},{24,152},{32,160},{40,168},{48,176},{56,1... | collective-permute-start | bytes 92936 | tf_op jit(solution)/shard_map/ppermute | solution.py:137
  18.6 0.9 copy-start.2
  19.5 0.9 copy-start.3
  20.4 0.9 copy-start.4
  21.3 0.9 copy-start.5
  22.2 0.8 copy-start.6
  23.3 41.4 %copy-start = (f32[176,352]{1,0:T(8,128)S(1)}, f32[176,352]{1,0:T(8,128)}, u32[]{:S(2)}) copy-start(f32[176,352]{1,0:T(8,128)} %p4_ref.1) | copy-start | bytes 743428
  23.3 41.4 %copy-start.1 = (f32[176,352]{1,0:T(8,128)S(1)}, f32[176,352]{1,0:T(8,128)}, u32[]{:S(2)}) copy-start(f32[176,352]{1,0:T(8,128)} %f4_ref.1) | copy-start | bytes 743428
  23.3 18.0 %collective-permute-start.1 = (f32[3,88,176]{2,1,0:T(8,128)S(1)}, f32[3,88,176]{2,1,0:T(8,128)S(1)}, u32[]{:S(2)}, u32[]{:S(2)}) collective-permute-start(f32[3,88,176]{2,1,0:T(8,128)S(1)} %get-tuple-element.40), channel_id=1, source_target_pairs={{0,64},{8,72},{16,80},{24,88},{32,96},{40,104},{48,112},{56,120},{... | collective-permute-start | bytes 557576 | tf_op jit(solution)/shard_map/ppermute | solution.py:137
  41.4 23.3 %collective-permute-start.2 = (f32[10,88,176]{2,1,0:T(8,128)S(1)}, f32[10,88,176]{2,1,0:T(8,128)S(1)}, u32[]{:S(2)}, u32[]{:S(2)}) collective-permute-start(f32[10,88,176]{2,1,0:T(8,128)S(1)} %constant_dynamic-update-slice_fusion.own_ref), channel_id=1, source_target_pairs={{0,32},{8,40},{16,48},{24,56},{32,0},{40,8},{48,16},{56,24},{64,96... | collective-permute-start | bytes 1858568 | tf_op jit(solution)/shard_map/ppermute | solution.py:137
  67.2 133.3 %all-gather.11.cloned.1.call-start = ((), (), s32[]{:S(2)}) async-start(), calls=%async_computation.1 | async-start | bytes 4866048 | tf_op jit(solution)/shard_map/all_gather | solution.py:216
  85.9 24.2 %collective-permute-start.3 = (f32[4,176,352]{2,1,0:T(8,128)S(1)}, f32[4,176,352]{2,1,0:T(8,128)S(1)}, u32[]{:S(2)}, u32[]{:S(2)}) collective-permute-start(f32[4,176,352]{2,1,0:T(8,128)S(1)} %get-tuple-element.44), channel_id=1, source_target_pairs={{0,1},{1,0},{2,3},{3,2},{4,5},{5,4},{6,7},{7,6},{8,9},{9,8},{10,11... | collective-permute-start | bytes 2973704 | tf_op jit(solution)/shard_map/ppermute | solution.py:140
  87.9 11.2 %collective-permute-start.9 = (f32[176,352]{1,0:T(8,128)S(1)}, f32[176,352]{1,0:T(8,128)S(1)}, u32[]{:S(2)}, u32[]{:S(2)}) collective-permute-start(f32[176,352]{1,0:T(8,128)S(1)} %get-tuple-element.49), channel_id=1, source_target_pairs={{0,2},{1,3},{2,4},{3,5},{4,6},{5,7},{6,0},{7,1},{8,10},{9,11},{10,... | collective-permute-start | bytes 743432 | tf_op jit(solution)/shard_map/ppermute | solution.py:146
  90.3 12.7 %collective-permute-start.8 = (f32[176,352]{1,0:T(8,128)S(1)}, f32[176,352]{1,0:T(8,128)S(1)}, u32[]{:S(2)}, u32[]{:S(2)}) collective-permute-start(f32[176,352]{1,0:T(8,128)S(1)} %get-tuple-element.49), channel_id=1, source_target_pairs={{0,4},{1,5},{2,6},{3,7},{4,0},{5,1},{6,2},{7,3},{8,12},{9,13},{10,... | collective-permute-start | bytes 743432 | tf_op jit(solution)/shard_map/ppermute | solution.py:146
  94.6 13.5 %collective-permute-start.7 = (f32[176,352]{1,0:T(8,128)S(1)}, f32[176,352]{1,0:T(8,128)S(1)}, u32[]{:S(2)}, u32[]{:S(2)}) collective-permute-start(f32[176,352]{1,0:T(8,128)S(1)} %get-tuple-element.49), channel_id=1, source_target_pairs={{0,6},{1,7},{2,0},{3,1},{4,2},{5,3},{6,4},{7,5},{8,14},{9,15},{10,... | collective-permute-start | bytes 743432 | tf_op jit(solution)/shard_map/ppermute | solution.py:146
  108.1 42.7 %collective-permute-start.10 = (f32[4,176,352]{2,1,0:T(8,128)S(1)}, f32[4,176,352]{2,1,0:T(8,128)S(1)}, u32[]{:S(2)}, u32[]{:S(2)}) collective-permute-start(f32[4,176,352]{2,1,0:T(8,128)S(1)} %pad_maximum_fusion.refs_0_), channel_id=1, source_target_pairs={{0,1},{1,0},{2,3},{3,2},{4,5},{5,4},{6,7},{7,6},{8,9},{9,8},{10,11... | collective-permute-start | bytes 2973704 | tf_op jit(solution)/shard_map/ppermute | solution.py:140
  110.3 12.7 %collective-permute-start.6 = (f32[176,352]{1,0:T(8,128)S(1)}, f32[176,352]{1,0:T(8,128)S(1)}, u32[]{:S(2)}, u32[]{:S(2)}) collective-permute-start(f32[176,352]{1,0:T(8,128)S(1)} %get-tuple-element.48), channel_id=1, source_target_pairs={{0,4},{1,5},{2,6},{3,7},{4,0},{5,1},{6,2},{7,3},{8,12},{9,13},{10,... | collective-permute-start | bytes 743432 | tf_op jit(solution)/shard_map/ppermute | solution.py:146
  114.7 13.6 %collective-permute-start.5 = (f32[176,352]{1,0:T(8,128)S(1)}, f32[176,352]{1,0:T(8,128)S(1)}, u32[]{:S(2)}, u32[]{:S(2)}) collective-permute-start(f32[176,352]{1,0:T(8,128)S(1)} %get-tuple-element.47), channel_id=1, source_target_pairs={{0,6},{1,7},{2,0},{3,1},{4,2},{5,3},{6,4},{7,5},{8,14},{9,15},{10,... | collective-permute-start | bytes 743432 | tf_op jit(solution)/shard_map/ppermute | solution.py:146
  116.6 11.7 %collective-permute-start.4 = (f32[176,352]{1,0:T(8,128)S(1)}, f32[176,352]{1,0:T(8,128)S(1)}, u32[]{:S(2)}, u32[]{:S(2)}) collective-permute-start(f32[176,352]{1,0:T(8,128)S(1)} %get-tuple-element.46), channel_id=1, source_target_pairs={{0,2},{1,3},{2,4},{3,5},{4,6},{5,7},{6,0},{7,1},{8,10},{9,11},{10,... | collective-permute-start | bytes 743432 | tf_op jit(solution)/shard_map/ppermute | solution.py:146
  128.3 23.1 %copy-start.7 = (f32[176,352]{1,0:T(8,128)}, f32[176,352]{1,0:T(8,128)S(1)}, u32[]{:S(2)}) copy-start(f32[176,352]{1,0:T(8,128)S(1)} %add_add_fusion.3) | copy-start | bytes 743428
  157.6 4.6 %collective-permute-start.11 = (f32[4,176,352]{2,1,0:T(8,128)S(1)}, f32[4,176,352]{2,1,0:T(8,128)S(1)}, u32[]{:S(2)}, u32[]{:S(2)}) collective-permute-start(f32[4,176,352]{2,1,0:T(8,128)S(1)} %get-tuple-element.53), channel_id=1, source_target_pairs={{0,1},{1,0},{2,3},{3,2},{4,5},{5,4},{6,7},{7,6},{8,9},{9,8},{10,11... | collective-permute-start | bytes 2973704 | tf_op jit(solution)/shard_map/ppermute | solution.py:140
  162.4 13.1 %collective-permute-start.14 = (f32[176,352]{1,0:T(8,128)S(1)}, f32[176,352]{1,0:T(8,128)S(1)}, u32[]{:S(2)}, u32[]{:S(2)}) collective-permute-start(f32[176,352]{1,0:T(8,128)S(1)} %get-tuple-element.57), channel_id=1, source_target_pairs={{0,4},{1,5},{2,6},{3,7},{4,0},{5,1},{6,2},{7,3},{8,12},{9,13},{10,... | collective-permute-start | bytes 743432 | tf_op jit(solution)/shard_map/ppermute | solution.py:146
  165.4 20.1 %collective-permute-start.13 = (f32[176,352]{1,0:T(8,128)S(1)}, f32[176,352]{1,0:T(8,128)S(1)}, u32[]{:S(2)}, u32[]{:S(2)}) collective-permute-start(f32[176,352]{1,0:T(8,128)S(1)} %get-tuple-element.56), channel_id=1, source_target_pairs={{0,6},{1,7},{2,0},{3,1},{4,2},{5,3},{6,4},{7,5},{8,14},{9,15},{10,... | collective-permute-start | bytes 743432 | tf_op jit(solution)/shard_map/ppermute | solution.py:146
  167.4 18.2 %collective-permute-start.12 = (f32[176,352]{1,0:T(8,128)S(1)}, f32[176,352]{1,0:T(8,128)S(1)}, u32[]{:S(2)}, u32[]{:S(2)}) collective-permute-start(f32[176,352]{1,0:T(8,128)S(1)} %get-tuple-element.55), channel_id=1, source_target_pairs={{0,2},{1,3},{2,4},{3,5},{4,6},{5,7},{6,0},{7,1},{8,10},{9,11},{10,... | collective-permute-start | bytes 743432 | tf_op jit(solution)/shard_map/ppermute | solution.py:146
  207.4 4.6 %collective-permute-start.15 = (f32[4,176,352]{2,1,0:T(8,128)S(1)}, f32[4,176,352]{2,1,0:T(8,128)S(1)}, u32[]{:S(2)}, u32[]{:S(2)}) collective-permute-start(f32[4,176,352]{2,1,0:T(8,128)S(1)} %get-tuple-element.61), channel_id=1, source_target_pairs={{0,1},{1,0},{2,3},{3,2},{4,5},{5,4},{6,7},{7,6},{8,9},{9,8},{10,11... | collective-permute-start | bytes 2973704 | tf_op jit(solution)/shard_map/ppermute | solution.py:140
  212.2 12.7 %collective-permute-start.18 = (f32[176,352]{1,0:T(8,128)S(1)}, f32[176,352]{1,0:T(8,128)S(1)}, u32[]{:S(2)}, u32[]{:S(2)}) collective-permute-start(f32[176,352]{1,0:T(8,128)S(1)} %get-tuple-element.65), channel_id=1, source_target_pairs={{0,4},{1,5},{2,6},{3,7},{4,0},{5,1},{6,2},{7,3},{8,12},{9,13},{10,... | collective-permute-start | bytes 743432 | tf_op jit(solution)/shard_map/ppermute | solution.py:146
  217.3 12.6 %collective-permute-start.17 = (f32[176,352]{1,0:T(8,128)S(1)}, f32[176,352]{1,0:T(8,128)S(1)}, u32[]{:S(2)}, u32[]{:S(2)}) collective-permute-start(f32[176,352]{1,0:T(8,128)S(1)} %get-tuple-element.64), channel_id=1, source_target_pairs={{0,6},{1,7},{2,0},{3,1},{4,2},{5,3},{6,4},{7,5},{8,14},{9,15},{10,... | collective-permute-start | bytes 743432 | tf_op jit(solution)/shard_map/ppermute | solution.py:146
  219.7 10.4 %collective-permute-start.16 = (f32[176,352]{1,0:T(8,128)S(1)}, f32[176,352]{1,0:T(8,128)S(1)}, u32[]{:S(2)}, u32[]{:S(2)}) collective-permute-start(f32[176,352]{1,0:T(8,128)S(1)} %get-tuple-element.63), channel_id=1, source_target_pairs={{0,2},{1,3},{2,4},{3,5},{4,6},{5,7},{6,0},{7,1},{8,10},{9,11},{10,... | collective-permute-start | bytes 743432 | tf_op jit(solution)/shard_map/ppermute | solution.py:146
  252.9 4.8 %collective-permute-start.19 = (f32[4,176,352]{2,1,0:T(8,128)}, f32[4,176,352]{2,1,0:T(8,128)S(1)}, u32[]{:S(2)}, u32[]{:S(2)}) collective-permute-start(f32[4,176,352]{2,1,0:T(8,128)} %get-tuple-element.68), channel_id=1, source_target_pairs={{0,1},{1,0},{2,3},{3,2},{4,5},{5,4},{6,7},{7,6},{8,9},{9,8},{10,11... | collective-permute-start | bytes 2973704 | tf_op jit(solution)/shard_map/ppermute | solution.py:140
  257.9 14.8 %collective-permute-start.22 = (f32[176,352]{1,0:T(8,128)S(1)}, f32[176,352]{1,0:T(8,128)S(1)}, u32[]{:S(2)}, u32[]{:S(2)}) collective-permute-start(f32[176,352]{1,0:T(8,128)S(1)} %get-tuple-element.72), channel_id=1, source_target_pairs={{0,4},{1,5},{2,6},{3,7},{4,0},{5,1},{6,2},{7,3},{8,12},{9,13},{10,... | collective-permute-start | bytes 743432 | tf_op jit(solution)/shard_map/ppermute | solution.py:146
  263.3 12.6 %collective-permute-start.21 = (f32[176,352]{1,0:T(8,128)S(1)}, f32[176,352]{1,0:T(8,128)S(1)}, u32[]{:S(2)}, u32[]{:S(2)}) collective-permute-start(f32[176,352]{1,0:T(8,128)S(1)} %get-tuple-element.71), channel_id=1, source_target_pairs={{0,6},{1,7},{2,0},{3,1},{4,2},{5,3},{6,4},{7,5},{8,14},{9,15},{10,... | collective-permute-start | bytes 743432 | tf_op jit(solution)/shard_map/ppermute | solution.py:146
  266.2 10.4 %collective-permute-start.20 = (f32[176,352]{1,0:T(8,128)S(1)}, f32[176,352]{1,0:T(8,128)S(1)}, u32[]{:S(2)}, u32[]{:S(2)}) collective-permute-start(f32[176,352]{1,0:T(8,128)S(1)} %get-tuple-element.70), channel_id=1, source_target_pairs={{0,2},{1,3},{2,4},{3,5},{4,6},{5,7},{6,0},{7,1},{8,10},{9,11},{10,... | collective-permute-start | bytes 743432 | tf_op jit(solution)/shard_map/ppermute | solution.py:146
Sparse Core Ops, SparseCore 0:
  67.3 84.0 all-gather.8
  153.5 45.4 all-gather.10
where the time goes:
time: 288 us; the launch traced here: 284 us
  waiting for transfers between devices  83 us (29%)
  starting transfers between devices  81.9 us (28%)
  blocking collectives  67.4 us (23%)
  Pallas kernels  27 us (9%)
  between operations  14.4 us (5%)
  local copies, waits for them, and re-layouts  9.27 us (3%)
    all_gather x4, blocking collectives, y_gather(): return lax.all_gather(value, 'leaf', axis=0, axis_index_groups=y_groups)  67.4 us
    ppermute x15, starting transfers between devices, shift_x(): return lax.ppermute(value, 'front', pairs)  54.8 us
    ppermute x15, waiting for transfers between devices, shift_x(): return lax.ppermute(value, 'front', pairs)  40.8 us
    ppermute x3, waiting for transfers between devices, from_plane(): return lax.ppermute(value, 'leaf', pairs)  35.2 us
    pallas_call x10, Pallas kernels, call(): pl.pallas_call(kernel, out_shape=out_shape, grid=(1,), in_specs=in_specs,...  27 us
    ppermute x3, starting transfers between devices, from_plane(): return lax.ppermute(value, 'leaf', pairs)  17.3 us
    ppermute x5, starting transfers between devices, from_core(): return lax.ppermute(value, 'front', [(i, i ^ 1) for i in range(fronts)])  9.7 us
  transfers between devices with their start and end apart: 25, of which 19 were waited for; matrix products, arithmetic and copies ran while one was open for 2% of the time, Pallas kernels for 3%

commit v1 on v0

v1 whole, which is shorter than its diff:
```python
import functools

import jax
import jax.numpy as jnp
from jax import lax
from jax.experimental import pallas as pl
from jax.experimental.pallas import tpu as pltpu
from jax.sharding import PartitionSpec as P

Y = 4
XS = 4
CORES = 2
VMEM_BYTES = 48 * 1024 * 1024


def split(value):
    high = value.astype(jnp.bfloat16)
    low = (value - high.astype(jnp.float32)).astype(jnp.bfloat16)
    return high, low


def product(first, second):
    (fh, fl), (sh, sl) = first, second
    run = functools.partial(jnp.dot, preferred_element_type=jnp.float32)
    return run(fh, sh) + (run(fh, sl) + run(fl, sh))


def block_of(ref, index):
    return ref[:, index * 176 : (index + 1) * 176]


def turn(p2_ref, f2_ref, own_ref, got_ref, out_ref):
    top = jnp.concatenate([own_ref[...], got_ref[...]], 0)
    out_ref[...] = jnp.concatenate([p2_ref[...].T, f2_ref[...].T, top], 1)


def pack(two_ref, got_ref, p3_ref, f3_ref, out_ref):
    parts = [two_ref[...], got_ref[...]]
    for ref in (p3_ref, f3_ref):
        turned = ref[...].T
        parts += [turned[:88], turned[88:]]
    out_ref[...] = jnp.concatenate(parts, 1)


def join(where_ref, own_ref, got_ref, panels_ref, f1_ref, rows_ref):
    del panels_ref
    z = where_ref[2]

    def at(which, distance):
        far = ((distance >> 1) & 1) == 1
        own = jnp.where(far, block_of(own_ref, which + 3), block_of(own_ref, which))
        got = jnp.where(far, block_of(got_ref, which + 3), block_of(got_ref, which))
        return jnp.where((distance & 1) == 1, got, own)

    pieces = []
    for plane in range(8):
        distance = plane ^ z
        both = at(2, distance)
        pieces.append(jnp.where((distance >> 2) == 1, both[44:], both[:44]))
    f1_ref[...] = jnp.concatenate(pieces, 0).T
    for which in range(2):
        pieces = [at(which, plane ^ (z % 4)) for plane in range(4)]
        rows_ref[which] = jnp.concatenate(pieces, 0).T
    for which in range(2):
        pieces = []
        for plane in range(2):
            near = plane == (z % 2)
            for index in (6 + 2 * which, 7 + 2 * which):
                pieces.append(
                    jnp.where(near, block_of(own_ref, index), block_of(got_ref, index))
                )
        rows_ref[2 + which] = jnp.concatenate(pieces, 0).T


def share_terms(where_ref, planes, tiles, factors, other_ref, mine_ref):
    x, core = where_ref[0], where_ref[1]
    width = tiles[0](0).shape[1] // planes
    step = min(width, 176)
    for y in range(Y):
        total = None
        for tile, factor in zip(tiles, factors):
            term = product(split(tile(y).T), factor)
            total = term if total is None else total + term
        for plane in range(planes):
            for part in range(0, width, step):
                column = (plane * Y + y) * width + part
                block, offset = column // 176, column % 176
                value = total[plane * width + part : plane * width + part + step]
                at = (block // CORES - x) % XS
                same = core == (block % CORES)

                @pl.when(same)
                def _():
                    mine_ref[at, offset : offset + step, :] = value

                @pl.when(jnp.logical_not(same))
                def _():
                    other_ref[at, offset : offset + step, :] = value


def top_terms(where_ref, rows_ref, own_ref, p4_ref, f4_ref, other_ref, mine_ref, last_ref):
    factors = [split(own_ref[...])]
    share_terms(where_ref, 8, [lambda y: rows_ref[y]], factors, other_ref, mine_ref)
    last_ref[0] = p4_ref[...]
    last_ref[1] = f4_ref[...]


def level_terms(planes, where_ref, parent_ref, columns_ref, rows_ref, own_ref, *out_refs):
    cross_ref, other_ref, mine_ref = out_refs
    z, count = where_ref[2], own_ref.shape[1]
    total = None
    for y in range(Y):
        if planes == 4:
            left = parent_ref[y]
            parts = [
                columns_ref[p, y * 44 : (y + 1) * 44, :count] for p in range(8)
            ]
        elif planes == 2:
            left = parent_ref[4 * y : 4 * y + 4].reshape(352, 176).T
            low = (y % 2) * 88
            parts = []
            for q in range(4):
                p = (z % 4) ^ ((q & 1) * 2 + (q >> 1))
                parts.append(columns_ref[p * 2 + y // 2, low : low + 88, :count])
        else:
            left = parent_ref[2 * y : 2 * y + 2].reshape(352, 176).T
            parts = [columns_ref[((z % 2) ^ q) * Y + y, :, :count] for q in range(2)]
        term = product(split(left), split(jnp.concatenate(parts, 0)))
        total = term if total is None else total + term
    cross_ref[...] = -total
    tiles = [lambda y: rows_ref[y, 0], lambda y: rows_ref[y, 1]]
    factors = [split(total), split(own_ref[...])]
    share_terms(where_ref, planes, tiles, factors, other_ref, mine_ref)


def finish(*refs):
    *in_refs, out_ref, turned_ref = refs
    total = sum(ref[...] for ref in in_refs)
    out_ref[...] = total
    turned_ref[...] = total.T


def add_pieces(mine_ref, got_ref, *out_refs):
    for step, out_ref in enumerate(out_refs):
        out_ref[...] = mine_ref[step] + got_ref[step]


def local(top_factor, panel_two, panel_three, panel_four, factor_two, factor_three, factor_four):
    leaves = lax.axis_size("leaf")
    fronts = lax.axis_size("front")
    share = top_factor.shape[0]
    width = panel_four.shape[1]
    leaf = lax.axis_index("leaf")
    front = lax.axis_index("front")
    z, x, core = leaf // Y, front // CORES, front % CORES
    where = jnp.stack([x, core, z % 8]).astype(jnp.int32)
    y_groups = [list(range(i, i + Y)) for i in range(0, leaves, Y)]

    def from_plane(value, distance):
        pairs = [(i, ((i // Y) ^ distance) * Y + i % Y) for i in range(leaves)]
        return lax.ppermute(value, "leaf", pairs)

    def from_core(value):
        return lax.ppermute(value, "front", [(i, i ^ 1) for i in range(fronts)])

    def shift_x(value, distance):
        pairs = [
            (i, (i // CORES + distance) % XS * CORES + i % CORES) for i in range(fronts)
        ]
        return lax.ppermute(value, "front", pairs)

    def y_gather(value):
        return lax.all_gather(value, "leaf", axis=0, axis_index_groups=y_groups)

    stack = functools.partial(jax.ShapeDtypeStruct, dtype=jnp.float32)
    tile, tiles = stack((share, width)), stack((XS, share, width))
    scalars = pl.BlockSpec(memory_space=pltpu.SMEM)

    def full(value):
        return pl.BlockSpec(value.shape, lambda i: (0,) * len(value.shape))

    def call(kernel, out_shape, in_specs, flops, *args):
        many = isinstance(out_shape, (tuple, list))
        specs = [full(o) for o in (out_shape if many else [out_shape])]
        return pl.pallas_call(
            kernel,
            out_shape=out_shape,
            grid=(1,),
            in_specs=in_specs,
            out_specs=specs if many else specs[0],
            compiler_params=pltpu.CompilerParams(vmem_limit_bytes=VMEM_BYTES),
            cost_estimate=pl.CostEstimate(
                flops=flops, bytes_accessed=8_000_000, transcendentals=0
            ),
        )(*args)

    def front_total(other, mine):
        got = from_core(other)
        piece = stack(mine.shape[1:])
        pieces = call(
            add_pieces, [piece] * XS, [full(mine), full(got)], 1_000_000, mine, got
        )
        parts = [pieces[0]] + [shift_x(pieces[d], d) for d in (1, 3, 2)]
        turned = stack(piece.shape[::-1])
        return call(finish, [piece, turned], [full(piece)] * XS, 1_000_000, *parts)

    def padded(value):
        return jnp.pad(value, ((0, 0), (0, -value.shape[1] % 128)))

    panels = jnp.concatenate([padded(panel_four), padded(panel_two), padded(panel_three)], 1)
    panels = lax.all_gather(panels, "front", axis=0)

    half = share // 2
    first = top_factor.T
    raw = [panel_two, factor_two, first, from_plane(first, 4)]
    two = call(turn, stack((half, 3 * share)), [full(v) for v in raw], 1_000_000, *raw)
    raw = [two, from_plane(two, 2), panel_three, factor_three]
    near = call(pack, stack((half, 10 * share)), [full(v) for v in raw], 1_000_000, *raw)
    f1, deep = call(
        join,
        [tile, stack((4, share, width))],
        [scalars, full(near), full(near), pl.BlockSpec(memory_space=pl.ANY)],
        1_000_000,
        where,
        near,
        from_plane(near, 1),
        panels,
    )
    rows = y_gather(deep)

    work = 6 * share * share * XS * width
    other, mine, last = call(
        top_terms,
        [tiles, tiles, stack((2, share, width))],
        [scalars, full(tiles), full(tile), full(tile), full(tile)],
        2 * work,
        where,
        y_gather(f1),
        f1,
        panel_four,
        factor_four,
    )
    last_rows = y_gather(last)
    parent, _ = front_total(other, mine)
    part = width // 8
    results = [lax.dynamic_slice_in_dim(parent, (z % 8) * part, part, 1)]

    shifts = {4: (), 2: (2, 1), 1: (1,)}
    for planes, factor, lanes, at in (
        (4, factor_two, 128, 3),
        (2, factor_three, 256, 2),
        (1, factor_four, 384, 0),
    ):
        if planes < 4:
            parent = parent[None]
        for distance in shifts[planes]:
            parent = jnp.concatenate([parent, from_plane(parent, distance)], 0)
        gathered = y_gather(parent)
        if planes < 4:
            gathered = gathered.reshape(-1, *gathered.shape[2:])
        count = factor.shape[1]
        level = 0 if planes == 4 else 1 if planes == 2 else 0
        source = last_rows if planes == 1 else rows
        cross, other, mine = call(
            functools.partial(level_terms, planes),
            [stack((share, count)), stack((XS, share, count)), stack((XS, share, count))],
            [
                scalars,
                full(gathered),
                pl.BlockSpec((fronts, share, lanes), lambda i, n=at: (0, 0, n)),
                pl.BlockSpec((Y, 2, share, width), lambda i, n=level: (0, n, 0, 0)),
                full(factor),
            ],
            4 * work // planes,
            where,
            gathered,
            panels,
            source,
            factor,
        )
        covariance, parent = front_total(other, mine)
        results.append(cross)
        results.append(covariance)
    return tuple(results)


def solution(mesh):
    spec = P("front", "leaf")
    return jax.shard_map(
        local, mesh=mesh, in_specs=(spec,) * 7, out_specs=(spec,) * 7, check_vma=False
    )
```

time: 288 us -> 275 us (0.955); the launches traced: 284 us -> 275 us
  starting transfers between devices: 81.9 us -> 72.6 us
  local copies, waits for them, and re-layouts: 9.27 us -> 4.67 us
  Pallas kernels: 27 us -> 30.9 us
    ppermute x15 -> x12, starting transfers between devices: 54.8 us -> 36 us  [shift_x(): return lax.ppermute(value, 'front', pairs)]
    ppermute x3 -> x6, starting transfers between devices: 17.3 us -> 28.9 us  [from_plane(): return lax.ppermute(value, 'leaf', pairs)]
    ppermute x15 -> x12, waiting for transfers between devices: 40.8 us -> 34.3 us  [shift_x(): return lax.ppermute(value, 'front', pairs)]
    dynamic_slice x5 -> x1, local copies, waits for them, and re-layouts: 4.05 us -> 0.09 us  [local(): results = [lax.dynamic_slice_in_dim(parent, z % 8 * part, part, 1)]]
    pallas_call x10 -> x15, Pallas kernels: 27 us -> 30.9 us  [call(): pl.pallas_call(kernel, out_shape=out_shape, grid=(1,), in_specs=in_specs,...]
    ppermute x5 -> x4, waiting for transfers between devices: 5.72 us -> 9.14 us  [from_core(): return lax.ppermute(value, 'front', [(i, i ^ 1) for i in range(fronts)])]
    ppermute x3 -> x6, waiting for transfers between devices: 35.2 us -> 37.6 us  [from_plane(): return lax.ppermute(value, 'leaf', pairs)]
    ppermute x5 -> x4, starting transfers between devices: 9.7 us -> 7.63 us  [from_core(): return lax.ppermute(value, 'front', [(i, i ^ 1) for i in range(fronts)])]
  transfers between devices with their start and end apart: 25 -> 25, of which waited for: 19 -> 17; matrix products, arithmetic and copies ran while one was open for 2% -> 0% of each run, Pallas kernels for 3% -> 7%
where the time goes in v1:
time: 275 us
  waiting for transfers between devices  81.1 us (29%)
  starting transfers between devices  72.6 us (26%)
  blocking collectives  69 us (25%)
  Pallas kernels  30.9 us (11%)
  between operations  14.1 us (5%)
  local copies, waits for them, and re-layouts  4.67 us (2%)
    all_gather x4, blocking collectives, y_gather(): return lax.all_gather(value, 'leaf', axis=0, axis_index_groups=y_groups)  69 us
    ppermute x6, waiting for transfers between devices, from_plane(): return lax.ppermute(value, 'leaf', pairs)  37.6 us
    ppermute x12, starting transfers between devices, shift_x(): return lax.ppermute(value, 'front', pairs)  36 us
    ppermute x12, waiting for transfers between devices, shift_x(): return lax.ppermute(value, 'front', pairs)  34.3 us
    pallas_call x15, Pallas kernels, call(): pl.pallas_call(kernel, out_shape=out_shape, grid=(1,), in_specs=in_specs,...  30.9 us
    ppermute x6, starting transfers between devices, from_plane(): return lax.ppermute(value, 'leaf', pairs)  28.9 us
    ppermute x4, waiting for transfers between devices, from_core(): return lax.ppermute(value, 'front', [(i, i ^ 1) for i in range(fronts)])  9.14 us
    ppermute x4, starting transfers between devices, from_core(): return lax.ppermute(value, 'front', [(i, i ^ 1) for i in range(fronts)])  7.63 us
  transfers between devices with their start and end apart: 25, of which 17 were waited for; matrix products, arithmetic and copies ran while one was open for 0% of the time, Pallas kernels for 7%

profile of v1, /device:TPU:6, one launch (start us, length us, event | category | flops | bytes accessed | tf_op | source)
XLA Modules:
  0.0 274.6 jit_solution(11457652506345790975)
XLA Ops:
  7.3 2.0 select_maximum_fusion
  9.4 9.1 %collective-permute-start = (f32[44,176]{1,0:T(8,128)S(1)}, f32[44,176]{1,0:T(8,128)S(1)}, u32[]{:S(2)}, u32[]{:S(2)}) collective-permute-start(f32[44,176]{1,0:T(8,128)S(1)} %bitcast.23), channel_id=1, source_target_pairs={{0,128},{8,136},{16,144},{24,152},{32,160},{40,168},{48,176},{56,1... | collective-permute-start | bytes 92936 | tf_op jit(solution)/shard_map/ppermute | solution.py:161
  18.5 2.1 collective-permute-done.got_ref
  20.6 0.2 shard_map.126.two_ref
  20.8 5.3 %collective-permute-start.1 = (f32[88,528]{1,0:T(8,128)S(1)}, f32[88,528]{1,0:T(8,128)S(1)}, u32[]{:S(2)}, u32[]{:S(2)}) collective-permute-start(f32[88,528]{1,0:T(8,128)S(1)} %shard_map.126.two_ref), channel_id=1, source_target_pairs={{0,64},{8,72},{16,80},{24,88},{32,96},{40,104},{48,112},{56,120},{... | collective-permute-start | bytes 557576 | tf_op jit(solution)/shard_map/ppermute | solution.py:161
  26.1 10.5 %collective-permute-done.1.got_ref = f32[88,528]{1,0:T(8,128)S(1)} collective-permute-done((f32[88,528]{1,0:T(8,128)S(1)}, f32[88,528]{1,0:T(8,128)S(1)}, u32[]{:S(2)}, u32[]{:S(2)}) %collective-permute-start.1) | collective-permute-done | bytes 185888 | tf_op jit(solution)/shard_map/ppermute | solution.py:161
  36.6 0.3 shard_map.127.own_ref
  36.9 2.6 collective-permute-start.2
  39.6 0.1 pad_add_fusion.where_ref
  39.7 14.8 %collective-permute-done.2.got_ref = f32[88,1760]{1,0:T(8,128)S(1)} collective-permute-done((f32[88,1760]{1,0:T(8,128)S(1)}, f32[88,1760]{1,0:T(8,128)S(1)}, u32[]{:S(2)}, u32[]{:S(2)}) %collective-permute-start.2) | collective-permute-done | bytes 619552 | tf_op jit(solution)/shard_map/ppermute | solution.py:161
  54.5 3.0 %shard_map.128 = (f32[176,352]{1,0:T(8,128)S(1)}, f32[4,176,352]{2,1,0:T(8,128)}) custom-call(s32[3]{0:T(128)S(1)} %pad_add_fusion.where_ref, f32[88,1760]{1,0:T(8,128)S(1)} %shard_map.127.own_ref, f32[88,1760]{1,0:T(8,128)S(1)} %collective-permute-done.2.got_ref, f32[8,176,768]{2,1,0:T(8,128)} %bitcast.11), custom_call_target="tpu_custom_call" | custom-call | flops 1000000 | bytes 8000000 | tf_op jit(solution)/shard_map/pallas_call | solution.py:185
  57.6 15.3 %all-gather.1 = f32[704,352]{1,0:T(8,128)S(1)} all-gather(f32[176,352]{1,0:T(8,128)S(1)} %get-tuple-element.43.own_ref), channel_id=3, replica_groups={{0,8,16,24},{32,40,48,56},{64,72,80,88},{96,104,112,120},{128,136,144,1..., dimensions={0}, use_global_device_ids=true | all-gather | bytes 1239040 | tf_op jit(solution)/shard_map/all_gather | solution.py:173
  72.9 3.7 %shard_map.129 = (f32[4,176,352]{2,1,0:T(8,128)S(1)}, f32[4,176,352]{2,1,0:T(8,128)S(1)}, f32[2,176,352]{2,1,0:T(8,128)}) custom-call(s32[3]{0:T(128)S(1)} %pad_add_fusion.where_ref, f32[4,176,352]{2,1,0:T(8,128)S(1)} %bitcast.17, f32[176,352]{1,0:T(8,128)S(1)} %get-tuple-element.43.own_ref, f32[176,352]{1,0:T(8,128)S(1)} %copy-done.7, f32[176,352]{1,0:T(8,128)S(1)} %copy-done.6), custom_call_target="tpu_custom_call" | custom-call | flops 523370496 | bytes 8000000 | tf_op jit(solution)/shard_map/pallas_call | solution.py:185
  76.6 1.9 collective-permute-start.3
  78.5 2.7 collective-permute-done.3.got_ref
  81.2 0.2 shard_map.130
  81.4 3.3 %collective-permute-start.4 = (f32[176,352]{1,0:T(8,128)S(1)}, f32[176,352]{1,0:T(8,128)S(1)}, u32[]{:S(2)}, u32[]{:S(2)}) collective-permute-start(f32[176,352]{1,0:T(8,128)S(1)} %get-tuple-element.47), channel_id=1, source_target_pairs={{0,2},{1,3},{2,4},{3,5},{4,6},{5,7},{6,0},{7,1},{8,10},{9,11},{10,... | collective-permute-start | bytes 743432 | tf_op jit(solution)/shard_map/ppermute | solution.py:170
  84.7 2.5 collective-permute-start.5
  87.2 3.2 %collective-permute-start.6 = (f32[176,352]{1,0:T(8,128)S(1)}, f32[176,352]{1,0:T(8,128)S(1)}, u32[]{:S(2)}, u32[]{:S(2)}) collective-permute-start(f32[176,352]{1,0:T(8,128)S(1)} %get-tuple-element.49), channel_id=1, source_target_pairs={{0,4},{1,5},{2,6},{3,7},{4,0},{5,1},{6,2},{7,3},{8,12},{9,13},{10,... | collective-permute-start | bytes 743432 | tf_op jit(solution)/shard_map/ppermute | solution.py:170
  90.5 1.3 collective-permute-done.4.refs_1_
  91.8 10.0 %collective-permute-done.5.refs_2_ = f32[176,352]{1,0:T(8,128)S(1)} collective-permute-done((f32[176,352]{1,0:T(8,128)S(1)}, f32[176,352]{1,0:T(8,128)S(1)}, u32[]{:S(2)}, u32[]{:S(2)}) %collective-permute-start.5) | collective-permute-done | bytes 247840 | tf_op jit(solution)/shard_map/ppermute | solution.py:170
  101.8 0.9 shard_map.131
  102.7 21.6 %all-gather.2 = f32[704,352]{1,0:T(8,128)S(1)} all-gather(f32[176,352]{1,0:T(8,128)S(1)} %get-tuple-element.50), channel_id=4, replica_groups={{0,8,16,24},{32,40,48,56},{64,72,80,88},{96,104,112,120},{128,136,144,1..., dimensions={0}, use_global_device_ids=true | all-gather | bytes 1239040 | tf_op jit(solution)/shard_map/all_gather | solution.py:173
  124.4 2.2 copy-done
  126.6 6.0 %shard_map.132 = (f32[176,88]{1,0:T(8,128)}, f32[4,176,88]{2,1,0:T(8,128)S(1)}, f32[4,176,88]{2,1,0:T(8,128)S(1)}) custom-call(s32[3]{0:T(128)S(1)} %pad_add_fusion.where_ref, f32[4,176,352]{2,1,0:T(8,128)S(1)} %bitcast.15, f32[8,176,768]{2,1,0:T(8,128)S(1)} %bitcast.14, f32[4,4,176,352]{3,2,1,0:T(8,128)} %bitcast.25, f32[176,88]{1,0:T(8,128)S(1)} %copy-done.5), custom_call_target="tpu_custom_call" | custom-call | flops 261685248 | bytes 8000000 | tf_op jit(solution)/shard_map/pallas_call | solution.py:185
  132.7 1.9 collective-permute-start.7
  134.6 1.6 collective-permute-done.7.got_ref
  136.2 0.1 shard_map.133
  136.3 2.0 collective-permute-start.8
  138.3 3.8 %collective-permute-start.9 = (f32[176,88]{1,0:T(8,128)S(1)}, f32[176,88]{1,0:T(8,128)S(1)}, u32[]{:S(2)}, u32[]{:S(2)}) collective-permute-start(f32[176,88]{1,0:T(8,128)S(1)} %get-tuple-element.57), channel_id=1, source_target_pairs={{0,6},{1,7},{2,0},{3,1},{4,2},{5,3},{6,4},{7,5},{8,14},{9,15},{10,... | collective-permute-start | bytes 185864 | tf_op jit(solution)/shard_map/ppermute | solution.py:170
  142.1 2.7 collective-permute-start.10
  144.9 1.1 collective-permute-done.9.refs_2_
  146.0 4.1 %collective-permute-done.10.refs_3_ = f32[176,88]{1,0:T(8,128)S(1)} collective-permute-done((f32[176,88]{1,0:T(8,128)S(1)}, f32[176,88]{1,0:T(8,128)S(1)}, u32[]{:S(2)}, u32[]{:S(2)}) %collective-permute-start.10) | collective-permute-done | bytes 61984 | tf_op jit(solution)/shard_map/ppermute | solution.py:170
  150.0 0.7 shard_map.134
  150.7 4.5 %collective-permute-start.11 = (f32[1,88,176]{2,1,0:T(8,128)S(1)}, f32[1,88,176]{2,1,0:T(8,128)S(1)}, u32[]{:S(2)}, u32[]{:S(2)}) collective-permute-start(f32[1,88,176]{2,1,0:T(8,128)S(1)} %bitcast.18), channel_id=1, source_target_pairs={{0,64},{8,72},{16,80},{24,88},{32,96},{40,104},{48,112},{56,120},{... | collective-permute-start | bytes 185864 | tf_op jit(solution)/shard_map/ppermute | solution.py:161
  155.3 2.8 %collective-permute-done.11 = f32[1,88,176]{2,1,0:T(8,128)S(1)} collective-permute-done((f32[1,88,176]{2,1,0:T(8,128)S(1)}, f32[1,88,176]{2,1,0:T(8,128)S(1)}, u32[]{:S(2)}, u32[]{:S(2)}) %collective-permute-start.11) | collective-permute-done | bytes 61984 | tf_op jit(solution)/shard_map/ppermute | solution.py:161
  158.0 3.6 %collective-permute-start.12 = (f32[2,88,176]{2,1,0:T(8,128)S(1)}, f32[2,88,176]{2,1,0:T(8,128)S(1)}, u32[]{:S(2)}, u32[]{:S(2)}) collective-permute-start(f32[2,88,176]{2,1,0:T(8,128)S(1)} %pad_maximum_fusion.2), channel_id=1, source_target_pairs={{0,32},{8,40},{16,48},{24,56},{32,0},{40,8},{48,16},{56,24},{64,96... | collective-permute-start | bytes 371720 | tf_op jit(solution)/shard_map/ppermute | solution.py:161
  161.6 3.8 %collective-permute-done.12 = f32[2,88,176]{2,1,0:T(8,128)S(1)} collective-permute-done((f32[2,88,176]{2,1,0:T(8,128)S(1)}, f32[2,88,176]{2,1,0:T(8,128)S(1)}, u32[]{:S(2)}, u32[]{:S(2)}) %collective-permute-start.12) | collective-permute-done | bytes 123936 | tf_op jit(solution)/shard_map/ppermute | solution.py:161
  165.5 15.5 %all-gather.4.parent_ref = f32[16,88,176]{2,1,0:T(8,128)S(1)} all-gather(f32[4,88,176]{2,1,0:T(8,128)S(1)} %pad_maximum_fusion), channel_id=6, replica_groups={{0,8,16,24},{32,40,48,56},{64,72,80,88},{96,104,112,120},{128,136,144,1..., dimensions={0}, use_global_device_ids=true | all-gather | bytes 1239040 | tf_op jit(solution)/shard_map/all_gather | solution.py:173
  181.0 7.1 %shard_map.135 = (f32[176,176]{1,0:T(8,128)}, f32[4,176,176]{2,1,0:T(8,128)S(1)}, f32[4,176,176]{2,1,0:T(8,128)S(1)}) custom-call(s32[3]{0:T(128)S(1)} %pad_add_fusion.where_ref, f32[16,88,176]{2,1,0:T(8,128)S(1)} %all-gather.4.parent_ref, f32[8,176,768]{2,1,0:T(8,128)} %bitcast.12, f32[4,4,176,352]{3,2,1,0:T(8,128)} %bitcast.26, f32[176,176]{1,0:T(8,128)S(1)} %copy-done.3), custom_call_target="tpu_custom_call" | custom-call | flops 523370496 | bytes 8000000 | tf_op jit(solution)/shard_map/pallas_call | solution.py:185
  188.1 1.9 collective-permute-start.13
  190.0 2.2 collective-permute-done.13.got_ref
  192.1 0.1 shard_map.136
  192.2 3.4 %collective-permute-start.14 = (f32[176,176]{1,0:T(8,128)S(1)}, f32[176,176]{1,0:T(8,128)S(1)}, u32[]{:S(2)}, u32[]{:S(2)}) collective-permute-start(f32[176,176]{1,0:T(8,128)S(1)} %get-tuple-element.65), channel_id=1, source_target_pairs={{0,2},{1,3},{2,4},{3,5},{4,6},{5,7},{6,0},{7,1},{8,10},{9,11},{10,... | collective-permute-start | bytes 371720 | tf_op jit(solution)/shard_map/ppermute | solution.py:170
  195.6 2.4 collective-permute-start.15
  198.1 3.5 %collective-permute-start.16 = (f32[176,176]{1,0:T(8,128)S(1)}, f32[176,176]{1,0:T(8,128)S(1)}, u32[]{:S(2)}, u32[]{:S(2)}) collective-permute-start(f32[176,176]{1,0:T(8,128)S(1)} %get-tuple-element.67), channel_id=1, source_target_pairs={{0,4},{1,5},{2,6},{3,7},{4,0},{5,1},{6,2},{7,3},{8,12},{9,13},{10,... | collective-permute-start | bytes 371720 | tf_op jit(solution)/shard_map/ppermute | solution.py:170
  201.6 7.3 %collective-permute-done.15.refs_2_ = f32[176,176]{1,0:T(8,128)S(1)} collective-permute-done((f32[176,176]{1,0:T(8,128)S(1)}, f32[176,176]{1,0:T(8,128)S(1)}, u32[]{:S(2)}, u32[]{:S(2)}) %collective-permute-start.15) | collective-permute-done | bytes 123936 | tf_op jit(solution)/shard_map/ppermute | solution.py:170
  208.9 0.7 shard_map.137
  209.6 3.7 %collective-permute-start.17 = (f32[1,176,176]{2,1,0:T(8,128)S(1)}, f32[1,176,176]{2,1,0:T(8,128)S(1)}, u32[]{:S(2)}, u32[]{:S(2)}) collective-permute-start(f32[1,176,176]{2,1,0:T(8,128)S(1)} %bitcast.21), channel_id=1, source_target_pairs={{0,32},{8,40},{16,48},{24,56},{32,0},{40,8},{48,16},{56,24},{64,96... | collective-permute-start | bytes 371720 | tf_op jit(solution)/shard_map/ppermute | solution.py:161
  213.3 3.7 %collective-permute-done.17 = f32[1,176,176]{2,1,0:T(8,128)S(1)} collective-permute-done((f32[1,176,176]{2,1,0:T(8,128)S(1)}, f32[1,176,176]{2,1,0:T(8,128)S(1)}, u32[]{:S(2)}, u32[]{:S(2)}) %collective-permute-start.17) | collective-permute-done | bytes 123936 | tf_op jit(solution)/shard_map/ppermute | solution.py:161
  217.0 16.6 %all-gather.5.parent_ref = f32[8,176,176]{2,1,0:T(8,128)S(1)} all-gather(f32[2,176,176]{2,1,0:T(8,128)S(1)} %pad_maximum_fusion.1), channel_id=7, replica_groups={{0,8,16,24},{32,40,48,56},{64,72,80,88},{96,104,112,120},{128,136,144,1..., dimensions={0}, use_global_device_ids=true | all-gather | bytes 1239040 | tf_op jit(solution)/shard_map/all_gather | solution.py:173
  233.6 1.6 copy-done.1
  235.2 6.9 %shard_map.138 = (f32[176,352]{1,0:T(8,128)}, f32[4,176,352]{2,1,0:T(8,128)S(1)}, f32[4,176,352]{2,1,0:T(8,128)S(1)}) custom-call(s32[3]{0:T(128)S(1)} %pad_add_fusion.where_ref, f32[8,176,176]{2,1,0:T(8,128)S(1)} %all-gather.5.parent_ref, f32[8,176,768]{2,1,0:T(8,128)} %bitcast.13, f32[4,2,176,352]{3,2,1,0:T(8,128)S(1)} %bitcast.16, f32[176,352]{1,0:T(8,128)S(1)} %copy-done.6), custom_call_target="tpu_custom_call" | custom-call | flops 1046740992 | bytes 8000000 | tf_op jit(solution)/shard_map/pallas_call | solution.py:185
  242.1 1.9 collective-permute-start.18
  244.0 2.7 collective-permute-done.18.got_ref
  246.7 0.2 shard_map.139
  246.8 3.1 %collective-permute-start.19 = (f32[176,352]{1,0:T(8,128)S(1)}, f32[176,352]{1,0:T(8,128)S(1)}, u32[]{:S(2)}, u32[]{:S(2)}) collective-permute-start(f32[176,352]{1,0:T(8,128)S(1)} %get-tuple-element.75), channel_id=1, source_target_pairs={{0,2},{1,3},{2,4},{3,5},{4,6},{5,7},{6,0},{7,1},{8,10},{9,11},{10,... | collective-permute-start | bytes 743432 | tf_op jit(solution)/shard_map/ppermute | solution.py:170
  250.0 2.7 collective-permute-start.20
  252.7 3.1 %collective-permute-start.21 = (f32[176,352]{1,0:T(8,128)S(1)}, f32[176,352]{1,0:T(8,128)S(1)}, u32[]{:S(2)}, u32[]{:S(2)}) collective-permute-start(f32[176,352]{1,0:T(8,128)S(1)} %get-tuple-element.77), channel_id=1, source_target_pairs={{0,4},{1,5},{2,6},{3,7},{4,0},{5,1},{6,2},{7,3},{8,12},{9,13},{10,... | collective-permute-start | bytes 743432 | tf_op jit(solution)/shard_map/ppermute | solution.py:170
  255.8 0.1 constant_dynamic-slice_fusion
  255.9 0.7 copy.15
  256.6 0.6 collective-permute-done.19.refs_1_
  257.2 9.9 %collective-permute-done.20.refs_2_ = f32[176,352]{1,0:T(8,128)S(1)} collective-permute-done((f32[176,352]{1,0:T(8,128)S(1)}, f32[176,352]{1,0:T(8,128)S(1)}, u32[]{:S(2)}, u32[]{:S(2)}) %collective-permute-start.20) | collective-permute-done | bytes 247840 | tf_op jit(solution)/shard_map/ppermute | solution.py:170
  267.1 0.9 shard_map.140
  (33 shorter events, 0.3 us)
Async XLA Ops:
  7.2 13.4 %copy-start.4 = (f32[176,88]{1,0:T(8,128)S(1)}, f32[176,88]{1,0:T(8,128)}, u32[]{:S(2)}) copy-start(f32[176,88]{1,0:T(8,128)} %p2_ref.1) | copy-start | bytes 185860
  7.2 29.4 %copy-start.2 = (f32[176,176]{1,0:T(8,128)S(1)}, f32[176,176]{1,0:T(8,128)}, u32[]{:S(2)}) copy-start(f32[176,176]{1,0:T(8,128)} %p3_ref.1) | copy-start | bytes 371716
  7.2 2.2 copy-start.8
  7.2 13.4 %copy-start.5 = (f32[176,88]{1,0:T(8,128)S(1)}, f32[176,88]{1,0:T(8,128)}, u32[]{:S(2)}) copy-start(f32[176,88]{1,0:T(8,128)} %own_ref.3) | copy-start | bytes 185860
  7.2 29.4 %copy-start.3 = (f32[176,176]{1,0:T(8,128)S(1)}, f32[176,176]{1,0:T(8,128)}, u32[]{:S(2)}) copy-start(f32[176,176]{1,0:T(8,128)} %own_ref.4) | copy-start | bytes 371716
  7.2 47.3 %all-gather.11.cloned.1.call-start = ((), (), s32[]{:S(2)}) async-start(), calls=%async_computation | async-start | bytes 4866048 | tf_op jit(solution)/shard_map/all_gather | solution.py:211
  9.3 115.0 %all-gather.13.cloned.1.call-start = ((), (), s32[]{:S(2)}) async-start(), calls=%async_computation.1 | async-start | bytes 5406720 | tf_op jit(solution)/shard_map/all_gather | solution.py:173
  9.4 11.2 %collective-permute-start = (f32[44,176]{1,0:T(8,128)S(1)}, f32[44,176]{1,0:T(8,128)S(1)}, u32[]{:S(2)}, u32[]{:S(2)}) collective-permute-start(f32[44,176]{1,0:T(8,128)S(1)} %bitcast.23), channel_id=1, source_target_pairs={{0,128},{8,136},{16,144},{24,152},{32,160},{40,168},{48,176},{56,1... | collective-permute-start | bytes 92936 | tf_op jit(solution)/shard_map/ppermute | solution.py:161
  20.8 15.8 %collective-permute-start.1 = (f32[88,528]{1,0:T(8,128)S(1)}, f32[88,528]{1,0:T(8,128)S(1)}, u32[]{:S(2)}, u32[]{:S(2)}) collective-permute-start(f32[88,528]{1,0:T(8,128)S(1)} %shard_map.126.two_ref), channel_id=1, source_target_pairs={{0,64},{8,72},{16,80},{24,88},{32,96},{40,104},{48,112},{56,120},{... | collective-permute-start | bytes 557576 | tf_op jit(solution)/shard_map/ppermute | solution.py:161
  36.9 17.6 %collective-permute-start.2 = (f32[88,1760]{1,0:T(8,128)S(1)}, f32[88,1760]{1,0:T(8,128)S(1)}, u32[]{:S(2)}, u32[]{:S(2)}) collective-permute-start(f32[88,1760]{1,0:T(8,128)S(1)} %shard_map.127.own_ref), channel_id=1, source_target_pairs={{0,32},{8,40},{16,48},{24,56},{32,0},{40,8},{48,16},{56,24},{64,96... | collective-permute-start | bytes 1858568 | tf_op jit(solution)/shard_map/ppermute | solution.py:161
  57.5 15.4 %copy-start.6 = (f32[176,352]{1,0:T(8,128)S(1)}, f32[176,352]{1,0:T(8,128)}, u32[]{:S(2)}) copy-start(f32[176,352]{1,0:T(8,128)} %own_ref.5) | copy-start | bytes 743428
  57.5 15.4 %copy-start.7 = (f32[176,352]{1,0:T(8,128)S(1)}, f32[176,352]{1,0:T(8,128)}, u32[]{:S(2)}) copy-start(f32[176,352]{1,0:T(8,128)} %p4_ref.1) | copy-start | bytes 743428
  57.6 176.0 %all-gather.15.cloned.1.call-start = ((), (), s32[]{:S(2)}) async-start(), calls=%async_computation.2 | async-start | bytes 2703360 | tf_op jit(solution)/shard_map/all_gather | solution.py:173
  76.6 4.6 %collective-permute-start.3 = (f32[4,176,352]{2,1,0:T(8,128)S(1)}, f32[4,176,352]{2,1,0:T(8,128)S(1)}, u32[]{:S(2)}, u32[]{:S(2)}) collective-permute-start(f32[4,176,352]{2,1,0:T(8,128)S(1)} %get-tuple-element.45), channel_id=1, source_target_pairs={{0,1},{1,0},{2,3},{3,2},{4,5},{5,4},{6,7},{7,6},{8,9},{9,8},{10,11... | collective-permute-start | bytes 2973704 | tf_op jit(solution)/shard_map/ppermute | solution.py:164
  81.4 10.4 %collective-permute-start.4 = (f32[176,352]{1,0:T(8,128)S(1)}, f32[176,352]{1,0:T(8,128)S(1)}, u32[]{:S(2)}, u32[]{:S(2)}) collective-permute-start(f32[176,352]{1,0:T(8,128)S(1)} %get-tuple-element.47), channel_id=1, source_target_pairs={{0,2},{1,3},{2,4},{3,5},{4,6},{5,7},{6,0},{7,1},{8,10},{9,11},{10,... | collective-permute-start | bytes 743432 | tf_op jit(solution)/shard_map/ppermute | solution.py:170
  84.7 17.1 %collective-permute-start.5 = (f32[176,352]{1,0:T(8,128)S(1)}, f32[176,352]{1,0:T(8,128)S(1)}, u32[]{:S(2)}, u32[]{:S(2)}) collective-permute-start(f32[176,352]{1,0:T(8,128)S(1)} %get-tuple-element.48), channel_id=1, source_target_pairs={{0,6},{1,7},{2,0},{3,1},{4,2},{5,3},{6,4},{7,5},{8,14},{9,15},{10,... | collective-permute-start | bytes 743432 | tf_op jit(solution)/shard_map/ppermute | solution.py:170
  87.2 14.6 %collective-permute-start.6 = (f32[176,352]{1,0:T(8,128)S(1)}, f32[176,352]{1,0:T(8,128)S(1)}, u32[]{:S(2)}, u32[]{:S(2)}) collective-permute-start(f32[176,352]{1,0:T(8,128)S(1)} %get-tuple-element.49), channel_id=1, source_target_pairs={{0,4},{1,5},{2,6},{3,7},{4,0},{5,1},{6,2},{7,3},{8,12},{9,13},{10,... | collective-permute-start | bytes 743432 | tf_op jit(solution)/shard_map/ppermute | solution.py:170
  124.4 2.2 copy-start
  132.7 3.6 %collective-permute-start.7 = (f32[4,176,88]{2,1,0:T(8,128)S(1)}, f32[4,176,88]{2,1,0:T(8,128)S(1)}, u32[]{:S(2)}, u32[]{:S(2)}) collective-permute-start(f32[4,176,88]{2,1,0:T(8,128)S(1)} %get-tuple-element.54), channel_id=1, source_target_pairs={{0,1},{1,0},{2,3},{3,2},{4,5},{5,4},{6,7},{7,6},{8,9},{9,8},{10,11... | collective-permute-start | bytes 743432 | tf_op jit(solution)/shard_map/ppermute | solution.py:164
  136.3 8.6 %collective-permute-start.8 = (f32[176,88]{1,0:T(8,128)S(1)}, f32[176,88]{1,0:T(8,128)S(1)}, u32[]{:S(2)}, u32[]{:S(2)}) collective-permute-start(f32[176,88]{1,0:T(8,128)S(1)} %get-tuple-element.56), channel_id=1, source_target_pairs={{0,2},{1,3},{2,4},{3,5},{4,6},{5,7},{6,0},{7,1},{8,10},{9,11},{10,... | collective-permute-start | bytes 185864 | tf_op jit(solution)/shard_map/ppermute | solution.py:170
  138.3 7.7 %collective-permute-start.9 = (f32[176,88]{1,0:T(8,128)S(1)}, f32[176,88]{1,0:T(8,128)S(1)}, u32[]{:S(2)}, u32[]{:S(2)}) collective-permute-start(f32[176,88]{1,0:T(8,128)S(1)} %get-tuple-element.57), channel_id=1, source_target_pairs={{0,6},{1,7},{2,0},{3,1},{4,2},{5,3},{6,4},{7,5},{8,14},{9,15},{10,... | collective-permute-start | bytes 185864 | tf_op jit(solution)/shard_map/ppermute | solution.py:170
  142.1 7.9 %collective-permute-start.10 = (f32[176,88]{1,0:T(8,128)S(1)}, f32[176,88]{1,0:T(8,128)S(1)}, u32[]{:S(2)}, u32[]{:S(2)}) collective-permute-start(f32[176,88]{1,0:T(8,128)S(1)} %get-tuple-element.58), channel_id=1, source_target_pairs={{0,4},{1,5},{2,6},{3,7},{4,0},{5,1},{6,2},{7,3},{8,12},{9,13},{10,... | collective-permute-start | bytes 185864 | tf_op jit(solution)/shard_map/ppermute | solution.py:170
  150.7 7.3 %collective-permute-start.11 = (f32[1,88,176]{2,1,0:T(8,128)S(1)}, f32[1,88,176]{2,1,0:T(8,128)S(1)}, u32[]{:S(2)}, u32[]{:S(2)}) collective-permute-start(f32[1,88,176]{2,1,0:T(8,128)S(1)} %bitcast.18), channel_id=1, source_target_pairs={{0,64},{8,72},{16,80},{24,88},{32,96},{40,104},{48,112},{56,120},{... | collective-permute-start | bytes 185864 | tf_op jit(solution)/shard_map/ppermute | solution.py:161
  158.0 7.4 %collective-permute-start.12 = (f32[2,88,176]{2,1,0:T(8,128)S(1)}, f32[2,88,176]{2,1,0:T(8,128)S(1)}, u32[]{:S(2)}, u32[]{:S(2)}) collective-permute-start(f32[2,88,176]{2,1,0:T(8,128)S(1)} %pad_maximum_fusion.2), channel_id=1, source_target_pairs={{0,32},{8,40},{16,48},{24,56},{32,0},{40,8},{48,16},{56,24},{64,96... | collective-permute-start | bytes 371720 | tf_op jit(solution)/shard_map/ppermute | solution.py:161
  188.1 4.1 %collective-permute-start.13 = (f32[4,176,176]{2,1,0:T(8,128)S(1)}, f32[4,176,176]{2,1,0:T(8,128)S(1)}, u32[]{:S(2)}, u32[]{:S(2)}) collective-permute-start(f32[4,176,176]{2,1,0:T(8,128)S(1)} %get-tuple-element.63), channel_id=1, source_target_pairs={{0,1},{1,0},{2,3},{3,2},{4,5},{5,4},{6,7},{7,6},{8,9},{9,8},{10,11... | collective-permute-start | bytes 1486856 | tf_op jit(solution)/shard_map/ppermute | solution.py:164
  192.2 9.4 %collective-permute-start.14 = (f32[176,176]{1,0:T(8,128)S(1)}, f32[176,176]{1,0:T(8,128)S(1)}, u32[]{:S(2)}, u32[]{:S(2)}) collective-permute-start(f32[176,176]{1,0:T(8,128)S(1)} %get-tuple-element.65), channel_id=1, source_target_pairs={{0,2},{1,3},{2,4},{3,5},{4,6},{5,7},{6,0},{7,1},{8,10},{9,11},{10,... | collective-permute-start | bytes 371720 | tf_op jit(solution)/shard_map/ppermute | solution.py:170
  195.6 13.3 %collective-permute-start.15 = (f32[176,176]{1,0:T(8,128)S(1)}, f32[176,176]{1,0:T(8,128)S(1)}, u32[]{:S(2)}, u32[]{:S(2)}) collective-permute-start(f32[176,176]{1,0:T(8,128)S(1)} %get-tuple-element.66), channel_id=1, source_target_pairs={{0,6},{1,7},{2,0},{3,1},{4,2},{5,3},{6,4},{7,5},{8,14},{9,15},{10,... | collective-permute-start | bytes 371720 | tf_op jit(solution)/shard_map/ppermute | solution.py:170
  198.1 10.8 %collective-permute-start.16 = (f32[176,176]{1,0:T(8,128)S(1)}, f32[176,176]{1,0:T(8,128)S(1)}, u32[]{:S(2)}, u32[]{:S(2)}) collective-permute-start(f32[176,176]{1,0:T(8,128)S(1)} %get-tuple-element.67), channel_id=1, source_target_pairs={{0,4},{1,5},{2,6},{3,7},{4,0},{5,1},{6,2},{7,3},{8,12},{9,13},{10,... | collective-permute-start | bytes 371720 | tf_op jit(solution)/shard_map/ppermute | solution.py:170
  209.6 7.4 %collective-permute-start.17 = (f32[1,176,176]{2,1,0:T(8,128)S(1)}, f32[1,176,176]{2,1,0:T(8,128)S(1)}, u32[]{:S(2)}, u32[]{:S(2)}) collective-permute-start(f32[1,176,176]{2,1,0:T(8,128)S(1)} %bitcast.21), channel_id=1, source_target_pairs={{0,32},{8,40},{16,48},{24,56},{32,0},{40,8},{48,16},{56,24},{64,96... | collective-permute-start | bytes 371720 | tf_op jit(solution)/shard_map/ppermute | solution.py:161
  233.6 1.6 copy-start.1
  242.1 4.6 %collective-permute-start.18 = (f32[4,176,352]{2,1,0:T(8,128)S(1)}, f32[4,176,352]{2,1,0:T(8,128)S(1)}, u32[]{:S(2)}, u32[]{:S(2)}) collective-permute-start(f32[4,176,352]{2,1,0:T(8,128)S(1)} %get-tuple-element.73), channel_id=1, source_target_pairs={{0,1},{1,0},{2,3},{3,2},{4,5},{5,4},{6,7},{7,6},{8,9},{9,8},{10,11... | collective-permute-start | bytes 2973704 | tf_op jit(solution)/shard_map/ppermute | solution.py:164
  246.8 10.4 %collective-permute-start.19 = (f32[176,352]{1,0:T(8,128)S(1)}, f32[176,352]{1,0:T(8,128)S(1)}, u32[]{:S(2)}, u32[]{:S(2)}) collective-permute-start(f32[176,352]{1,0:T(8,128)S(1)} %get-tuple-element.75), channel_id=1, source_target_pairs={{0,2},{1,3},{2,4},{3,5},{4,6},{5,7},{6,0},{7,1},{8,10},{9,11},{10,... | collective-permute-start | bytes 743432 | tf_op jit(solution)/shard_map/ppermute | solution.py:170
  250.0 17.1 %collective-permute-start.20 = (f32[176,352]{1,0:T(8,128)S(1)}, f32[176,352]{1,0:T(8,128)S(1)}, u32[]{:S(2)}, u32[]{:S(2)}) collective-permute-start(f32[176,352]{1,0:T(8,128)S(1)} %get-tuple-element.76), channel_id=1, source_target_pairs={{0,6},{1,7},{2,0},{3,1},{4,2},{5,3},{6,4},{7,5},{8,14},{9,15},{10,... | collective-permute-start | bytes 743432 | tf_op jit(solution)/shard_map/ppermute | solution.py:170
  252.7 14.4 %collective-permute-start.21 = (f32[176,352]{1,0:T(8,128)S(1)}, f32[176,352]{1,0:T(8,128)S(1)}, u32[]{:S(2)}, u32[]{:S(2)}) collective-permute-start(f32[176,352]{1,0:T(8,128)S(1)} %get-tuple-element.77), channel_id=1, source_target_pairs={{0,4},{1,5},{2,6},{3,7},{4,0},{5,1},{6,2},{7,3},{8,12},{9,13},{10,... | collective-permute-start | bytes 743432 | tf_op jit(solution)/shard_map/ppermute | solution.py:170
Sparse Core Ops, SparseCore 0:
  10.2 42.8 all-gather.10
  57.7 65.6 all-gather.12
  125.5 40.0 all-gather.14

commit v2 on v1

v2 whole, which is shorter than its diff:
```python
import functools

import jax
import jax.numpy as jnp
from jax import lax
from jax.experimental import pallas as pl
from jax.experimental.pallas import tpu as pltpu
from jax.sharding import PartitionSpec as P

Y = 4
XS = 4
CORES = 2
VMEM_BYTES = 48 * 1024 * 1024


def split(value):
    high = value.astype(jnp.bfloat16)
    low = (value - high.astype(jnp.float32)).astype(jnp.bfloat16)
    return high, low


def product(first, second):
    (fh, fl), (sh, sl) = first, second
    run = functools.partial(jnp.dot, preferred_element_type=jnp.float32)
    return run(fh, sh) + (run(fh, sl) + run(fl, sh))


def block_of(ref, index):
    return ref[:, index * 176 : (index + 1) * 176]


def turn(f2_ref, own_ref, got_ref, out_ref):
    top = jnp.concatenate([own_ref[...], got_ref[...]], 0)
    out_ref[...] = jnp.concatenate([f2_ref[...].T, top], 1)


def pack(two_ref, got_ref, p3_ref, f3_ref, out_ref):
    parts = [two_ref[...], got_ref[...]]
    for ref in (p3_ref, f3_ref):
        turned = ref[...].T
        parts += [turned[:88], turned[88:]]
    out_ref[...] = jnp.concatenate(parts, 1)


def join(where_ref, own_ref, got_ref, panels_ref, f1_ref, rows_ref, p3_ref):
    del panels_ref
    z = where_ref[2]

    def at(which, distance):
        far = ((distance >> 1) & 1) == 1
        own = jnp.where(far, block_of(own_ref, which + 2), block_of(own_ref, which))
        got = jnp.where(far, block_of(got_ref, which + 2), block_of(got_ref, which))
        return jnp.where((distance & 1) == 1, got, own)

    pieces = []
    for plane in range(8):
        distance = plane ^ z
        both = at(1, distance)
        pieces.append(jnp.where((distance >> 2) == 1, both[44:], both[:44]))
    f1_ref[...] = jnp.concatenate(pieces, 0).T
    pieces = [at(0, plane ^ (z % 4)) for plane in range(4)]
    rows_ref[0] = jnp.concatenate(pieces, 0).T
    for which in range(2):
        pieces = []
        for plane in range(2):
            near = plane == (z % 2)
            for index in (4 + 2 * which, 5 + 2 * which):
                pieces.append(
                    jnp.where(near, block_of(own_ref, index), block_of(got_ref, index))
                )
        tile = jnp.concatenate(pieces, 0).T
        if which == 0:
            p3_ref[...] = tile
        else:
            rows_ref[1] = tile


def share_terms(where_ref, planes, turned, factors, first, other_ref, mine_ref):
    x, core = where_ref[0], where_ref[1]
    last = first + factors[0][0].shape[1]
    for y in range(Y):
        total = None
        for tile, factor in zip(turned, factors):
            term = product(split(tile(y)), factor)
            total = term if total is None else total + term
        width = total.shape[0] // planes
        step = min(width, 176)
        for plane in range(planes):
            for part in range(0, width, step):
                column = (plane * Y + y) * width + part
                block, offset = column // 176, column % 176
                value = total[plane * width + part : plane * width + part + step]
                at = (block // CORES - x) % XS
                same = core == (block % CORES)

                @pl.when(same)
                def _():
                    mine_ref[at, offset : offset + step, first:last] = value

                @pl.when(jnp.logical_not(same))
                def _():
                    other_ref[at, offset : offset + step, first:last] = value


def times_columns(planes, z, left, columns_ref, count):
    total = None
    for y in range(Y):
        if planes == 4:
            parts = [
                columns_ref[p, y * 44 : (y + 1) * 44, :count] for p in range(8)
            ]
        elif planes == 2:
            low = (y % 2) * 88
            parts = []
            for q in range(4):
                p = (z % 4) ^ ((q & 1) * 2 + (q >> 1))
                parts.append(columns_ref[p * 2 + y // 2, low : low + 88, :count])
        else:
            parts = [columns_ref[((z % 2) ^ q) * Y + y, :, :count] for q in range(2)]
        term = product(split(left(y)), split(jnp.concatenate(parts, 0)))
        total = term if total is None else total + term
    return total


def top_product(where_ref, rows_ref, columns_ref, *refs):
    *in_refs, out_ref, turned_ref, last_ref = refs
    count = out_ref.shape[1]
    total = times_columns(4, where_ref[2], lambda y: rows_ref[y], columns_ref, count)
    out_ref[...] = total
    turned_ref[...] = total.T
    for index, ref in enumerate(in_refs):
        last_ref[index] = ref[...]


def top_terms(where_ref, f1_rows_ref, f1_ref, a_ref, a_rows_ref, f2_rows_ref, f2_ref, *refs):
    p4_ref, other_ref, mine_ref, last_ref = refs
    last_ref[...] = p4_ref[...]
    z = where_ref[2]

    def a_turned(y):
        pieces = []
        for plane in range(4):
            distance = plane ^ (z % 4)
            pieces.append(a_rows_ref[y * 4 + (distance >> 1) + (distance & 1) * 2])
        return jnp.concatenate(pieces, 0)

    one = [split(jnp.concatenate([f1_ref[...], -a_ref[...]], 1))]
    two = [split(a_ref[...]), split(f2_ref[...])]
    first = one[0][0].shape[1]
    share_terms(where_ref, 8, [lambda y: f1_rows_ref[y].T], one, 0, other_ref, mine_ref)
    turned = [a_turned, lambda y: f2_rows_ref[y, 0].T]
    share_terms(where_ref, 4, turned, two, first, other_ref, mine_ref)


def level_terms(planes, where_ref, parent_ref, columns_ref, p_rows_ref, f_rows_ref, own_ref, *refs):
    cross_ref, other_ref, mine_ref = refs
    tiles = parent_ref.shape[0] // Y
    count = own_ref.shape[1]

    def left(y):
        return parent_ref[tiles * y : tiles * y + tiles].reshape(352, 176).T

    total = times_columns(planes, where_ref[2], left, columns_ref, count)
    cross_ref[...] = -total
    turned = [lambda y: p_rows_ref[y, 0].T, lambda y: f_rows_ref[y, 0].T]
    factors = [split(total), split(own_ref[...])]
    share_terms(where_ref, planes, turned, factors, 0, other_ref, mine_ref)


def add_pieces(mine_ref, got_ref, *out_refs):
    for step, out_ref in enumerate(out_refs):
        out_ref[...] = mine_ref[step] + got_ref[step]


def finish(*refs):
    in_refs, (*out_refs, turned_ref) = refs[:XS], refs[XS:]
    total = sum(ref[...] for ref in in_refs)
    at = 0
    for out_ref in out_refs:
        run = total[:, at : at + out_ref.shape[1]]
        out_ref[...] = run
        at += out_ref.shape[1]
    turned_ref[...] = run.T


def local(top_factor, panel_two, panel_three, panel_four, factor_two, factor_three, factor_four):
    leaves = lax.axis_size("leaf")
    fronts = lax.axis_size("front")
    share = top_factor.shape[0]
    width = panel_four.shape[1]
    leaf = lax.axis_index("leaf")
    front = lax.axis_index("front")
    z, x, core = leaf // Y, front // CORES, front % CORES
    where = jnp.stack([x, core, z % 8]).astype(jnp.int32)
    y_groups = [list(range(i, i + Y)) for i in range(0, leaves, Y)]

    def from_plane(value, distance):
        pairs = [(i, ((i // Y) ^ distance) * Y + i % Y) for i in range(leaves)]
        return lax.ppermute(value, "leaf", pairs)

    def from_core(value):
        return lax.ppermute(value, "front", [(i, i ^ 1) for i in range(fronts)])

    def shift_x(value, distance):
        pairs = [
            (i, (i // CORES + distance) % XS * CORES + i % CORES) for i in range(fronts)
        ]
        return lax.ppermute(value, "front", pairs)

    def y_gather(value):
        return lax.all_gather(value, "leaf", axis=0, axis_index_groups=y_groups)

    stack = functools.partial(jax.ShapeDtypeStruct, dtype=jnp.float32)
    tile, tiles = stack((share, width)), stack((XS, share, width))
    scalars = pl.BlockSpec(memory_space=pltpu.SMEM)

    def full(value):
        return pl.BlockSpec(value.shape, lambda i: (0,) * len(value.shape))

    def call(kernel, out_shape, in_specs, flops, *args):
        many = isinstance(out_shape, (tuple, list))
        specs = [full(o) for o in (out_shape if many else [out_shape])]
        return pl.pallas_call(
            kernel,
            out_shape=out_shape,
            grid=(1,),
            in_specs=in_specs,
            out_specs=specs if many else specs[0],
            compiler_params=pltpu.CompilerParams(vmem_limit_bytes=VMEM_BYTES),
            cost_estimate=pl.CostEstimate(
                flops=flops, bytes_accessed=8_000_000, transcendentals=0
            ),
        )(*args)

    def front_total(other, mine, widths):
        got = from_core(other)
        piece = stack(mine.shape[1:])
        pieces = call(
            add_pieces, [piece] * XS, [full(mine), full(got)], 1_000_000, mine, got
        )
        parts = [pieces[0]] + [shift_x(pieces[d], d) for d in (1, 3, 2)]
        outs = [stack((share, w)) for w in widths] + [stack((widths[-1], share))]
        return call(finish, outs, [full(piece)] * XS, 1_000_000, *parts)

    def plane_gather(turned, distances):
        turned = turned[None]
        for distance in distances:
            turned = jnp.concatenate([turned, from_plane(turned, distance)], 0)
        gathered = y_gather(turned)
        return gathered.reshape(-1, *gathered.shape[2:])

    def padded(value):
        return jnp.pad(value, ((0, 0), (0, -value.shape[1] % 128)))

    panels = jnp.concatenate([padded(panel_three), padded(panel_two)], 1)
    panels = lax.all_gather(panels, "front", axis=0)

    def columns_spec(lanes, at):
        return pl.BlockSpec((fronts, share, lanes), lambda i: (0, 0, at))

    def rows_spec(at):
        return pl.BlockSpec((Y, 1, share, width), lambda i: (0, at, 0, 0))

    half = share // 2
    first = top_factor.T
    raw = [factor_two, first, from_plane(first, 4)]
    two = call(turn, stack((half, 2 * share)), [full(v) for v in raw], 1_000_000, *raw)
    raw = [two, from_plane(two, 2), panel_three, factor_three]
    near = call(pack, stack((half, 8 * share)), [full(v) for v in raw], 1_000_000, *raw)
    f1, deep, p3 = call(
        join,
        [tile, stack((2, share, width)), tile],
        [scalars, full(near), full(near), pl.BlockSpec(memory_space=pltpu.HBM)],
        1_000_000,
        where,
        near,
        from_plane(near, 1),
        panels,
    )
    rows = y_gather(deep)

    work = 6 * share * share * XS * width
    count = panel_two.shape[1]
    f1_rows = y_gather(f1)
    inner, turned, last = call(
        top_product,
        [stack((share, count)), stack((count, share)), stack((3, share, width))],
        [scalars, full(f1_rows), columns_spec(128, 2)] + [full(tile)] * 3,
        work // 4,
        where,
        f1_rows,
        panels,
        p3,
        panel_four,
        factor_four,
    )
    last_rows = y_gather(last)
    inner_rows = plane_gather(turned, (2, 1))
    widths = [top_factor.shape[1], count, count]
    sums = stack((XS, share, sum(widths)))
    other, mine, p4 = call(
        top_terms,
        [sums, sums, tile],
        [
            scalars,
            full(f1_rows),
            full(top_factor),
            full(inner),
            full(inner_rows),
            rows_spec(0),
            full(factor_two),
            full(tile),
        ],
        work,
        where,
        f1_rows,
        top_factor,
        inner,
        inner_rows,
        rows,
        factor_two,
        panel_four,
    )
    last_panel = lax.all_gather(p4, "front", axis=0)
    *results, turned = front_total(other, mine, widths)

    for planes, factor, distances, sources, specs in (
        (
            2,
            factor_three,
            (2, 1),
            [panels, last_rows, rows],
            [columns_spec(256, 0), rows_spec(0), rows_spec(1)],
        ),
        (
            1,
            factor_four,
            (1,),
            [last_panel, last_rows, last_rows],
            [columns_spec(width, 0), rows_spec(1), rows_spec(2)],
        ),
    ):
        gathered = plane_gather(turned, distances)
        count = factor.shape[1]
        sums = stack((XS, share, count))
        cross, other, mine = call(
            functools.partial(level_terms, planes),
            [stack((share, count)), sums, sums],
            [scalars, full(gathered), *specs, full(factor)],
            4 * work // planes,
            where,
            gathered,
            *sources,
            factor,
        )
        covariance, turned = front_total(other, mine, [count])
        results += [cross, covariance]
    return tuple(results)


def solution(mesh):
    spec = P("front", "leaf")
    return jax.shard_map(
        local, mesh=mesh, in_specs=(spec,) * 7, out_specs=(spec,) * 7, check_vma=False
    )
```

time: 275 us -> 277 us (level)
  local copies, waits for them, and re-layouts: 4.67 us -> 23.3 us
  waiting for transfers between devices: 81.1 us -> 66.2 us
  Pallas kernels: 30.9 us -> 28.1 us
    unnamed x19 -> x56, local copies, waits for them, and re-layouts: 4.58 us -> 23.3 us
    ppermute x12 -> x9, waiting for transfers between devices: 34.3 us -> 22.2 us  [shift_x(): return lax.ppermute(value, 'front', pairs)]
    ppermute x6 -> x8, starting transfers between devices: 28.9 us -> 37.3 us  [from_plane(): return lax.ppermute(value, 'leaf', pairs)]
    ppermute x12 -> x9, starting transfers between devices: 36 us -> 29.3 us  [shift_x(): return lax.ppermute(value, 'front', pairs)]
    pallas_call x15 -> x13, Pallas kernels: 30.9 us -> 28.1 us  [call(): pl.pallas_call(kernel, out_shape=out_shape, grid=(1,), in_specs=in_specs,...]
    ppermute x4 -> x3, waiting for transfers between devices: 9.14 us -> 7.2 us  [from_core(): return lax.ppermute(value, 'front', [(i, i ^ 1) for i in range(fronts)])]
    ppermute x4 -> x3, starting transfers between devices: 7.63 us -> 5.74 us  [from_core(): return lax.ppermute(value, 'front', [(i, i ^ 1) for i in range(fronts)])]
    ppermute x6 -> x8, waiting for transfers between devices: 37.6 us -> 36.7 us  [from_plane(): return lax.ppermute(value, 'leaf', pairs)]
  transfers between devices with their start and end apart: 25 -> 24, of which waited for: 17 -> 16; matrix products, arithmetic and copies ran while one was open for 0% -> 2% of each run, Pallas kernels for 7% -> 6%
where the time goes in v2:
time: 277 us; the launch traced here: 275 us
  starting transfers between devices  72.4 us (26%)
  blocking collectives  66.9 us (24%)
  waiting for transfers between devices  66.2 us (24%)
  Pallas kernels  28.1 us (10%)
  local copies, waits for them, and re-layouts  23.3 us (8%)
  between operations  14.1 us (5%)
  other arithmetic  4.47 us (2%)
    all_gather x4, blocking collectives, y_gather(): return lax.all_gather(value, 'leaf', axis=0, axis_index_groups=y_groups)  66.9 us
    ppermute x8, starting transfers between devices, from_plane(): return lax.ppermute(value, 'leaf', pairs)  37.3 us
    ppermute x8, waiting for transfers between devices, from_plane(): return lax.ppermute(value, 'leaf', pairs)  36.7 us
    ppermute x9, starting transfers between devices, shift_x(): return lax.ppermute(value, 'front', pairs)  29.3 us
    pallas_call x13, Pallas kernels, call(): pl.pallas_call(kernel, out_shape=out_shape, grid=(1,), in_specs=in_specs,...  28.1 us
    unnamed x56, local copies, waits for them, and re-layouts  23.3 us
    ppermute x9, waiting for transfers between devices, shift_x(): return lax.ppermute(value, 'front', pairs)  22.2 us
    ppermute x3, waiting for transfers between devices, from_core(): return lax.ppermute(value, 'front', [(i, i ^ 1) for i in range(fronts)])  7.2 us
  transfers between devices with their start and end apart: 24, of which 16 were waited for; matrix products, arithmetic and copies ran while one was open for 2% of the time, Pallas kernels for 6%

profile of v2, /device:TPU:6, one launch (start us, length us, event | category | flops | bytes accessed | tf_op | source)
XLA Modules:
  0.0 275.4 jit_solution(15533508035402415876)
XLA Ops:
  7.2 1.7 select_maximum_fusion
  9.0 9.1 %collective-permute-start = (f32[44,176]{1,0:T(8,128)}, f32[44,176]{1,0:T(8,128)S(1)}, u32[]{:S(2)}, u32[]{:S(2)}) collective-permute-start(f32[44,176]{1,0:T(8,128)} %bitcast.24), channel_id=1, source_target_pairs={{0,128},{8,136},{16,144},{24,152},{32,160},{40,168},{48,176},{56,1... | collective-permute-start | bytes 92936 | tf_op jit(solution)/shard_map/ppermute | solution.py:199
  18.1 2.3 collective-permute-done.got_ref
  20.4 0.9 copy-done.16
  22.2 5.4 %collective-permute-start.1 = (f32[88,352]{1,0:T(8,128)S(1)}, f32[88,352]{1,0:T(8,128)S(1)}, u32[]{:S(2)}, u32[]{:S(2)}) collective-permute-start(f32[88,352]{1,0:T(8,128)S(1)} %shard_map.126.two_ref), channel_id=1, source_target_pairs={{0,64},{8,72},{16,80},{24,88},{32,96},{40,104},{48,112},{56,120},{... | collective-permute-start | bytes 371720 | tf_op jit(solution)/shard_map/ppermute | solution.py:199
  27.6 6.6 %collective-permute-done.1.got_ref = f32[88,352]{1,0:T(8,128)S(1)} collective-permute-done((f32[88,352]{1,0:T(8,128)S(1)}, f32[88,352]{1,0:T(8,128)S(1)}, u32[]{:S(2)}, u32[]{:S(2)}) %collective-permute-start.1) | collective-permute-done | bytes 123936 | tf_op jit(solution)/shard_map/ppermute | solution.py:199
  34.3 0.9 copy-done.9
  35.2 0.9 copy-done.12
  36.4 2.6 collective-permute-start.2
  39.2 11.8 %collective-permute-done.2.got_ref = f32[88,1408]{1,0:T(8,128)S(1)} collective-permute-done((f32[88,1408]{1,0:T(8,128)S(1)}, f32[88,1408]{1,0:T(8,128)S(1)}, u32[]{:S(2)}, u32[]{:S(2)}) %collective-permute-start.2) | collective-permute-done | bytes 495648 | tf_op jit(solution)/shard_map/ppermute | solution.py:199
  51.0 1.6 copy-done
  52.6 2.7 shard_map.128
  56.8 15.5 %all-gather.1 = f32[704,352]{1,0:T(8,128)S(1)} all-gather(f32[176,352]{1,0:T(8,128)} %copy-done.21), channel_id=3, replica_groups={{0,8,16,24},{32,40,48,56},{64,72,80,88},{96,104,112,120},{128,136,144,1..., dimensions={0}, use_global_device_ids=true | all-gather | bytes 1239040 | tf_op jit(solution)/shard_map/all_gather | solution.py:211
  72.3 0.9 copy-done.6
  73.3 1.4 shard_map.129
  74.6 0.9 copy-done.8
  76.9 4.9 %collective-permute-start.3 = (f32[1,88,176]{2,1,0:T(8,128)}, f32[1,88,176]{2,1,0:T(8,128)S(1)}, u32[]{:S(2)}, u32[]{:S(2)}) collective-permute-start(f32[1,88,176]{2,1,0:T(8,128)} %bitcast.18), channel_id=1, source_target_pairs={{0,64},{8,72},{16,80},{24,88},{32,96},{40,104},{48,112},{56,120},{... | collective-permute-start | bytes 185864 | tf_op jit(solution)/shard_map/ppermute | solution.py:199
  81.8 2.7 collective-permute-done.3
  85.1 1.6 pad_maximum_fusion.3
  86.7 4.0 %collective-permute-start.4 = (f32[2,88,176]{2,1,0:T(8,128)}, f32[2,88,176]{2,1,0:T(8,128)}, u32[]{:S(2)}, u32[]{:S(2)}) collective-permute-start(f32[2,88,176]{2,1,0:T(8,128)} %pad_maximum_fusion.3), channel_id=1, source_target_pairs={{0,32},{8,40},{16,48},{24,56},{32,0},{40,8},{48,16},{56,24},{64,96... | collective-permute-start | bytes 371720 | tf_op jit(solution)/shard_map/ppermute | solution.py:199
  90.6 1.5 copy.16.f1_ref
  92.2 2.2 collective-permute-done.4
  94.4 1.0 pad_maximum_fusion
  95.5 17.2 %all-gather.2.a_rows_ref = f32[16,88,176]{2,1,0:T(8,128)} all-gather(f32[4,88,176]{2,1,0:T(8,128)S(1)} %pad_maximum_fusion), channel_id=4, replica_groups={{0,8,16,24},{32,40,48,56},{64,72,80,88},{96,104,112,120},{128,136,144,1..., dimensions={0}, use_global_device_ids=true | all-gather | bytes 1239040 | tf_op jit(solution)/shard_map/all_gather | solution.py:211
  112.6 1.4 copy-done.3
  114.0 0.9 copy-done.15
  114.9 0.9 copy-done.17
  115.8 0.9 copy-done.24
  116.7 7.4 %shard_map.130 = (f32[4,176,220]{2,1,0:T(8,128)S(1)}, f32[4,176,220]{2,1,0:T(8,128)S(1)}, f32[176,352]{1,0:T(8,128)S(1)}) custom-call(s32[3]{0:T(128)S(1)} %pad_add_fusion.where_ref, f32[4,176,352]{2,1,0:T(8,128)S(1)} %bitcast.16, f32[176,44]{1,0:T(8,128)S(1)} %copy-done.15, f32[176,88]{1,0:T(8,128)S(1)} %copy-done.24, f32[16,88,176]{2,1,0:T(8,128)S(1)} %copy-done.3, ...), custom_call_target="tpu_custom_call" | custom-call | flops 261685248 | bytes 8000000 | tf_op jit(solution)/shard_map/pallas_call | solution.py:223
  124.1 1.0 copy-done.10
  125.8 0.9 copy-done.25
  126.7 1.9 collective-permute-start.5
  128.6 2.4 collective-permute-done.5.got_ref
  131.0 1.1 copy-done.11
  132.2 2.4 collective-permute-start.6
  134.5 3.5 %collective-permute-start.7 = (f32[176,220]{1,0:T(8,128)S(1)}, f32[176,220]{1,0:T(8,128)S(1)}, u32[]{:S(2)}, u32[]{:S(2)}) collective-permute-start(f32[176,220]{1,0:T(8,128)S(1)} %get-tuple-element.50), channel_id=1, source_target_pairs={{0,6},{1,7},{2,0},{3,1},{4,2},{5,3},{6,4},{7,5},{8,14},{9,15},{10,... | collective-permute-start | bytes 464648 | tf_op jit(solution)/shard_map/ppermute | solution.py:208
  138.0 3.3 %collective-permute-start.8 = (f32[176,220]{1,0:T(8,128)S(1)}, f32[176,220]{1,0:T(8,128)S(1)}, u32[]{:S(2)}, u32[]{:S(2)}) collective-permute-start(f32[176,220]{1,0:T(8,128)S(1)} %get-tuple-element.51), channel_id=1, source_target_pairs={{0,4},{1,5},{2,6},{3,7},{4,0},{5,1},{6,2},{7,3},{8,12},{9,13},{10,... | collective-permute-start | bytes 464648 | tf_op jit(solution)/shard_map/ppermute | solution.py:208
  141.4 6.5 %collective-permute-done.7.refs_2_ = f32[176,220]{1,0:T(8,128)S(1)} collective-permute-done((f32[176,220]{1,0:T(8,128)S(1)}, f32[176,220]{1,0:T(8,128)S(1)}, u32[]{:S(2)}, u32[]{:S(2)}) %collective-permute-start.7) | collective-permute-done | bytes 154912 | tf_op jit(solution)/shard_map/ppermute | solution.py:208
  148.6 4.6 %collective-permute-start.9 = (f32[1,88,176]{2,1,0:T(8,128)S(1)}, f32[1,88,176]{2,1,0:T(8,128)S(1)}, u32[]{:S(2)}, u32[]{:S(2)}) collective-permute-start(f32[1,88,176]{2,1,0:T(8,128)S(1)} %bitcast.21), channel_id=1, source_target_pairs={{0,64},{8,72},{16,80},{24,88},{32,96},{40,104},{48,112},{56,120},{... | collective-permute-start | bytes 185864 | tf_op jit(solution)/shard_map/ppermute | solution.py:199
  153.3 2.8 %collective-permute-done.9 = f32[1,88,176]{2,1,0:T(8,128)S(1)} collective-permute-done((f32[1,88,176]{2,1,0:T(8,128)S(1)}, f32[1,88,176]{2,1,0:T(8,128)S(1)}, u32[]{:S(2)}, u32[]{:S(2)}) %collective-permute-start.9) | collective-permute-done | bytes 61984 | tf_op jit(solution)/shard_map/ppermute | solution.py:199
  156.1 3.6 %collective-permute-start.10 = (f32[2,88,176]{2,1,0:T(8,128)S(1)}, f32[2,88,176]{2,1,0:T(8,128)S(1)}, u32[]{:S(2)}, u32[]{:S(2)}) collective-permute-start(f32[2,88,176]{2,1,0:T(8,128)S(1)} %pad_maximum_fusion.4), channel_id=1, source_target_pairs={{0,32},{8,40},{16,48},{24,56},{32,0},{40,8},{48,16},{56,24},{64,96... | collective-permute-start | bytes 371720 | tf_op jit(solution)/shard_map/ppermute | solution.py:199
  159.7 3.8 %collective-permute-done.10 = f32[2,88,176]{2,1,0:T(8,128)S(1)} collective-permute-done((f32[2,88,176]{2,1,0:T(8,128)S(1)}, f32[2,88,176]{2,1,0:T(8,128)S(1)}, u32[]{:S(2)}, u32[]{:S(2)}) %collective-permute-start.10) | collective-permute-done | bytes 123936 | tf_op jit(solution)/shard_map/ppermute | solution.py:199
  163.5 17.6 %all-gather.4.parent_ref = f32[16,88,176]{2,1,0:T(8,128)} all-gather(f32[4,88,176]{2,1,0:T(8,128)S(1)} %pad_maximum_fusion.1), channel_id=6, replica_groups={{0,8,16,24},{32,40,48,56},{64,72,80,88},{96,104,112,120},{128,136,144,1..., dimensions={0}, use_global_device_ids=true | all-gather | bytes 1239040 | tf_op jit(solution)/shard_map/all_gather | solution.py:211
  181.1 1.4 copy-done.2
  182.5 6.7 %shard_map.133 = (f32[176,176]{1,0:T(8,128)}, f32[4,176,176]{2,1,0:T(8,128)S(1)}, f32[4,176,176]{2,1,0:T(8,128)S(1)}) custom-call(s32[3]{0:T(128)S(1)} %pad_add_fusion.where_ref, f32[16,88,176]{2,1,0:T(8,128)S(1)} %copy-done.2, f32[8,176,384]{2,1,0:T(8,128)S(1)} %bitcast.14, f32[4,3,176,352]{3,2,1,0:T(8,128)} %bitcast.28, f32[4,2,176,352]{3,2,1,0:T(8,128)} %bitcast.32, ...), custom_call_target="tpu_custom_call" | custom-call | flops 523370496 | bytes 8000000 | tf_op jit(solution)/shard_map/pallas_call | solution.py:223
  189.2 1.9 collective-permute-start.11
  191.1 2.2 collective-permute-done.11.got_ref
  193.3 3.1 %collective-permute-start.12 = (f32[176,176]{1,0:T(8,128)S(1)}, f32[176,176]{1,0:T(8,128)S(1)}, u32[]{:S(2)}, u32[]{:S(2)}) collective-permute-start(f32[176,176]{1,0:T(8,128)S(1)} %get-tuple-element.61), channel_id=1, source_target_pairs={{0,2},{1,3},{2,4},{3,5},{4,6},{5,7},{6,0},{7,1},{8,10},{9,11},{10,... | collective-permute-start | bytes 371720 | tf_op jit(solution)/shard_map/ppermute | solution.py:208
  196.4 2.7 collective-permute-start.13
  199.2 5.1 %collective-permute-start.14 = (f32[176,176]{1,0:T(8,128)S(1)}, f32[176,176]{1,0:T(8,128)S(1)}, u32[]{:S(2)}, u32[]{:S(2)}) collective-permute-start(f32[176,176]{1,0:T(8,128)S(1)} %get-tuple-element.63), channel_id=1, source_target_pairs={{0,4},{1,5},{2,6},{3,7},{4,0},{5,1},{6,2},{7,3},{8,12},{9,13},{10,... | collective-permute-start | bytes 371720 | tf_op jit(solution)/shard_map/ppermute | solution.py:208
  204.4 1.8 collective-permute-done.13.refs_2_
  206.1 4.4 %collective-permute-done.14.refs_3_ = f32[176,176]{1,0:T(8,128)S(1)} collective-permute-done((f32[176,176]{1,0:T(8,128)S(1)}, f32[176,176]{1,0:T(8,128)S(1)}, u32[]{:S(2)}, u32[]{:S(2)}) %collective-permute-start.14) | collective-permute-done | bytes 123936 | tf_op jit(solution)/shard_map/ppermute | solution.py:208
  211.3 3.1 %collective-permute-start.15 = (f32[1,176,176]{2,1,0:T(8,128)S(1)}, f32[1,176,176]{2,1,0:T(8,128)S(1)}, u32[]{:S(2)}, u32[]{:S(2)}) collective-permute-start(f32[1,176,176]{2,1,0:T(8,128)S(1)} %bitcast.26), channel_id=1, source_target_pairs={{0,32},{8,40},{16,48},{24,56},{32,0},{40,8},{48,16},{56,24},{64,96... | collective-permute-start | bytes 371720 | tf_op jit(solution)/shard_map/ppermute | solution.py:199
  214.4 4.4 %collective-permute-done.15 = f32[1,176,176]{2,1,0:T(8,128)S(1)} collective-permute-done((f32[1,176,176]{2,1,0:T(8,128)S(1)}, f32[1,176,176]{2,1,0:T(8,128)S(1)}, u32[]{:S(2)}, u32[]{:S(2)}) %collective-permute-start.15) | collective-permute-done | bytes 123936 | tf_op jit(solution)/shard_map/ppermute | solution.py:199
  218.8 16.6 %all-gather.6.parent_ref = f32[8,176,176]{2,1,0:T(8,128)S(1)} all-gather(f32[2,176,176]{2,1,0:T(8,128)S(1)} %pad_maximum_fusion.2), channel_id=8, replica_groups={{0,8,16,24},{32,40,48,56},{64,72,80,88},{96,104,112,120},{128,136,144,1..., dimensions={0}, use_global_device_ids=true | all-gather | bytes 1239040 | tf_op jit(solution)/shard_map/all_gather | solution.py:211
  235.5 1.6 copy-done.4
  237.1 6.8 %shard_map.136 = (f32[176,352]{1,0:T(8,128)}, f32[4,176,352]{2,1,0:T(8,128)S(1)}, f32[4,176,352]{2,1,0:T(8,128)S(1)}) custom-call(s32[3]{0:T(128)S(1)} %pad_add_fusion.where_ref, f32[8,176,176]{2,1,0:T(8,128)S(1)} %all-gather.6.parent_ref, f32[8,176,352]{2,1,0:T(8,128)S(1)} %bitcast.17, f32[4,3,176,352]{3,2,1,0:T(8,128)} %bitcast.29, ...), custom_call_target="tpu_custom_call" | custom-call | flops 1046740992 | bytes 8000000 | tf_op jit(solution)/shard_map/pallas_call | solution.py:223
  243.9 1.9 collective-permute-start.16
  245.8 2.7 collective-permute-done.16.got_ref
  248.6 2.2 collective-permute-start.17
  250.8 3.6 %collective-permute-start.18 = (f32[176,352]{1,0:T(8,128)S(1)}, f32[176,352]{1,0:T(8,128)S(1)}, u32[]{:S(2)}, u32[]{:S(2)}) collective-permute-start(f32[176,352]{1,0:T(8,128)S(1)} %get-tuple-element.72), channel_id=1, source_target_pairs={{0,6},{1,7},{2,0},{3,1},{4,2},{5,3},{6,4},{7,5},{8,14},{9,15},{10,... | collective-permute-start | bytes 743432 | tf_op jit(solution)/shard_map/ppermute | solution.py:208
  254.4 3.3 %collective-permute-start.19 = (f32[176,352]{1,0:T(8,128)S(1)}, f32[176,352]{1,0:T(8,128)S(1)}, u32[]{:S(2)}, u32[]{:S(2)}) collective-permute-start(f32[176,352]{1,0:T(8,128)S(1)} %get-tuple-element.73), channel_id=1, source_target_pairs={{0,4},{1,5},{2,6},{3,7},{4,0},{5,1},{6,2},{7,3},{8,12},{9,13},{10,... | collective-permute-start | bytes 743432 | tf_op jit(solution)/shard_map/ppermute | solution.py:208
  259.1 8.8 %collective-permute-done.18.refs_2_ = f32[176,352]{1,0:T(8,128)S(1)} collective-permute-done((f32[176,352]{1,0:T(8,128)S(1)}, f32[176,352]{1,0:T(8,128)S(1)}, u32[]{:S(2)}, u32[]{:S(2)}) %collective-permute-start.18) | collective-permute-done | bytes 247840 | tf_op jit(solution)/shard_map/ppermute | solution.py:208
  267.9 0.9 shard_map.138
  (68 shorter events, 8.9 us)
Async XLA Ops:
  7.2 43.9 %all-gather.13.cloned.1.call-start = ((), (), s32[]{:S(2)}) async-start(), calls=%async_computation | async-start | bytes 2433024 | tf_op jit(solution)/shard_map/all_gather | solution.py:256
  8.9 103.7 %all-gather.15.cloned.1.call-start = ((), (), s32[]{:S(2)}) async-start(), calls=%async_computation.1 | async-start | bytes 2703360 | tf_op jit(solution)/shard_map/all_gather | solution.py:211
  9.0 11.4 %collective-permute-start = (f32[44,176]{1,0:T(8,128)}, f32[44,176]{1,0:T(8,128)S(1)}, u32[]{:S(2)}, u32[]{:S(2)}) collective-permute-start(f32[44,176]{1,0:T(8,128)} %bitcast.24), channel_id=1, source_target_pairs={{0,128},{8,136},{16,144},{24,152},{32,160},{40,168},{48,176},{56,1... | collective-permute-start | bytes 92936 | tf_op jit(solution)/shard_map/ppermute | solution.py:199
  20.4 0.9 copy-start.16
  21.2 0.8 copy-start.22
  22.2 12.1 %collective-permute-start.1 = (f32[88,352]{1,0:T(8,128)S(1)}, f32[88,352]{1,0:T(8,128)S(1)}, u32[]{:S(2)}, u32[]{:S(2)}) collective-permute-start(f32[88,352]{1,0:T(8,128)S(1)} %shard_map.126.two_ref), channel_id=1, source_target_pairs={{0,64},{8,72},{16,80},{24,88},{32,96},{40,104},{48,112},{56,120},{... | collective-permute-start | bytes 371720 | tf_op jit(solution)/shard_map/ppermute | solution.py:199
  34.3 0.9 copy-start.9
  35.2 0.9 copy-start.12
  36.4 14.6 %collective-permute-start.2 = (f32[88,1408]{1,0:T(8,128)S(1)}, f32[88,1408]{1,0:T(8,128)S(1)}, u32[]{:S(2)}, u32[]{:S(2)}) collective-permute-start(f32[88,1408]{1,0:T(8,128)S(1)} %shard_map.127.own_ref), channel_id=1, source_target_pairs={{0,32},{8,40},{16,48},{24,56},{32,0},{40,8},{48,16},{56,24},{64,96... | collective-permute-start | bytes 1486856 | tf_op jit(solution)/shard_map/ppermute | solution.py:199
  51.0 1.6 copy-start
  52.6 19.7 %copy-start.1 = (f32[1408,384]{1,0:T(8,128)S(1)}, f32[1408,384]{1,0:T(8,128)}, u32[]{:S(2)}) copy-start(f32[1408,384]{1,0:T(8,128)} %all-gather.13.cloned.1.call-done) | copy-start | bytes 6488068
  55.3 0.7 copy-start.18
  56.0 0.7 copy-start.21
  56.7 15.6 %copy-start.5 = (f32[176,352]{1,0:T(8,128)S(1)}, f32[176,352]{1,0:T(8,128)}, u32[]{:S(2)}) copy-start(f32[176,352]{1,0:T(8,128)} %refs_0_.1) | copy-start | bytes 743428
  56.7 124.4 %all-gather.17.cloned.1.call-start = ((), (), s32[]{:S(2)}) async-start(), calls=%async_computation.2 | async-start | bytes 4055040 | tf_op jit(solution)/shard_map/all_gather | solution.py:211
  56.8 15.5 %copy-start.19 = (f32[176,352]{1,0:T(8,128)S(1)}, f32[176,352]{1,0:T(8,128)}, u32[]{:S(2)}) copy-start(f32[176,352]{1,0:T(8,128)} %copy-done.18) | copy-start | bytes 743428
  72.3 1.0 copy-start.6
  74.6 0.9 copy-start.8
  75.5 0.6 copy-start.14
  76.2 0.6 copy-start.23
  76.8 158.6 %all-gather.19.cloned.1.call-start = ((), (), s32[]{:S(2)}) async-start(), calls=%async_computation.3 | async-start | bytes 2433024 | tf_op jit(solution)/shard_map/all_gather | solution.py:324
  76.9 7.6 %collective-permute-start.3 = (f32[1,88,176]{2,1,0:T(8,128)}, f32[1,88,176]{2,1,0:T(8,128)S(1)}, u32[]{:S(2)}, u32[]{:S(2)}) collective-permute-start(f32[1,88,176]{2,1,0:T(8,128)} %bitcast.18), channel_id=1, source_target_pairs={{0,64},{8,72},{16,80},{24,88},{32,96},{40,104},{48,112},{56,120},{... | collective-permute-start | bytes 185864 | tf_op jit(solution)/shard_map/ppermute | solution.py:199
  84.5 0.6 copy-start.26
  86.7 7.7 %collective-permute-start.4 = (f32[2,88,176]{2,1,0:T(8,128)}, f32[2,88,176]{2,1,0:T(8,128)}, u32[]{:S(2)}, u32[]{:S(2)}) collective-permute-start(f32[2,88,176]{2,1,0:T(8,128)} %pad_maximum_fusion.3), channel_id=1, source_target_pairs={{0,32},{8,40},{16,48},{24,56},{32,0},{40,8},{48,16},{56,24},{64,96... | collective-permute-start | bytes 371720 | tf_op jit(solution)/shard_map/ppermute | solution.py:199
  112.6 1.4 copy-start.3
  114.0 0.9 copy-start.15
  114.9 0.9 copy-start.17
  115.8 0.9 copy-start.24
  124.1 1.0 copy-start.10
  125.1 0.7 copy-start.20
  125.8 0.9 copy-start.25
  126.7 4.3 %collective-permute-start.5 = (f32[4,176,220]{2,1,0:T(8,128)}, f32[4,176,220]{2,1,0:T(8,128)S(1)}, u32[]{:S(2)}, u32[]{:S(2)}) collective-permute-start(f32[4,176,220]{2,1,0:T(8,128)} %copy-done.25), channel_id=1, source_target_pairs={{0,1},{1,0},{2,3},{3,2},{4,5},{5,4},{6,7},{7,6},{8,9},{9,8},{10,11... | collective-permute-start | bytes 1858568 | tf_op jit(solution)/shard_map/ppermute | solution.py:202
  131.0 1.1 copy-start.11
  132.2 9.2 %collective-permute-start.6 = (f32[176,220]{1,0:T(8,128)S(1)}, f32[176,220]{1,0:T(8,128)S(1)}, u32[]{:S(2)}, u32[]{:S(2)}) collective-permute-start(f32[176,220]{1,0:T(8,128)S(1)} %get-tuple-element.49), channel_id=1, source_target_pairs={{0,2},{1,3},{2,4},{3,5},{4,6},{5,7},{6,0},{7,1},{8,10},{9,11},{10,... | collective-permute-start | bytes 464648 | tf_op jit(solution)/shard_map/ppermute | solution.py:208
  134.5 13.3 %collective-permute-start.7 = (f32[176,220]{1,0:T(8,128)S(1)}, f32[176,220]{1,0:T(8,128)S(1)}, u32[]{:S(2)}, u32[]{:S(2)}) collective-permute-start(f32[176,220]{1,0:T(8,128)S(1)} %get-tuple-element.50), channel_id=1, source_target_pairs={{0,6},{1,7},{2,0},{3,1},{4,2},{5,3},{6,4},{7,5},{8,14},{9,15},{10,... | collective-permute-start | bytes 464648 | tf_op jit(solution)/shard_map/ppermute | solution.py:208
  138.0 9.8 %collective-permute-start.8 = (f32[176,220]{1,0:T(8,128)S(1)}, f32[176,220]{1,0:T(8,128)S(1)}, u32[]{:S(2)}, u32[]{:S(2)}) collective-permute-start(f32[176,220]{1,0:T(8,128)S(1)} %get-tuple-element.51), channel_id=1, source_target_pairs={{0,4},{1,5},{2,6},{3,7},{4,0},{5,1},{6,2},{7,3},{8,12},{9,13},{10,... | collective-permute-start | bytes 464648 | tf_op jit(solution)/shard_map/ppermute | solution.py:208
  148.6 32.5 %copy-start.13 = (f32[176,176]{1,0:T(8,128)S(1)}, f32[176,176]{1,0:T(8,128)}, u32[]{:S(2)}) copy-start(f32[176,176]{1,0:T(8,128)} %own_ref.2) | copy-start | bytes 371716
  148.6 7.5 %collective-permute-start.9 = (f32[1,88,176]{2,1,0:T(8,128)S(1)}, f32[1,88,176]{2,1,0:T(8,128)S(1)}, u32[]{:S(2)}, u32[]{:S(2)}) collective-permute-start(f32[1,88,176]{2,1,0:T(8,128)S(1)} %bitcast.21), channel_id=1, source_target_pairs={{0,64},{8,72},{16,80},{24,88},{32,96},{40,104},{48,112},{56,120},{... | collective-permute-start | bytes 185864 | tf_op jit(solution)/shard_map/ppermute | solution.py:199
  156.1 7.4 %collective-permute-start.10 = (f32[2,88,176]{2,1,0:T(8,128)S(1)}, f32[2,88,176]{2,1,0:T(8,128)S(1)}, u32[]{:S(2)}, u32[]{:S(2)}) collective-permute-start(f32[2,88,176]{2,1,0:T(8,128)S(1)} %pad_maximum_fusion.4), channel_id=1, source_target_pairs={{0,32},{8,40},{16,48},{24,56},{32,0},{40,8},{48,16},{56,24},{64,96... | collective-permute-start | bytes 371720 | tf_op jit(solution)/shard_map/ppermute | solution.py:199
  181.1 1.4 copy-start.2
  189.2 4.1 %collective-permute-start.11 = (f32[4,176,176]{2,1,0:T(8,128)S(1)}, f32[4,176,176]{2,1,0:T(8,128)S(1)}, u32[]{:S(2)}, u32[]{:S(2)}) collective-permute-start(f32[4,176,176]{2,1,0:T(8,128)S(1)} %get-tuple-element.59), channel_id=1, source_target_pairs={{0,1},{1,0},{2,3},{3,2},{4,5},{5,4},{6,7},{7,6},{8,9},{9,8},{10,11... | collective-permute-start | bytes 1486856 | tf_op jit(solution)/shard_map/ppermute | solution.py:202
  193.3 11.0 %collective-permute-start.12 = (f32[176,176]{1,0:T(8,128)S(1)}, f32[176,176]{1,0:T(8,128)S(1)}, u32[]{:S(2)}, u32[]{:S(2)}) collective-permute-start(f32[176,176]{1,0:T(8,128)S(1)} %get-tuple-element.61), channel_id=1, source_target_pairs={{0,2},{1,3},{2,4},{3,5},{4,6},{5,7},{6,0},{7,1},{8,10},{9,11},{10,... | collective-permute-start | bytes 371720 | tf_op jit(solution)/shard_map/ppermute | solution.py:208
  196.4 9.7 %collective-permute-start.13 = (f32[176,176]{1,0:T(8,128)S(1)}, f32[176,176]{1,0:T(8,128)S(1)}, u32[]{:S(2)}, u32[]{:S(2)}) collective-permute-start(f32[176,176]{1,0:T(8,128)S(1)} %get-tuple-element.62), channel_id=1, source_target_pairs={{0,6},{1,7},{2,0},{3,1},{4,2},{5,3},{6,4},{7,5},{8,14},{9,15},{10,... | collective-permute-start | bytes 371720 | tf_op jit(solution)/shard_map/ppermute | solution.py:208
  199.2 11.4 %collective-permute-start.14 = (f32[176,176]{1,0:T(8,128)S(1)}, f32[176,176]{1,0:T(8,128)S(1)}, u32[]{:S(2)}, u32[]{:S(2)}) collective-permute-start(f32[176,176]{1,0:T(8,128)S(1)} %get-tuple-element.63), channel_id=1, source_target_pairs={{0,4},{1,5},{2,6},{3,7},{4,0},{5,1},{6,2},{7,3},{8,12},{9,13},{10,... | collective-permute-start | bytes 371720 | tf_op jit(solution)/shard_map/ppermute | solution.py:208
  211.3 24.2 %copy-start.7 = (f32[176,352]{1,0:T(8,128)S(1)}, f32[176,352]{1,0:T(8,128)}, u32[]{:S(2)}) copy-start(f32[176,352]{1,0:T(8,128)} %own_ref.3) | copy-start | bytes 743428
  211.3 7.5 %collective-permute-start.15 = (f32[1,176,176]{2,1,0:T(8,128)S(1)}, f32[1,176,176]{2,1,0:T(8,128)S(1)}, u32[]{:S(2)}, u32[]{:S(2)}) collective-permute-start(f32[1,176,176]{2,1,0:T(8,128)S(1)} %bitcast.26), channel_id=1, source_target_pairs={{0,32},{8,40},{16,48},{24,56},{32,0},{40,8},{48,16},{56,24},{64,96... | collective-permute-start | bytes 371720 | tf_op jit(solution)/shard_map/ppermute | solution.py:199
  235.5 1.6 copy-start.4
  243.9 4.6 %collective-permute-start.16 = (f32[4,176,352]{2,1,0:T(8,128)S(1)}, f32[4,176,352]{2,1,0:T(8,128)S(1)}, u32[]{:S(2)}, u32[]{:S(2)}) collective-permute-start(f32[4,176,352]{2,1,0:T(8,128)S(1)} %get-tuple-element.69), channel_id=1, source_target_pairs={{0,1},{1,0},{2,3},{3,2},{4,5},{5,4},{6,7},{7,6},{8,9},{9,8},{10,11... | collective-permute-start | bytes 2973704 | tf_op jit(solution)/shard_map/ppermute | solution.py:202
  248.6 10.5 %collective-permute-start.17 = (f32[176,352]{1,0:T(8,128)S(1)}, f32[176,352]{1,0:T(8,128)S(1)}, u32[]{:S(2)}, u32[]{:S(2)}) collective-permute-start(f32[176,352]{1,0:T(8,128)S(1)} %get-tuple-element.71), channel_id=1, source_target_pairs={{0,2},{1,3},{2,4},{3,5},{4,6},{5,7},{6,0},{7,1},{8,10},{9,11},{10,... | collective-permute-start | bytes 743432 | tf_op jit(solution)/shard_map/ppermute | solution.py:208
  250.8 17.1 %collective-permute-start.18 = (f32[176,352]{1,0:T(8,128)S(1)}, f32[176,352]{1,0:T(8,128)S(1)}, u32[]{:S(2)}, u32[]{:S(2)}) collective-permute-start(f32[176,352]{1,0:T(8,128)S(1)} %get-tuple-element.72), channel_id=1, source_target_pairs={{0,6},{1,7},{2,0},{3,1},{4,2},{5,3},{6,4},{7,5},{8,14},{9,15},{10,... | collective-permute-start | bytes 743432 | tf_op jit(solution)/shard_map/ppermute | solution.py:208
  254.4 13.5 %collective-permute-start.19 = (f32[176,352]{1,0:T(8,128)S(1)}, f32[176,352]{1,0:T(8,128)S(1)}, u32[]{:S(2)}, u32[]{:S(2)}) collective-permute-start(f32[176,352]{1,0:T(8,128)S(1)} %get-tuple-element.73), channel_id=1, source_target_pairs={{0,4},{1,5},{2,6},{3,7},{4,0},{5,1},{6,2},{7,3},{8,12},{9,13},{10,... | collective-permute-start | bytes 743432 | tf_op jit(solution)/shard_map/ppermute | solution.py:208
Sparse Core Ops, SparseCore 0:
  10.7 36.2 all-gather.12
  56.9 39.4 all-gather.14
  98.5 49.5 all-gather.16
  150.6 31.9 all-gather.18

commit v3 on v2

v3 whole, which is shorter than its diff:
```python
import functools

import jax
import jax.numpy as jnp
from jax import lax
from jax.experimental import pallas as pl
from jax.experimental.pallas import tpu as pltpu
from jax.sharding import PartitionSpec as P

Y = 4
XS = 4
CORES = 2
VMEM_BYTES = 52 * 1024 * 1024


class Staged:

    def __init__(self, source, index, scratch, semaphore):
        self.copy = pltpu.make_async_copy(source.at[index], scratch, semaphore)
        self.scratch, self.waited = scratch, False
        self.copy.start()

    def ready(self):
        if not self.waited:
            self.copy.wait()
            self.waited = True
        return self.scratch


def split(value):
    high = value.astype(jnp.bfloat16)
    low = (value - high.astype(jnp.float32)).astype(jnp.bfloat16)
    return high, low


def product(first, second):
    (fh, fl), (sh, sl) = first, second
    run = functools.partial(jnp.dot, preferred_element_type=jnp.float32)
    return run(fh, sh) + (run(fh, sl) + run(fl, sh))


def block_of(ref, index):
    return ref[:, index * 176 : (index + 1) * 176]


def turn(f2, own, got_ref, out_ref):
    top = jnp.concatenate([own.ready()[...], got_ref[...]], 0)
    out_ref[...] = jnp.concatenate([f2.ready()[...].T, top], 1)


def pack(two_ref, got_ref, p3, f3, out_ref):
    parts = [two_ref[...], got_ref[...]]
    for staged in (p3, f3):
        turned = staged.ready()[...].T
        parts += [turned[:88], turned[88:]]
    out_ref[...] = jnp.concatenate(parts, 1)


def join(where_ref, own_ref, got_ref, panels_ref, f1_ref, rows_ref):
    del panels_ref
    z = where_ref[2]

    def at(which, distance):
        far = ((distance >> 1) & 1) == 1
        own = jnp.where(far, block_of(own_ref, which + 2), block_of(own_ref, which))
        got = jnp.where(far, block_of(got_ref, which + 2), block_of(got_ref, which))
        return jnp.where((distance & 1) == 1, got, own)

    pieces = []
    for plane in range(8):
        distance = plane ^ z
        both = at(1, distance)
        pieces.append(jnp.where((distance >> 2) == 1, both[44:], both[:44]))
    f1_ref[...] = jnp.concatenate(pieces, 0).T
    pieces = [at(0, plane ^ (z % 4)) for plane in range(4)]
    rows_ref[0] = jnp.concatenate(pieces, 0).T
    for which in range(2):
        pieces = []
        for plane in range(2):
            near = plane == (z % 2)
            for index in (4 + 2 * which, 5 + 2 * which):
                pieces.append(
                    jnp.where(near, block_of(own_ref, index), block_of(got_ref, index))
                )
        rows_ref[1 + which] = jnp.concatenate(pieces, 0).T


def share_terms(where_ref, planes, turned, factors, first, other_ref, mine_ref):
    x, core = where_ref[0], where_ref[1]
    last = first + factors[0][0].shape[1]
    for y in range(Y):
        total = None
        for tile, factor in zip(turned, factors):
            term = product(split(tile(y)), factor)
            total = term if total is None else total + term
        width = total.shape[0] // planes
        step = min(width, 176)
        for plane in range(planes):
            for part in range(0, width, step):
                column = (plane * Y + y) * width + part
                block, offset = column // 176, column % 176
                value = total[plane * width + part : plane * width + part + step]
                at = (block // CORES - x) % XS
                same = core == (block % CORES)

                @pl.when(same)
                def _():
                    mine_ref[at, offset : offset + step, first:last] = value

                @pl.when(jnp.logical_not(same))
                def _():
                    other_ref[at, offset : offset + step, first:last] = value


def times_columns(planes, z, left, columns_ref, count):
    total = None
    for y in range(Y):
        if planes == 4:
            parts = [
                columns_ref[p, y * 44 : (y + 1) * 44, :count] for p in range(8)
            ]
        elif planes == 2:
            low = (y % 2) * 88
            parts = []
            for q in range(4):
                p = (z % 4) ^ ((q & 1) * 2 + (q >> 1))
                parts.append(columns_ref[p * 2 + y // 2, low : low + 88, :count])
        else:
            parts = [columns_ref[((z % 2) ^ q) * Y + y, :, :count] for q in range(2)]
        term = product(split(left(y)), split(jnp.concatenate(parts, 0)))
        total = term if total is None else total + term
    return total


def top_product(where_ref, rows_ref, columns, p4_ref, f4_ref, out_ref, turned_ref, last_ref, sems):
    copies = [
        pltpu.make_async_copy(ref, last_ref.at[index], sems.at[index])
        for index, ref in enumerate((p4_ref, f4_ref))
    ]
    for copy in copies:
        copy.start()
    count = out_ref.shape[1]
    left = rows_ref.ready()
    total = times_columns(4, where_ref[2], lambda y: left[y], columns.ready(), count)
    out_ref[...] = total
    turned_ref[...] = total.T
    for copy in copies:
        copy.wait()


def top_terms(where_ref, f1_rows, f1, a_ref, a_rows, f2_rows, f2, other_ref, mine_ref):
    z = where_ref[2]

    def a_turned(y):
        ref = a_rows.ready()
        pieces = []
        for plane in range(4):
            distance = plane ^ (z % 4)
            pieces.append(ref[y * 4 + (distance >> 1) + (distance & 1) * 2])
        return jnp.concatenate(pieces, 0)

    one = [split(jnp.concatenate([f1.ready()[...].T, -a_ref[...]], 1))]
    two = [split(a_ref[...]), split(f2.ready()[...])]
    first = one[0][0].shape[1]
    turned = [lambda y: f1_rows.ready()[y].T]
    share_terms(where_ref, 8, turned, one, 0, other_ref, mine_ref)
    turned = [a_turned, lambda y: f2_rows.ready()[y].T]
    share_terms(where_ref, 4, turned, two, first, other_ref, mine_ref)


def level_terms(planes, where_ref, parent, columns, p_rows, f_rows, own, *refs):
    cross_ref, other_ref, mine_ref = refs
    tiles = parent.scratch.shape[0] // Y
    count = cross_ref.shape[1]

    def left(y):
        return parent.ready()[tiles * y : tiles * y + tiles].reshape(352, 176).T

    total = times_columns(planes, where_ref[2], left, columns.ready(), count)
    cross_ref[...] = -total
    turned = [lambda y: p_rows.ready()[y].T, lambda y: f_rows.ready()[y].T]
    factors = [split(total), split(own.ready()[...])]
    share_terms(where_ref, planes, turned, factors, 0, other_ref, mine_ref)


def add_pieces(mine_ref, got_ref, *out_refs):
    for step, out_ref in enumerate(out_refs):
        out_ref[...] = mine_ref[step] + got_ref[step]


def finish(flip, *refs):
    in_refs, (*out_refs, turned_ref) = refs[:XS], refs[XS:]
    total = sum(ref[...] for ref in in_refs)
    at = 0
    for index, out_ref in enumerate(out_refs):
        turn_it = flip and index == 0
        count = out_ref.shape[0 if turn_it else 1]
        run = total[:, at : at + count]
        out_ref[...] = run.T if turn_it else run
        at += count
    turned_ref[...] = run.T


def local(top_factor, panel_two, panel_three, panel_four, factor_two, factor_three, factor_four):
    leaves = lax.axis_size("leaf")
    fronts = lax.axis_size("front")
    share = top_factor.shape[0]
    width = panel_four.shape[1]
    leaf = lax.axis_index("leaf")
    front = lax.axis_index("front")
    z, x, core = leaf // Y, front // CORES, front % CORES
    where = jnp.stack([x, core, z % 8]).astype(jnp.int32)
    y_groups = [list(range(i, i + Y)) for i in range(0, leaves, Y)]

    def from_plane(value, distance):
        pairs = [(i, ((i // Y) ^ distance) * Y + i % Y) for i in range(leaves)]
        return lax.ppermute(value, "leaf", pairs)

    def from_core(value):
        return lax.ppermute(value, "front", [(i, i ^ 1) for i in range(fronts)])

    def shift_x(value, distance):
        pairs = [
            (i, (i // CORES + distance) % XS * CORES + i % CORES) for i in range(fronts)
        ]
        return lax.ppermute(value, "front", pairs)

    def y_gather(value):
        return lax.all_gather(value, "leaf", axis=0, axis_index_groups=y_groups)

    stack = functools.partial(jax.ShapeDtypeStruct, dtype=jnp.float32)
    tile, tiles = stack((share, width)), stack((XS, share, width))
    def near_by(value):
        return ("near", value)

    def in_hbm(value):
        return ("hbm", value)

    def staged(value, *index):
        index = index or (slice(None),) * value.ndim
        part = jax.eval_shape(lambda v: v[index], value)
        return ("staged", value, index, part)

    def call(kernel, out_shape, flops, *inputs, hbm_outs=(), semaphores=0):
        specs, arrays, scratch = [], [], []
        for kind, value, *rest in inputs:
            arrays.append(value)
            if kind == "near":
                specs.append(pl.BlockSpec(value.shape, lambda i, n=value.ndim: (0,) * n))
            elif kind == "smem":
                specs.append(pl.BlockSpec(memory_space=pltpu.SMEM))
            else:
                specs.append(pl.BlockSpec(memory_space=pltpu.HBM))
            if kind == "staged":
                scratch.append(pltpu.VMEM(rest[1].shape, rest[1].dtype))
        count = len(scratch)
        scratch.append(pltpu.SemaphoreType.DMA((count + 1,)))
        if semaphores:
            scratch.append(pltpu.SemaphoreType.DMA((semaphores,)))

        def body(*refs):
            ins, rest = list(refs[: len(inputs)]), refs[len(inputs) :]
            outs, rest = rest[: len(out_shape)], rest[len(out_shape) :]
            parts, sems, more = rest[:count], rest[count], rest[count + 1 :]
            at = 0
            for index, (kind, *entry) in enumerate(inputs):
                if kind == "staged":
                    ins[index] = Staged(ins[index], entry[1], parts[at], sems.at[at])
                    at += 1
            kernel(*ins, *outs, *more)
            for value in ins:
                if isinstance(value, Staged):
                    value.ready()

        out_specs = [
            pl.BlockSpec(memory_space=pltpu.HBM)
            if index in hbm_outs
            else pl.BlockSpec(o.shape, lambda i, n=len(o.shape): (0,) * n)
            for index, o in enumerate(out_shape)
        ]
        return pl.pallas_call(
            body,
            out_shape=out_shape,
            grid=(1,),
            in_specs=specs,
            out_specs=out_specs,
            scratch_shapes=scratch,
            compiler_params=pltpu.CompilerParams(vmem_limit_bytes=VMEM_BYTES),
            cost_estimate=pl.CostEstimate(
                flops=flops, bytes_accessed=8_000_000, transcendentals=0
            ),
        )(*arrays)

    def front_total(other, mine, widths, flip=False):
        got = from_core(other)
        piece = stack(mine.shape[1:])
        pieces = call(add_pieces, [piece] * XS, 1_000_000, near_by(mine), near_by(got))
        parts = [pieces[0]] + [shift_x(pieces[d], d) for d in (1, 3, 2)]
        outs = [stack((share, w)) for w in widths] + [stack((widths[-1], share))]
        if flip:
            outs[0] = stack(outs[0].shape[::-1])
        kernel = functools.partial(finish, flip)
        return call(kernel, outs, 1_000_000, *[near_by(part) for part in parts])

    def plane_gather(turned, distances):
        turned = turned[None]
        for distance in distances:
            turned = jnp.concatenate([turned, from_plane(turned, distance)], 0)
        gathered = y_gather(turned)
        return gathered.reshape(-1, *gathered.shape[2:])

    def padded(value):
        return jnp.pad(value, ((0, 0), (0, -value.shape[1] % 128)))

    panels = jnp.concatenate([padded(panel_four), padded(panel_two), padded(panel_three)], 1)
    panels = lax.all_gather(panels, "front", axis=0)
    lanes = slice(None), slice(None)
    where = ("smem", where)

    half = share // 2
    first = top_factor.T
    (two,) = call(
        turn,
        [stack((half, 2 * share))],
        1_000_000,
        staged(factor_two),
        staged(first),
        near_by(from_plane(first, 4)),
    )
    (near,) = call(
        pack,
        [stack((half, 8 * share))],
        1_000_000,
        near_by(two),
        near_by(from_plane(two, 2)),
        staged(panel_three),
        staged(factor_three),
    )
    f1, deep = call(
        join,
        [tile, stack((3, share, width))],
        1_000_000,
        where,
        near_by(near),
        near_by(from_plane(near, 1)),
        in_hbm(panels),
    )
    rows = y_gather(deep)

    work = 6 * share * share * XS * width
    count = panel_two.shape[1]
    f1_rows = y_gather(f1)
    inner, turned, last = call(
        top_product,
        [stack((share, count)), stack((count, share)), stack((2, share, width))],
        work // 4,
        where,
        staged(f1_rows),
        staged(panels, *lanes, slice(384, 512)),
        in_hbm(panel_four),
        in_hbm(factor_four),
        hbm_outs=(2,),
        semaphores=2,
    )
    last_rows = y_gather(last)
    inner_rows = plane_gather(turned, (2, 1))
    widths = [top_factor.shape[1], count, count]
    sums = stack((XS, share, sum(widths)))
    other, mine = call(
        top_terms,
        [sums, sums],
        work,
        where,
        staged(f1_rows),
        staged(first),
        near_by(inner),
        staged(inner_rows),
        staged(rows, slice(None), 0),
        staged(factor_two),
    )
    top, *results, turned = front_total(other, mine, widths, flip=True)
    results = [top.T] + results

    for planes, factor, distances, sources, at, columns in (
        (2, factor_three, (2, 1), [rows, rows], (1, 2), slice(512, 768)),
        (1, factor_four, (1,), [last_rows, last_rows], (0, 1), slice(0, 384)),
    ):
        gathered = plane_gather(turned, distances)
        count = factor.shape[1]
        sums = stack((XS, share, count))
        cross, other, mine = call(
            functools.partial(level_terms, planes),
            [stack((share, count)), sums, sums],
            4 * work // planes,
            where,
            staged(gathered),
            staged(panels, *lanes, columns),
            *[staged(source, slice(None), n) for source, n in zip(sources, at)],
            staged(factor),
        )
        covariance, turned = front_total(other, mine, [count])
        results += [cross, covariance]
    return tuple(results)


def solution(mesh):
    spec = P("front", "leaf")
    return jax.shard_map(
        local, mesh=mesh, in_specs=(spec,) * 7, out_specs=(spec,) * 7, check_vma=False
    )
```

time: 277 us -> 280 us (1.011)
  local copies, waits for them, and re-layouts: 23.3 us -> 2.78 us
  Pallas kernels: 28.1 us -> 37.7 us
  blocking collectives: 66.9 us -> 75.8 us
  waiting for transfers between devices: 66.2 us -> 74.9 us
    unnamed x56 -> x18, local copies, waits for them, and re-layouts: 23.3 us -> 2.78 us
    pallas_call x13, Pallas kernels: 28.1 us -> 37.7 us  [call(): pl.pallas_call(body, out_shape=out_shape, grid=(1,), in_specs=specs, out_...]
    all_gather x4, blocking collectives: 66.9 us -> 75.8 us  [y_gather(): return lax.all_gather(value, 'leaf', axis=0, axis_index_groups=y_groups)]
    all_gather x1, waiting for transfers between devices: 0.01 us -> 4.78 us  [local(): panels = lax.all_gather(panels, 'front', axis=0)]
  transfers between devices with their start and end apart: 24 -> 23, of which waited for: 16 -> 18; matrix products, arithmetic and copies ran while one was open for 2% -> 0% of each run, Pallas kernels for 6% -> 8%
where the time goes in v3:
time: 280 us; the launch traced here: 279 us
  blocking collectives  75.8 us (27%)
  waiting for transfers between devices  74.9 us (27%)
  starting transfers between devices  71.8 us (26%)
  Pallas kernels  37.7 us (13%)
  between operations  14.2 us (5%)
    all_gather x4, blocking collectives, y_gather(): return lax.all_gather(value, 'leaf', axis=0, axis_index_groups=y_groups)  75.8 us
    ppermute x8, waiting for transfers between devices, from_plane(): return lax.ppermute(value, 'leaf', pairs)  38.2 us
    pallas_call x13, Pallas kernels, call(): pl.pallas_call(body, out_shape=out_shape, grid=(1,), in_specs=specs, out_...  37.7 us
    ppermute x8, starting transfers between devices, from_plane(): return lax.ppermute(value, 'leaf', pairs)  36.8 us
    ppermute x9, starting transfers between devices, shift_x(): return lax.ppermute(value, 'front', pairs)  29.2 us
    ppermute x9, waiting for transfers between devices, shift_x(): return lax.ppermute(value, 'front', pairs)  24.5 us
    ppermute x3, waiting for transfers between devices, from_core(): return lax.ppermute(value, 'front', [(i, i ^ 1) for i in range(fronts)])  6.99 us
    ppermute x3, starting transfers between devices, from_core(): return lax.ppermute(value, 'front', [(i, i ^ 1) for i in range(fronts)])  5.76 us
  transfers between devices with their start and end apart: 23, of which 18 were waited for; matrix products, arithmetic and copies ran while one was open for 0% of the time, Pallas kernels for 8%

profile of v3, /device:TPU:6, one launch (start us, length us, event | category | flops | bytes accessed | tf_op | source)
XLA Modules:
  0.0 279.3 jit_solution(7733498466437845861)
XLA Ops:
  7.2 0.0 all-gather.11.cloned.1.call-start
  7.3 2.0 select_maximum_fusion
  9.3 0.0 all-gather.13.cloned.1.call-start
  9.4 9.1 %collective-permute-start = (f32[44,176]{1,0:T(8,128)S(1)}, f32[44,176]{1,0:T(8,128)S(1)}, u32[]{:S(2)}, u32[]{:S(2)}) collective-permute-start(f32[44,176]{1,0:T(8,128)S(1)} %bitcast.18), channel_id=1, source_target_pairs={{0,128},{8,136},{16,144},{24,152},{32,160},{40,168},{48,176},{56,1... | collective-permute-start | bytes 92936 | tf_op jit(solution)/shard_map/ppermute | solution.py:217
  18.5 2.1 collective-permute-done.refs_2_
  20.5 0.3 shard_map.126.refs_0_
  20.9 5.3 %collective-permute-start.1 = (f32[88,352]{1,0:T(8,128)S(1)}, f32[88,352]{1,0:T(8,128)S(1)}, u32[]{:S(2)}, u32[]{:S(2)}) collective-permute-start(f32[88,352]{1,0:T(8,128)S(1)} %shard_map.126.refs_0_), channel_id=1, source_target_pairs={{0,64},{8,72},{16,80},{24,88},{32,96},{40,104},{48,112},{56,120},{... | collective-permute-start | bytes 371720 | tf_op jit(solution)/shard_map/ppermute | solution.py:217
  26.2 6.6 %collective-permute-done.1.refs_1_ = f32[88,352]{1,0:T(8,128)S(1)} collective-permute-done((f32[88,352]{1,0:T(8,128)S(1)}, f32[88,352]{1,0:T(8,128)S(1)}, u32[]{:S(2)}, u32[]{:S(2)}) %collective-permute-start.1) | collective-permute-done | bytes 123936 | tf_op jit(solution)/shard_map/ppermute | solution.py:217
  32.8 0.9 shard_map.127.refs_1_
  33.7 2.6 collective-permute-start.2
  36.4 0.1 pad_add_fusion.refs_0_
  36.5 11.8 %collective-permute-done.2.refs_2_ = f32[88,1408]{1,0:T(8,128)S(1)} collective-permute-done((f32[88,1408]{1,0:T(8,128)S(1)}, f32[88,1408]{1,0:T(8,128)S(1)}, u32[]{:S(2)}, u32[]{:S(2)}) %collective-permute-start.2) | collective-permute-done | bytes 495648 | tf_op jit(solution)/shard_map/ppermute | solution.py:217
  48.3 4.8 %all-gather.11.cloned.1.call-done = f32[1408,768]{1,0:T(8,128)} async-done(((f32[176,768]{1,0:T(8,128)}), f32[1408,768]{1,0:T(8,128)}) %all-gather.11.cloned.1.call-update) | async-done | bytes 4325392 | tf_op jit(solution)/shard_map/all_gather | solution.py:316
  53.1 2.8 shard_map.128
  55.9 0.0 all-gather.13.cloned.1.call-update
  55.9 0.0 all-gather.15.cloned.1.call-start
  56.0 15.9 %all-gather.1 = f32[704,352]{1,0:T(8,128)} all-gather(f32[176,352]{1,0:T(8,128)S(1)} %get-tuple-element.39), channel_id=3, replica_groups={{0,8,16,24},{32,40,48,56},{64,72,80,88},{96,104,112,120},{128,136,144,1..., dimensions={0}, use_global_device_ids=true | all-gather | bytes 1239040 | tf_op jit(solution)/shard_map/all_gather | solution.py:229
  71.8 3.0 %shard_map.129 = (f32[176,88]{1,0:T(8,128)S(1)}, f32[88,176]{1,0:T(8,128)S(1)}, f32[2,176,352]{2,1,0:T(8,128)}) custom-call(s32[3]{0:T(128)S(1)} %pad_add_fusion.refs_0_, f32[4,176,352]{2,1,0:T(8,128)} %bitcast.30, f32[8,176,768]{2,1,0:T(8,128)} %bitcast.24, f32[176,352]{1,0:T(8,128)S(1)} %copy-done, f32[176,352]{1,0:T(8,128)S(1)} %copy-done.1), custom_call_target="tpu_custom_call" | custom-call | flops 65421312 | bytes 8000000 | tf_op jit(solution)/shard_map/pallas_call | solution.py:281
  74.9 4.5 %collective-permute-start.3 = (f32[1,88,176]{2,1,0:T(8,128)S(1)}, f32[1,88,176]{2,1,0:T(8,128)S(1)}, u32[]{:S(2)}, u32[]{:S(2)}) collective-permute-start(f32[1,88,176]{2,1,0:T(8,128)S(1)} %bitcast.12), channel_id=1, source_target_pairs={{0,64},{8,72},{16,80},{24,88},{32,96},{40,104},{48,112},{56,120},{... | collective-permute-start | bytes 185864 | tf_op jit(solution)/shard_map/ppermute | solution.py:217
  79.3 2.9 %collective-permute-done.3 = f32[1,88,176]{2,1,0:T(8,128)S(1)} collective-permute-done((f32[1,88,176]{2,1,0:T(8,128)S(1)}, f32[1,88,176]{2,1,0:T(8,128)S(1)}, u32[]{:S(2)}, u32[]{:S(2)}) %collective-permute-start.3) | collective-permute-done | bytes 61984 | tf_op jit(solution)/shard_map/ppermute | solution.py:217
  82.2 3.5 %collective-permute-start.4 = (f32[2,88,176]{2,1,0:T(8,128)S(1)}, f32[2,88,176]{2,1,0:T(8,128)S(1)}, u32[]{:S(2)}, u32[]{:S(2)}) collective-permute-start(f32[2,88,176]{2,1,0:T(8,128)S(1)} %pad_maximum_fusion.3), channel_id=1, source_target_pairs={{0,32},{8,40},{16,48},{24,56},{32,0},{40,8},{48,16},{56,24},{64,96... | collective-permute-start | bytes 371720 | tf_op jit(solution)/shard_map/ppermute | solution.py:217
  85.7 3.9 %collective-permute-done.4 = f32[2,88,176]{2,1,0:T(8,128)S(1)} collective-permute-done((f32[2,88,176]{2,1,0:T(8,128)S(1)}, f32[2,88,176]{2,1,0:T(8,128)S(1)}, u32[]{:S(2)}, u32[]{:S(2)}) %collective-permute-start.4) | collective-permute-done | bytes 123936 | tf_op jit(solution)/shard_map/ppermute | solution.py:217
  89.6 27.6 %all-gather.2.refs_4_ = f32[16,88,176]{2,1,0:T(8,128)} all-gather(f32[4,88,176]{2,1,0:T(8,128)S(1)} %pad_maximum_fusion), channel_id=4, replica_groups={{0,8,16,24},{32,40,48,56},{64,72,80,88},{96,104,112,120},{128,136,144,1..., dimensions={0}, use_global_device_ids=true | all-gather | bytes 1239040 | tf_op jit(solution)/shard_map/all_gather | solution.py:229
  117.2 0.4 all-gather.13.cloned.1.call-done
  117.6 8.0 %shard_map.130 = (f32[4,176,220]{2,1,0:T(8,128)S(1)}, f32[4,176,220]{2,1,0:T(8,128)S(1)}) custom-call(s32[3]{0:T(128)S(1)} %pad_add_fusion.refs_0_, f32[4,176,352]{2,1,0:T(8,128)} %bitcast.31, f32[44,176]{1,0:T(8,128)S(1)} %bitcast.20, f32[176,88]{1,0:T(8,128)S(1)} %get-tuple-element.40.refs_3_, f32[16,88,176]{2,1,0:T(8,128)} %all-gather.2.refs_4_, ...), custom_call_target="tpu_custom_call" | custom-call | flops 261685248 | bytes 8000000 | tf_op jit(solution)/shard_map/pallas_call | solution.py:281
  125.6 1.9 collective-permute-start.5
  127.5 2.2 collective-permute-done.5.refs_1_
  129.7 0.9 copy-done.7
  130.5 1.2 shard_map.131
  131.7 2.4 collective-permute-start.6
  134.1 3.4 %collective-permute-start.7 = (f32[176,220]{1,0:T(8,128)S(1)}, f32[176,220]{1,0:T(8,128)S(1)}, u32[]{:S(2)}, u32[]{:S(2)}) collective-permute-start(f32[176,220]{1,0:T(8,128)S(1)} %get-tuple-element.47), channel_id=1, source_target_pairs={{0,6},{1,7},{2,0},{3,1},{4,2},{5,3},{6,4},{7,5},{8,14},{9,15},{10,... | collective-permute-start | bytes 464648 | tf_op jit(solution)/shard_map/ppermute | solution.py:226
  137.6 3.1 %collective-permute-start.8 = (f32[176,220]{1,0:T(8,128)S(1)}, f32[176,220]{1,0:T(8,128)S(1)}, u32[]{:S(2)}, u32[]{:S(2)}) collective-permute-start(f32[176,220]{1,0:T(8,128)S(1)} %get-tuple-element.48), channel_id=1, source_target_pairs={{0,4},{1,5},{2,6},{3,7},{4,0},{5,1},{6,2},{7,3},{8,12},{9,13},{10,... | collective-permute-start | bytes 464648 | tf_op jit(solution)/shard_map/ppermute | solution.py:226
  140.7 6.7 %collective-permute-done.7.refs_2_ = f32[176,220]{1,0:T(8,128)S(1)} collective-permute-done((f32[176,220]{1,0:T(8,128)S(1)}, f32[176,220]{1,0:T(8,128)S(1)}, u32[]{:S(2)}, u32[]{:S(2)}) %collective-permute-start.7) | collective-permute-done | bytes 154912 | tf_op jit(solution)/shard_map/ppermute | solution.py:226
  147.4 0.8 shard_map.132
  148.3 5.4 %collective-permute-start.9 = (f32[1,88,176]{2,1,0:T(8,128)S(1)}, f32[1,88,176]{2,1,0:T(8,128)S(1)}, u32[]{:S(2)}, u32[]{:S(2)}) collective-permute-start(f32[1,88,176]{2,1,0:T(8,128)S(1)} %bitcast.15), channel_id=1, source_target_pairs={{0,64},{8,72},{16,80},{24,88},{32,96},{40,104},{48,112},{56,120},{... | collective-permute-start | bytes 185864 | tf_op jit(solution)/shard_map/ppermute | solution.py:217
  153.7 2.5 collective-permute-done.9
  156.3 3.8 %collective-permute-start.10 = (f32[2,88,176]{2,1,0:T(8,128)S(1)}, f32[2,88,176]{2,1,0:T(8,128)S(1)}, u32[]{:S(2)}, u32[]{:S(2)}) collective-permute-start(f32[2,88,176]{2,1,0:T(8,128)S(1)} %pad_maximum_fusion.4), channel_id=1, source_target_pairs={{0,32},{8,40},{16,48},{24,56},{32,0},{40,8},{48,16},{56,24},{64,96... | collective-permute-start | bytes 371720 | tf_op jit(solution)/shard_map/ppermute | solution.py:217
  160.1 3.6 %collective-permute-done.10 = f32[2,88,176]{2,1,0:T(8,128)S(1)} collective-permute-done((f32[2,88,176]{2,1,0:T(8,128)S(1)}, f32[2,88,176]{2,1,0:T(8,128)S(1)}, u32[]{:S(2)}, u32[]{:S(2)}) %collective-permute-start.10) | collective-permute-done | bytes 123936 | tf_op jit(solution)/shard_map/ppermute | solution.py:217
  163.7 15.7 %all-gather.4.refs_1_ = f32[16,88,176]{2,1,0:T(8,128)} all-gather(f32[4,88,176]{2,1,0:T(8,128)S(1)} %pad_maximum_fusion.1), channel_id=6, replica_groups={{0,8,16,24},{32,40,48,56},{64,72,80,88},{96,104,112,120},{128,136,144,1..., dimensions={0}, use_global_device_ids=true | all-gather | bytes 1239040 | tf_op jit(solution)/shard_map/all_gather | solution.py:229
  179.4 7.6 %shard_map.133 = (f32[176,176]{1,0:T(8,128)}, f32[4,176,176]{2,1,0:T(8,128)S(1)}, f32[4,176,176]{2,1,0:T(8,128)S(1)}) custom-call(s32[3]{0:T(128)S(1)} %pad_add_fusion.refs_0_, f32[16,88,176]{2,1,0:T(8,128)} %all-gather.4.refs_1_, f32[8,176,768]{2,1,0:T(8,128)} %bitcast.25, f32[4,3,176,352]{3,2,1,0:T(8,128)} %bitcast.28, f32[4,3,176,352]{3,2,1,0:T(8,128)} %bitcast.29, ...), custom_call_target="tpu_custom_call" | custom-call | flops 523370496 | bytes 8000000 | tf_op jit(solution)/shard_map/pallas_call | solution.py:281
  187.0 1.9 collective-permute-start.11
  188.9 2.2 collective-permute-done.11.refs_1_
  191.1 0.9 copy-done.8
  191.9 1.2 shard_map.134
  193.1 3.6 %collective-permute-start.12 = (f32[176,176]{1,0:T(8,128)S(1)}, f32[176,176]{1,0:T(8,128)S(1)}, u32[]{:S(2)}, u32[]{:S(2)}) collective-permute-start(f32[176,176]{1,0:T(8,128)S(1)} %get-tuple-element.57), channel_id=1, source_target_pairs={{0,2},{1,3},{2,4},{3,5},{4,6},{5,7},{6,0},{7,1},{8,10},{9,11},{10,... | collective-permute-start | bytes 371720 | tf_op jit(solution)/shard_map/ppermute | solution.py:226
  196.7 2.2 collective-permute-start.13
  199.0 5.8 %collective-permute-start.14 = (f32[176,176]{1,0:T(8,128)S(1)}, f32[176,176]{1,0:T(8,128)S(1)}, u32[]{:S(2)}, u32[]{:S(2)}) collective-permute-start(f32[176,176]{1,0:T(8,128)S(1)} %get-tuple-element.59), channel_id=1, source_target_pairs={{0,4},{1,5},{2,6},{3,7},{4,0},{5,1},{6,2},{7,3},{8,12},{9,13},{10,... | collective-permute-start | bytes 371720 | tf_op jit(solution)/shard_map/ppermute | solution.py:226
  204.8 1.4 collective-permute-done.13.refs_2_
  206.3 4.8 %collective-permute-done.14.refs_3_ = f32[176,176]{1,0:T(8,128)S(1)} collective-permute-done((f32[176,176]{1,0:T(8,128)S(1)}, f32[176,176]{1,0:T(8,128)S(1)}, u32[]{:S(2)}, u32[]{:S(2)}) %collective-permute-start.14) | collective-permute-done | bytes 123936 | tf_op jit(solution)/shard_map/ppermute | solution.py:226
  211.0 0.7 shard_map.135
  211.8 2.5 collective-permute-start.15
  214.3 4.9 %collective-permute-done.15 = f32[1,176,176]{2,1,0:T(8,128)S(1)} collective-permute-done((f32[1,176,176]{2,1,0:T(8,128)S(1)}, f32[1,176,176]{2,1,0:T(8,128)S(1)}, u32[]{:S(2)}, u32[]{:S(2)}) %collective-permute-start.15) | collective-permute-done | bytes 123936 | tf_op jit(solution)/shard_map/ppermute | solution.py:217
  219.2 16.6 %all-gather.5.refs_1_ = f32[8,176,176]{2,1,0:T(8,128)} all-gather(f32[2,176,176]{2,1,0:T(8,128)S(1)} %pad_maximum_fusion.2), channel_id=7, replica_groups={{0,8,16,24},{32,40,48,56},{64,72,80,88},{96,104,112,120},{128,136,144,1..., dimensions={0}, use_global_device_ids=true | all-gather | bytes 1239040 | tf_op jit(solution)/shard_map/all_gather | solution.py:229
  235.8 8.5 %shard_map.136 = (f32[176,352]{1,0:T(8,128)}, f32[4,176,352]{2,1,0:T(8,128)S(1)}, f32[4,176,352]{2,1,0:T(8,128)}) custom-call(s32[3]{0:T(128)S(1)} %pad_add_fusion.refs_0_, f32[8,176,176]{2,1,0:T(8,128)} %all-gather.5.refs_1_, f32[8,176,768]{2,1,0:T(8,128)} %bitcast.26, f32[4,2,176,352]{3,2,1,0:T(8,128)} %bitcast.32, f32[4,2,176,352]{3,2,1,0:T(8,128)} %bitcast.33, ...), custom_call_target="tpu_custom_call" | custom-call | flops 1046740992 | bytes 8000000 | tf_op jit(solution)/shard_map/pallas_call | solution.py:281
  244.4 1.9 collective-permute-start.16
  246.3 2.7 collective-permute-done.16.refs_1_
  249.0 1.0 copy-done.6
  250.0 1.7 shard_map.137
  251.7 3.0 %collective-permute-start.17 = (f32[176,352]{1,0:T(8,128)S(1)}, f32[176,352]{1,0:T(8,128)S(1)}, u32[]{:S(2)}, u32[]{:S(2)}) collective-permute-start(f32[176,352]{1,0:T(8,128)S(1)} %get-tuple-element.67), channel_id=1, source_target_pairs={{0,2},{1,3},{2,4},{3,5},{4,6},{5,7},{6,0},{7,1},{8,10},{9,11},{10,... | collective-permute-start | bytes 743432 | tf_op jit(solution)/shard_map/ppermute | solution.py:226
  254.7 2.8 %collective-permute-start.18 = (f32[176,352]{1,0:T(8,128)S(1)}, f32[176,352]{1,0:T(8,128)S(1)}, u32[]{:S(2)}, u32[]{:S(2)}) collective-permute-start(f32[176,352]{1,0:T(8,128)S(1)} %get-tuple-element.68), channel_id=1, source_target_pairs={{0,6},{1,7},{2,0},{3,1},{4,2},{5,3},{6,4},{7,5},{8,14},{9,15},{10,... | collective-permute-start | bytes 743432 | tf_op jit(solution)/shard_map/ppermute | solution.py:226
  257.5 2.7 collective-permute-start.19
  260.2 1.9 collective-permute-done.17.refs_1_
  262.1 9.8 %collective-permute-done.18.refs_2_ = f32[176,352]{1,0:T(8,128)S(1)} collective-permute-done((f32[176,352]{1,0:T(8,128)S(1)}, f32[176,352]{1,0:T(8,128)S(1)}, u32[]{:S(2)}, u32[]{:S(2)}) %collective-permute-start.18) | collective-permute-done | bytes 247840 | tf_op jit(solution)/shard_map/ppermute | solution.py:226
  271.8 0.9 shard_map.138
  (27 shorter events, 0.2 us)
Async XLA Ops:
  7.2 25.7 %copy-start.2 = (f32[176,176]{1,0:T(8,128)S(1)}, f32[176,176]{1,0:T(8,128)}, u32[]{:S(2)}) copy-start(f32[176,176]{1,0:T(8,128)} %refs_2_.1) | copy-start | bytes 371716
  7.2 2.2 copy-start.5
  7.2 13.4 %copy-start.4 = (f32[176,88]{1,0:T(8,128)S(1)}, f32[176,88]{1,0:T(8,128)}, u32[]{:S(2)}) copy-start(f32[176,88]{1,0:T(8,128)} %refs_6_.1) | copy-start | bytes 185860
  7.2 25.6 %copy-start.3 = (f32[176,176]{1,0:T(8,128)S(1)}, f32[176,176]{1,0:T(8,128)}, u32[]{:S(2)}) copy-start(f32[176,176]{1,0:T(8,128)} %refs_5_.2) | copy-start | bytes 371716
  7.2 45.9 %all-gather.11.cloned.1.call-start = ((), (), s32[]{:S(2)}) async-start(), calls=%async_computation | async-start | bytes 4866048 | tf_op jit(solution)/shard_map/all_gather | solution.py:316
  9.3 108.3 %all-gather.13.cloned.1.call-start = ((), (), s32[]{:S(2)}) async-start(), calls=%async_computation.1 | async-start | bytes 4055040 | tf_op jit(solution)/shard_map/all_gather | solution.py:229
  9.4 11.2 %collective-permute-start = (f32[44,176]{1,0:T(8,128)S(1)}, f32[44,176]{1,0:T(8,128)S(1)}, u32[]{:S(2)}, u32[]{:S(2)}) collective-permute-start(f32[44,176]{1,0:T(8,128)S(1)} %bitcast.18), channel_id=1, source_target_pairs={{0,128},{8,136},{16,144},{24,152},{32,160},{40,168},{48,176},{56,1... | collective-permute-start | bytes 92936 | tf_op jit(solution)/shard_map/ppermute | solution.py:217
  20.9 11.9 %collective-permute-start.1 = (f32[88,352]{1,0:T(8,128)S(1)}, f32[88,352]{1,0:T(8,128)S(1)}, u32[]{:S(2)}, u32[]{:S(2)}) collective-permute-start(f32[88,352]{1,0:T(8,128)S(1)} %shard_map.126.refs_0_), channel_id=1, source_target_pairs={{0,64},{8,72},{16,80},{24,88},{32,96},{40,104},{48,112},{56,120},{... | collective-permute-start | bytes 371720 | tf_op jit(solution)/shard_map/ppermute | solution.py:217
  33.7 14.6 %collective-permute-start.2 = (f32[88,1408]{1,0:T(8,128)S(1)}, f32[88,1408]{1,0:T(8,128)S(1)}, u32[]{:S(2)}, u32[]{:S(2)}) collective-permute-start(f32[88,1408]{1,0:T(8,128)S(1)} %shard_map.127.refs_1_), channel_id=1, source_target_pairs={{0,32},{8,40},{16,48},{24,56},{32,0},{40,8},{48,16},{56,24},{64,96... | collective-permute-start | bytes 1486856 | tf_op jit(solution)/shard_map/ppermute | solution.py:217
  55.9 16.0 %copy-start = (f32[176,352]{1,0:T(8,128)S(1)}, f32[176,352]{1,0:T(8,128)}, u32[]{:S(2)}) copy-start(f32[176,352]{1,0:T(8,128)} %refs_3_.3) | copy-start | bytes 743428
  55.9 15.9 %copy-start.1 = (f32[176,352]{1,0:T(8,128)S(1)}, f32[176,352]{1,0:T(8,128)}, u32[]{:S(2)}) copy-start(f32[176,352]{1,0:T(8,128)} %refs_5_.3) | copy-start | bytes 743428
  55.9 179.9 %all-gather.15.cloned.1.call-start = ((), (), s32[]{:S(2)}) async-start(), calls=%async_computation.2 | async-start | bytes 2703360 | tf_op jit(solution)/shard_map/all_gather | solution.py:229
  74.9 7.3 %collective-permute-start.3 = (f32[1,88,176]{2,1,0:T(8,128)S(1)}, f32[1,88,176]{2,1,0:T(8,128)S(1)}, u32[]{:S(2)}, u32[]{:S(2)}) collective-permute-start(f32[1,88,176]{2,1,0:T(8,128)S(1)} %bitcast.12), channel_id=1, source_target_pairs={{0,64},{8,72},{16,80},{24,88},{32,96},{40,104},{48,112},{56,120},{... | collective-permute-start | bytes 185864 | tf_op jit(solution)/shard_map/ppermute | solution.py:217
  82.2 7.4 %collective-permute-start.4 = (f32[2,88,176]{2,1,0:T(8,128)S(1)}, f32[2,88,176]{2,1,0:T(8,128)S(1)}, u32[]{:S(2)}, u32[]{:S(2)}) collective-permute-start(f32[2,88,176]{2,1,0:T(8,128)S(1)} %pad_maximum_fusion.3), channel_id=1, source_target_pairs={{0,32},{8,40},{16,48},{24,56},{32,0},{40,8},{48,16},{56,24},{64,96... | collective-permute-start | bytes 371720 | tf_op jit(solution)/shard_map/ppermute | solution.py:217
  125.6 4.1 %collective-permute-start.5 = (f32[4,176,220]{2,1,0:T(8,128)S(1)}, f32[4,176,220]{2,1,0:T(8,128)S(1)}, u32[]{:S(2)}, u32[]{:S(2)}) collective-permute-start(f32[4,176,220]{2,1,0:T(8,128)S(1)} %get-tuple-element.44), channel_id=1, source_target_pairs={{0,1},{1,0},{2,3},{3,2},{4,5},{5,4},{6,7},{7,6},{8,9},{9,8},{10,11... | collective-permute-start | bytes 1858568 | tf_op jit(solution)/shard_map/ppermute | solution.py:220
  129.7 0.9 copy-start.7
  131.7 9.0 %collective-permute-start.6 = (f32[176,220]{1,0:T(8,128)S(1)}, f32[176,220]{1,0:T(8,128)S(1)}, u32[]{:S(2)}, u32[]{:S(2)}) collective-permute-start(f32[176,220]{1,0:T(8,128)S(1)} %get-tuple-element.46), channel_id=1, source_target_pairs={{0,2},{1,3},{2,4},{3,5},{4,6},{5,7},{6,0},{7,1},{8,10},{9,11},{10,... | collective-permute-start | bytes 464648 | tf_op jit(solution)/shard_map/ppermute | solution.py:226
  134.1 13.3 %collective-permute-start.7 = (f32[176,220]{1,0:T(8,128)S(1)}, f32[176,220]{1,0:T(8,128)S(1)}, u32[]{:S(2)}, u32[]{:S(2)}) collective-permute-start(f32[176,220]{1,0:T(8,128)S(1)} %get-tuple-element.47), channel_id=1, source_target_pairs={{0,6},{1,7},{2,0},{3,1},{4,2},{5,3},{6,4},{7,5},{8,14},{9,15},{10,... | collective-permute-start | bytes 464648 | tf_op jit(solution)/shard_map/ppermute | solution.py:226
  137.6 9.8 %collective-permute-start.8 = (f32[176,220]{1,0:T(8,128)S(1)}, f32[176,220]{1,0:T(8,128)S(1)}, u32[]{:S(2)}, u32[]{:S(2)}) collective-permute-start(f32[176,220]{1,0:T(8,128)S(1)} %get-tuple-element.48), channel_id=1, source_target_pairs={{0,4},{1,5},{2,6},{3,7},{4,0},{5,1},{6,2},{7,3},{8,12},{9,13},{10,... | collective-permute-start | bytes 464648 | tf_op jit(solution)/shard_map/ppermute | solution.py:226
  148.3 8.0 %collective-permute-start.9 = (f32[1,88,176]{2,1,0:T(8,128)S(1)}, f32[1,88,176]{2,1,0:T(8,128)S(1)}, u32[]{:S(2)}, u32[]{:S(2)}) collective-permute-start(f32[1,88,176]{2,1,0:T(8,128)S(1)} %bitcast.15), channel_id=1, source_target_pairs={{0,64},{8,72},{16,80},{24,88},{32,96},{40,104},{48,112},{56,120},{... | collective-permute-start | bytes 185864 | tf_op jit(solution)/shard_map/ppermute | solution.py:217
  156.3 7.4 %collective-permute-start.10 = (f32[2,88,176]{2,1,0:T(8,128)S(1)}, f32[2,88,176]{2,1,0:T(8,128)S(1)}, u32[]{:S(2)}, u32[]{:S(2)}) collective-permute-start(f32[2,88,176]{2,1,0:T(8,128)S(1)} %pad_maximum_fusion.4), channel_id=1, source_target_pairs={{0,32},{8,40},{16,48},{24,56},{32,0},{40,8},{48,16},{56,24},{64,96... | collective-permute-start | bytes 371720 | tf_op jit(solution)/shard_map/ppermute | solution.py:217
  187.0 4.1 %collective-permute-start.11 = (f32[4,176,176]{2,1,0:T(8,128)S(1)}, f32[4,176,176]{2,1,0:T(8,128)S(1)}, u32[]{:S(2)}, u32[]{:S(2)}) collective-permute-start(f32[4,176,176]{2,1,0:T(8,128)S(1)} %get-tuple-element.55), channel_id=1, source_target_pairs={{0,1},{1,0},{2,3},{3,2},{4,5},{5,4},{6,7},{7,6},{8,9},{9,8},{10,11... | collective-permute-start | bytes 1486856 | tf_op jit(solution)/shard_map/ppermute | solution.py:220
  191.1 0.9 copy-start.8
  193.1 11.7 %collective-permute-start.12 = (f32[176,176]{1,0:T(8,128)S(1)}, f32[176,176]{1,0:T(8,128)S(1)}, u32[]{:S(2)}, u32[]{:S(2)}) collective-permute-start(f32[176,176]{1,0:T(8,128)S(1)} %get-tuple-element.57), channel_id=1, source_target_pairs={{0,2},{1,3},{2,4},{3,5},{4,6},{5,7},{6,0},{7,1},{8,10},{9,11},{10,... | collective-permute-start | bytes 371720 | tf_op jit(solution)/shard_map/ppermute | solution.py:226
  196.7 9.5 %collective-permute-start.13 = (f32[176,176]{1,0:T(8,128)S(1)}, f32[176,176]{1,0:T(8,128)S(1)}, u32[]{:S(2)}, u32[]{:S(2)}) collective-permute-start(f32[176,176]{1,0:T(8,128)S(1)} %get-tuple-element.58), channel_id=1, source_target_pairs={{0,6},{1,7},{2,0},{3,1},{4,2},{5,3},{6,4},{7,5},{8,14},{9,15},{10,... | collective-permute-start | bytes 371720 | tf_op jit(solution)/shard_map/ppermute | solution.py:226
  199.0 12.0 %collective-permute-start.14 = (f32[176,176]{1,0:T(8,128)S(1)}, f32[176,176]{1,0:T(8,128)S(1)}, u32[]{:S(2)}, u32[]{:S(2)}) collective-permute-start(f32[176,176]{1,0:T(8,128)S(1)} %get-tuple-element.59), channel_id=1, source_target_pairs={{0,4},{1,5},{2,6},{3,7},{4,0},{5,1},{6,2},{7,3},{8,12},{9,13},{10,... | collective-permute-start | bytes 371720 | tf_op jit(solution)/shard_map/ppermute | solution.py:226
  211.8 7.4 %collective-permute-start.15 = (f32[1,176,176]{2,1,0:T(8,128)S(1)}, f32[1,176,176]{2,1,0:T(8,128)S(1)}, u32[]{:S(2)}, u32[]{:S(2)}) collective-permute-start(f32[1,176,176]{2,1,0:T(8,128)S(1)} %bitcast.21), channel_id=1, source_target_pairs={{0,32},{8,40},{16,48},{24,56},{32,0},{40,8},{48,16},{56,24},{64,96... | collective-permute-start | bytes 371720 | tf_op jit(solution)/shard_map/ppermute | solution.py:217
  244.4 4.6 %collective-permute-start.16 = (f32[4,176,352]{2,1,0:T(8,128)S(1)}, f32[4,176,352]{2,1,0:T(8,128)S(1)}, u32[]{:S(2)}, u32[]{:S(2)}) collective-permute-start(f32[4,176,352]{2,1,0:T(8,128)S(1)} %get-tuple-element.65), channel_id=1, source_target_pairs={{0,1},{1,0},{2,3},{3,2},{4,5},{5,4},{6,7},{7,6},{8,9},{9,8},{10,11... | collective-permute-start | bytes 2973704 | tf_op jit(solution)/shard_map/ppermute | solution.py:220
  249.0 1.0 copy-start.6
  251.7 10.4 %collective-permute-start.17 = (f32[176,352]{1,0:T(8,128)S(1)}, f32[176,352]{1,0:T(8,128)S(1)}, u32[]{:S(2)}, u32[]{:S(2)}) collective-permute-start(f32[176,352]{1,0:T(8,128)S(1)} %get-tuple-element.67), channel_id=1, source_target_pairs={{0,2},{1,3},{2,4},{3,5},{4,6},{5,7},{6,0},{7,1},{8,10},{9,11},{10,... | collective-permute-start | bytes 743432 | tf_op jit(solution)/shard_map/ppermute | solution.py:226
  254.7 17.1 %collective-permute-start.18 = (f32[176,352]{1,0:T(8,128)S(1)}, f32[176,352]{1,0:T(8,128)S(1)}, u32[]{:S(2)}, u32[]{:S(2)}) collective-permute-start(f32[176,352]{1,0:T(8,128)S(1)} %get-tuple-element.68), channel_id=1, source_target_pairs={{0,6},{1,7},{2,0},{3,1},{4,2},{5,3},{6,4},{7,5},{8,14},{9,15},{10,... | collective-permute-start | bytes 743432 | tf_op jit(solution)/shard_map/ppermute | solution.py:226
  257.5 14.3 %collective-permute-start.19 = (f32[176,352]{1,0:T(8,128)S(1)}, f32[176,352]{1,0:T(8,128)S(1)}, u32[]{:S(2)}, u32[]{:S(2)}) collective-permute-start(f32[176,352]{1,0:T(8,128)S(1)} %get-tuple-element.69), channel_id=1, source_target_pairs={{0,4},{1,5},{2,6},{3,7},{4,0},{5,1},{6,2},{7,3},{8,12},{9,13},{10,... | collective-permute-start | bytes 743432 | tf_op jit(solution)/shard_map/ppermute | solution.py:226
Sparse Core Ops, SparseCore 0:
  10.2 42.8 all-gather.10
  56.0 61.5 all-gather.12
  119.7 38.9 all-gather.14

commit v4 on v3

v4 whole, which is shorter than its diff:
```python
import functools

import jax
import jax.numpy as jnp
from jax import lax
from jax.experimental import pallas as pl
from jax.experimental.pallas import tpu as pltpu
from jax.sharding import PartitionSpec as P

Y = 4
XS = 4
CORES = 2
VMEM_BYTES = 52 * 1024 * 1024


class Staged:

    def __init__(self, source, index, scratch, semaphore):
        self.copy = pltpu.make_async_copy(source.at[index], scratch, semaphore)
        self.scratch, self.waited = scratch, False
        self.copy.start()

    def ready(self):
        if not self.waited:
            self.copy.wait()
            self.waited = True
        return self.scratch


def split(value):
    high = value.astype(jnp.bfloat16)
    low = (value - high.astype(jnp.float32)).astype(jnp.bfloat16)
    return high, low


def product(first, second):
    (fh, fl), (sh, sl) = first, second
    run = functools.partial(jnp.dot, preferred_element_type=jnp.float32)
    return run(fh, sh) + (run(fh, sl) + run(fl, sh))


def block_of(ref, index):
    return ref[:, index * 176 : (index + 1) * 176]


def turn(f2, own, got_ref, out_ref):
    top = jnp.concatenate([own.ready()[...], got_ref[...]], 0)
    out_ref[...] = jnp.concatenate([f2.ready()[...].T, top], 1)


def pack(two_ref, got_ref, f3, out_ref):
    turned = f3.ready()[...].T
    parts = [two_ref[...], got_ref[...], turned[:88], turned[88:]]
    out_ref[...] = jnp.concatenate(parts, 1)


def join(where_ref, own_ref, got_ref, panels_ref, f1_ref, rows_ref):
    del panels_ref
    z = where_ref[2]

    def at(which, distance):
        far = ((distance >> 1) & 1) == 1
        own = jnp.where(far, block_of(own_ref, which + 2), block_of(own_ref, which))
        got = jnp.where(far, block_of(got_ref, which + 2), block_of(got_ref, which))
        return jnp.where((distance & 1) == 1, got, own)

    pieces = []
    for plane in range(8):
        distance = plane ^ z
        both = at(1, distance)
        pieces.append(jnp.where((distance >> 2) == 1, both[44:], both[:44]))
    f1_ref[...] = jnp.concatenate(pieces, 0).T
    pieces = [at(0, plane ^ (z % 4)) for plane in range(4)]
    rows_ref[0] = jnp.concatenate(pieces, 0).T
    pieces = []
    for plane in range(2):
        near = plane == (z % 2)
        for index in (4, 5):
            pieces.append(
                jnp.where(near, block_of(own_ref, index), block_of(got_ref, index))
            )
    rows_ref[1] = jnp.concatenate(pieces, 0).T


def sums(planes, turned, factors):
    for y in range(Y):
        total = None
        for tile, factor in zip(turned, factors):
            term = product(split(tile(y)), factor)
            total = term if total is None else total + term
        width = total.shape[0] // planes
        step = min(width, 176)
        for plane in range(planes):
            for part in range(0, width, step):
                column = (plane * Y + y) * width + part
                value = total[plane * width + part : plane * width + part + step]
                yield column // 176, slice(column % 176, column % 176 + step), value


def share_terms(where_ref, planes, turned, factors, other_ref, mine_ref):
    x, core = where_ref[0], where_ref[1]
    for block, rows, value in sums(planes, turned, factors):
        at = (block // CORES - x) % XS
        same = core == (block % CORES)

        @pl.when(same)
        def _():
            mine_ref[at, rows, :] = value

        @pl.when(jnp.logical_not(same))
        def _():
            other_ref[at, rows, :] = value


def times_columns(planes, distances, left, columns_ref, count):
    total = None
    for y in range(Y):
        if planes == 4:
            parts = [
                columns_ref[p, y * 44 : (y + 1) * 44, :count] for p in range(8)
            ]
        elif planes == 2:
            low = (y % 2) * 88
            parts = []
            for q in range(4):
                p = distances ^ ((q & 1) * 2 + (q >> 1)) if distances is not None else q
                parts.append(columns_ref[p * 2 + y // 2, low : low + 88, :count])
        else:
            parts = [columns_ref[(distances ^ q) * Y + y, :, :count] for q in range(2)]
        term = product(split(left(y)), split(jnp.concatenate(parts, 0)))
        total = term if total is None else total + term
    return total


def copied(pairs, sems):
    copies = [
        pltpu.make_async_copy(source, target, sems.at[index])
        for index, (source, target) in enumerate(pairs)
    ]
    for copy in copies:
        copy.start()
    return copies


def top_product(rows, columns, p4_ref, f4_ref, out_ref, turned_ref, last_ref, sems):
    copies = copied([(p4_ref, last_ref.at[0]), (f4_ref, last_ref.at[1])], sems)
    left = rows.ready()
    total = times_columns(4, None, lambda y: left[y], columns.ready(), out_ref.shape[1])
    out_ref[...] = total
    turned_ref[...] = total.T
    for copy in copies:
        copy.wait()


def next_products(where_ref, a_rows, f2_rows, columns, p4_ref, *refs):
    b_ref, g_ref, turned_ref, last_ref, sems = refs
    copies = copied([(p4_ref, last_ref)], sems)
    count, z = b_ref.shape[1], where_ref[2]
    a, f2, right = a_rows.ready(), f2_rows.ready(), columns.ready()
    b = times_columns(2, None, lambda y: f2[y], right, count)
    g = times_columns(
        2, z % 4, lambda y: a[4 * y : 4 * y + 4].reshape(352, 176).T, right, count
    )
    b_ref[...], g_ref[...] = b, g
    turned_ref[0], turned_ref[1] = b.T, g.T
    for copy in copies:
        copy.wait()


def pieces_of(ref, y, planes, z):
    pieces = []
    for plane in range(planes):
        distance = plane ^ (z % planes)
        at = distance if planes == 2 else (distance >> 1) + (distance & 1) * 2
        pieces.append(ref[y * planes + at])
    return jnp.concatenate(pieces, 0)


def third_terms(where_ref, b_ref, g_ref, b_rows, g_rows, f3_rows, f3, other_ref, mine_ref):
    z = where_ref[2]
    turned = [
        lambda y: pieces_of(b_rows.ready(), y, 2, z),
        lambda y: pieces_of(g_rows.ready(), y, 2, z),
        lambda y: f3_rows.ready()[y].T,
    ]
    factors = [split(b_ref[...]), split(g_ref[...]), split(f3.ready()[...])]
    share_terms(where_ref, 2, turned, factors, other_ref, mine_ref)


def early_terms(where_ref, f1_rows, f1, a, a_rows, f2_rows, f2, b, g, arrived_ref, out_ref):
    del arrived_ref
    z, inner = where_ref[2], a.ready()[...]
    factors = [split(jnp.concatenate([f1.ready()[...].T, -inner], 1))]
    first = factors[0][0].shape[1]
    for block, rows, value in sums(8, [lambda y: f1_rows.ready()[y].T], factors):
        out_ref[block, rows, :first] = value
    turned = [
        lambda y: pieces_of(a_rows.ready(), y, 4, z),
        lambda y: f2_rows.ready()[y].T,
    ]
    factors = [
        split(jnp.concatenate([inner, -g.ready()[...]], 1)),
        split(jnp.concatenate([f2.ready()[...], -b.ready()[...]], 1)),
    ]
    for block, rows, value in sums(4, turned, factors):
        out_ref[block, rows, first:] = value


def last_terms(where_ref, parent, columns, p_rows, f_rows, own, *refs):
    cross_ref, other_ref, mine_ref = refs
    count = cross_ref.shape[1]

    def left(y):
        return parent.ready()[2 * y : 2 * y + 2].reshape(352, 176).T

    total = times_columns(1, where_ref[2] % 2, left, columns.ready(), count)
    cross_ref[...] = -total
    turned = [lambda y: p_rows.ready()[y].T, lambda y: f_rows.ready()[y].T]
    factors = [split(total), split(own.ready()[...])]
    share_terms(where_ref, 1, turned, factors, other_ref, mine_ref)


def add_pieces(mine, got_ref, *out_refs):
    mine_ref = mine.ready()
    for step, out_ref in enumerate(out_refs):
        out_ref[...] = mine_ref[step] + got_ref[step]


def finish(*refs):
    *in_refs, out_ref, turned_ref = refs
    total = sum(ref[...] for ref in in_refs)
    out_ref[...] = total
    turned_ref[...] = total.T


def local(top_factor, panel_two, panel_three, panel_four, factor_two, factor_three, factor_four):
    leaves = lax.axis_size("leaf")
    fronts = lax.axis_size("front")
    share = top_factor.shape[0]
    width = panel_four.shape[1]
    leaf = lax.axis_index("leaf")
    front = lax.axis_index("front")
    z, x, core = leaf // Y, front // CORES, front % CORES
    where = jnp.stack([x, core, z % 8]).astype(jnp.int32)
    y_groups = [list(range(i, i + Y)) for i in range(0, leaves, Y)]

    def from_plane(value, distance):
        pairs = [(i, ((i // Y) ^ distance) * Y + i % Y) for i in range(leaves)]
        return lax.ppermute(value, "leaf", pairs)

    def from_core(value):
        return lax.ppermute(value, "front", [(i, i ^ 1) for i in range(fronts)])

    def shift_x(value, distance):
        pairs = [
            (i, (i // CORES + distance) % XS * CORES + i % CORES) for i in range(fronts)
        ]
        return lax.ppermute(value, "front", pairs)

    def y_gather(value):
        return lax.all_gather(value, "leaf", axis=0, axis_index_groups=y_groups)

    stack = functools.partial(jax.ShapeDtypeStruct, dtype=jnp.float32)
    tile, tiles = stack((share, width)), stack((XS, share, width))
    def near_by(value):
        return ("near", value)

    def in_hbm(value):
        return ("hbm", value)

    def staged(value, *index):
        index = index or (slice(None),) * value.ndim
        part = jax.eval_shape(lambda v: v[index], value)
        return ("staged", value, index, part)

    def call(kernel, out_shape, flops, *inputs, hbm_outs=(), semaphores=0):
        specs, arrays, scratch = [], [], []
        for kind, value, *rest in inputs:
            arrays.append(value)
            if kind == "near":
                specs.append(pl.BlockSpec(value.shape, lambda i, n=value.ndim: (0,) * n))
            elif kind == "smem":
                specs.append(pl.BlockSpec(memory_space=pltpu.SMEM))
            else:
                specs.append(pl.BlockSpec(memory_space=pltpu.HBM))
            if kind == "staged":
                scratch.append(pltpu.VMEM(rest[1].shape, rest[1].dtype))
        count = len(scratch)
        scratch.append(pltpu.SemaphoreType.DMA((count + 1,)))
        if semaphores:
            scratch.append(pltpu.SemaphoreType.DMA((semaphores,)))

        def body(*refs):
            ins, rest = list(refs[: len(inputs)]), refs[len(inputs) :]
            outs, rest = rest[: len(out_shape)], rest[len(out_shape) :]
            parts, sems, more = rest[:count], rest[count], rest[count + 1 :]
            at = 0
            for index, (kind, *entry) in enumerate(inputs):
                if kind == "staged":
                    ins[index] = Staged(ins[index], entry[1], parts[at], sems.at[at])
                    at += 1
            kernel(*ins, *outs, *more)
            for value in ins:
                if isinstance(value, Staged):
                    value.ready()

        out_specs = [
            pl.BlockSpec(memory_space=pltpu.HBM)
            if index in hbm_outs
            else pl.BlockSpec(o.shape, lambda i, n=len(o.shape): (0,) * n)
            for index, o in enumerate(out_shape)
        ]
        return pl.pallas_call(
            body,
            out_shape=out_shape,
            grid=(1,),
            in_specs=specs,
            out_specs=out_specs,
            scratch_shapes=scratch,
            compiler_params=pltpu.CompilerParams(vmem_limit_bytes=VMEM_BYTES),
            cost_estimate=pl.CostEstimate(
                flops=flops, bytes_accessed=8_000_000, transcendentals=0
            ),
        )(*arrays)

    def front_total(other, mine):
        got = from_core(other)
        piece = stack(mine.shape[1:])
        pieces = call(add_pieces, [piece] * XS, 1_000_000, staged(mine), near_by(got))
        parts = [pieces[0]] + [shift_x(pieces[d], d) for d in (1, 3, 2)]
        outs = [piece, stack(piece.shape[::-1])]
        outs = call(finish, outs, 1_000_000, *[near_by(part) for part in parts])
        return *outs, parts[1]

    def plane_gather(parts):
        gathered = y_gather(jnp.stack(parts))
        return gathered.reshape(-1, *gathered.shape[2:])

    def padded(value):
        return jnp.pad(value, ((0, 0), (0, -value.shape[1] % 128)))

    panels = jnp.concatenate([padded(panel_three), padded(panel_two)], 1)
    panels = lax.all_gather(panels, "front", axis=0)
    lanes = slice(None), slice(None)
    where = ("smem", where)

    half = share // 2
    first = top_factor.T
    (two,) = call(
        turn,
        [stack((half, 2 * share))],
        1_000_000,
        staged(factor_two),
        staged(first),
        near_by(from_plane(first, 4)),
    )
    (near,) = call(
        pack,
        [stack((half, 6 * share))],
        1_000_000,
        near_by(two),
        near_by(from_plane(two, 2)),
        staged(factor_three),
    )
    f1, deep = call(
        join,
        [tile, stack((2, share, width))],
        1_000_000,
        where,
        near_by(near),
        near_by(from_plane(near, 1)),
        in_hbm(panels),
    )
    rows = y_gather(deep)
    f1_rows = y_gather(f1)

    work = 6 * share * share * XS * width
    count = panel_two.shape[1]
    inner, turned, last = call(
        top_product,
        [stack((share, count)), stack((count, share)), stack((2, share, width))],
        work // 4,
        staged(f1_rows),
        staged(panels, *lanes, slice(256, 384)),
        in_hbm(panel_four),
        in_hbm(factor_four),
        hbm_outs=(2,),
        semaphores=2,
    )
    last_rows = y_gather(last)
    a_rows = plane_gather([turned] + [from_plane(turned, d) for d in (2, 1, 3)])
    b, g, turned, p4 = call(
        next_products,
        [stack((share, share))] * 2 + [stack((2, share, share)), tile],
        work,
        where,
        staged(a_rows),
        staged(rows, slice(None), 0),
        staged(panels, *lanes, slice(0, 256)),
        in_hbm(panel_four),
        hbm_outs=(3,),
        semaphores=1,
    )
    last_panel = lax.all_gather(p4, "front", axis=0)
    got = from_plane(turned, 1)
    b_rows, g_rows = (plane_gather([turned[i], got[i]]) for i in range(2))

    half_sums = stack((XS, share, share))
    other, mine = call(
        third_terms,
        [half_sums, half_sums],
        2 * work,
        where,
        near_by(b),
        near_by(g),
        staged(b_rows),
        staged(g_rows),
        staged(rows, slice(None), 1),
        staged(factor_three),
    )
    cov_three, turned, arrived = front_total(other, mine)

    widths = [top_factor.shape[1], count, count, share]
    (early,) = call(
        early_terms,
        [stack((fronts, share, sum(widths)))],
        2 * work,
        where,
        staged(f1_rows),
        staged(first),
        staged(inner),
        staged(a_rows),
        staged(rows, slice(None), 0),
        staged(factor_two),
        staged(b),
        staged(g),
        near_by(arrived),
    )
    early = early.reshape(fronts * share, -1)
    early = lax.psum_scatter(early, "front", scatter_dimension=0, tiled=True)
    at = [sum(widths[:i]) for i in range(len(widths))]
    cov_one, cross_two, cov_two, cross_three = (
        early[:, i : i + w] for i, w in zip(at, widths)
    )

    parent_rows = plane_gather([turned, from_plane(turned, 1)])
    cross_four, other, mine = call(
        last_terms,
        [tile, tiles, tiles],
        4 * work,
        where,
        staged(parent_rows),
        staged(last_panel),
        staged(last_rows, slice(None), 0),
        staged(last_rows, slice(None), 1),
        staged(factor_four),
    )
    cov_four, *_ = front_total(other, mine)
    return cov_one, cross_two, cov_two, cross_three, cov_three, cross_four, cov_four


def solution(mesh):
    spec = P("front", "leaf")
    return jax.shard_map(
        local, mesh=mesh, in_specs=(spec,) * 7, out_specs=(spec,) * 7, check_vma=False
    )
```

time: 280 us -> 283 us (1.011)
  blocking collectives: 75.8 us -> 97.5 us
  starting transfers between devices: 71.8 us -> 57.4 us
  waiting for transfers between devices: 74.9 us -> 63.6 us
  local copies, waits for them, and re-layouts: 2.78 us -> 9.7 us
    all_gather x4 -> x5, blocking collectives: 75.8 us -> 97.5 us  [y_gather(): return lax.all_gather(value, 'leaf', axis=0, axis_index_groups=y_groups)]
    ppermute x9 -> x6, starting transfers between devices: 29.2 us -> 19 us  [shift_x(): return lax.ppermute(value, 'front', pairs)]
    ppermute x8, waiting for transfers between devices: 38.2 us -> 33.1 us  [from_plane(): return lax.ppermute(value, 'leaf', pairs)]
    all_gather x1, waiting for transfers between devices: 4.78 us -> 0.01 us  [local(): panels = lax.all_gather(panels, 'front', axis=0)]
    slice x0 -> x5, local copies, waits for them, and re-layouts: none -> 4.46 us  [the longest x3 4.41 us: local(): early[:, i:i + w]]
    ppermute x3 -> x2, waiting for transfers between devices: 6.99 us -> 4.83 us  [from_core(): return lax.ppermute(value, 'front', [(i, i ^ 1) for i in range(fronts)])]
    ppermute x3 -> x2, starting transfers between devices: 5.76 us -> 3.97 us  [from_core(): return lax.ppermute(value, 'front', [(i, i ^ 1) for i in range(fronts)])]
    ppermute x9 -> x6, waiting for transfers between devices: 24.5 us -> 25.5 us  [shift_x(): return lax.ppermute(value, 'front', pairs)]
  transfers between devices with their start and end apart: 23 -> 21, of which waited for: 18 -> 14; matrix products, arithmetic and copies ran while one was open for 0% -> 0% of each run, Pallas kernels for 8% -> 12%
where the time goes in v4:
time: 283 us; the launch traced here: 282 us
  blocking collectives  97.5 us (34%)
  waiting for transfers between devices  63.6 us (22%)
  starting transfers between devices  57.4 us (20%)
  Pallas kernels  37.5 us (13%)
  between operations  14.2 us (5%)
  local copies, waits for them, and re-layouts  9.7 us (3%)
    all_gather x5, blocking collectives, y_gather(): return lax.all_gather(value, 'leaf', axis=0, axis_index_groups=y_groups)  97.5 us
    pallas_call x12, Pallas kernels, call(): pl.pallas_call(body, out_shape=out_shape, grid=(1,), in_specs=specs, out_...  37.5 us
    ppermute x8, starting transfers between devices, from_plane(): return lax.ppermute(value, 'leaf', pairs)  34.3 us
    ppermute x8, waiting for transfers between devices, from_plane(): return lax.ppermute(value, 'leaf', pairs)  33.1 us
    ppermute x6, waiting for transfers between devices, shift_x(): return lax.ppermute(value, 'front', pairs)  25.5 us
    ppermute x6, starting transfers between devices, shift_x(): return lax.ppermute(value, 'front', pairs)  19 us
  transfers between devices with their start and end apart: 21, of which 14 were waited for; matrix products, arithmetic and copies ran while one was open for 0% of the time, Pallas kernels for 12%

profile of v4, /device:TPU:6, one launch (start us, length us, event | category | flops | bytes accessed | tf_op | source)
XLA Modules:
  0.0 281.7 jit_solution(12630148830408900930)
XLA Ops:
  7.2 0.0 all-gather.14.cloned.1.call-start
  7.2 1.7 select_maximum_fusion
  8.9 0.0 all-gather.16.cloned.1.call-start
  9.0 9.1 %collective-permute-start = (f32[44,176]{1,0:T(8,128)}, f32[44,176]{1,0:T(8,128)S(1)}, u32[]{:S(2)}, u32[]{:S(2)}) collective-permute-start(f32[44,176]{1,0:T(8,128)} %bitcast.18), channel_id=1, source_target_pairs={{0,128},{8,136},{16,144},{24,152},{32,160},{40,168},{48,176},{56,1... | collective-permute-start | bytes 92936 | tf_op jit(solution)/shard_map/ppermute | solution.py:249
  18.1 2.3 collective-permute-done.refs_2_
  20.4 0.9 copy-done.5
  21.3 0.8 copy-done.7
  22.0 0.3 shard_map.126.refs_0_
  22.4 5.4 %collective-permute-start.1 = (f32[88,352]{1,0:T(8,128)S(1)}, f32[88,352]{1,0:T(8,128)S(1)}, u32[]{:S(2)}, u32[]{:S(2)}) collective-permute-start(f32[88,352]{1,0:T(8,128)S(1)} %shard_map.126.refs_0_), channel_id=1, source_target_pairs={{0,64},{8,72},{16,80},{24,88},{32,96},{40,104},{48,112},{56,120},{... | collective-permute-start | bytes 371720 | tf_op jit(solution)/shard_map/ppermute | solution.py:249
  27.8 6.6 %collective-permute-done.1.refs_1_ = f32[88,352]{1,0:T(8,128)S(1)} collective-permute-done((f32[88,352]{1,0:T(8,128)S(1)}, f32[88,352]{1,0:T(8,128)S(1)}, u32[]{:S(2)}, u32[]{:S(2)}) %collective-permute-start.1) | collective-permute-done | bytes 123936 | tf_op jit(solution)/shard_map/ppermute | solution.py:249
  34.5 0.9 copy-done.3
  35.4 0.4 shard_map.127.refs_1_
  35.8 2.6 collective-permute-start.2
  38.5 0.1 pad_add_fusion.refs_0_
  38.6 9.9 %collective-permute-done.2.refs_2_ = f32[88,1056]{1,0:T(8,128)S(1)} collective-permute-done((f32[88,1056]{1,0:T(8,128)S(1)}, f32[88,1056]{1,0:T(8,128)S(1)}, u32[]{:S(2)}, u32[]{:S(2)}) %collective-permute-start.2) | collective-permute-done | bytes 371744 | tf_op jit(solution)/shard_map/ppermute | solution.py:249
  48.5 2.4 shard_map.128
  50.9 0.0 all-gather.20.cloned.1.call-start
  51.0 16.2 %all-gather.1 = f32[704,352]{1,0:T(8,128)} all-gather(f32[176,352]{1,0:T(8,128)S(1)} %get-tuple-element.32), channel_id=3, replica_groups={{0,8,16,24},{32,40,48,56},{64,72,80,88},{96,104,112,120},{128,136,144,1..., dimensions={0}, use_global_device_ids=true | all-gather | bytes 1239040 | tf_op jit(solution)/shard_map/all_gather | solution.py:261
  67.1 2.6 shard_map.129
  69.7 0.0 all-gather.18.cloned.1.call-start
  69.8 5.5 %collective-permute-start.5 = (f32[88,176]{1,0:T(8,128)S(1)}, f32[88,176]{1,0:T(8,128)S(1)}, u32[]{:S(2)}, u32[]{:S(2)}) collective-permute-start(f32[88,176]{1,0:T(8,128)S(1)} %get-tuple-element.34), channel_id=1, source_target_pairs={{0,96},{8,104},{16,112},{24,120},{32,64},{40,72},{48,80},{56,88},{... | collective-permute-start | bytes 185864 | tf_op jit(solution)/shard_map/ppermute | solution.py:249
  75.3 1.9 collective-permute-start.4
  77.3 2.7 collective-permute-start.3
  79.9 2.5 collective-permute-done.4
  82.4 2.2 collective-permute-done.3
  84.6 19.2 %all-gather.2.refs_1_.refs_4_ = f32[16,88,176]{2,1,0:T(8,128)} all-gather(f32[4,88,176]{2,1,0:T(8,128)S(1)} %pad_maximum_fusion), channel_id=4, replica_groups={{0,8,16,24},{32,40,48,56},{64,72,80,88},{96,104,112,120},{128,136,144,1..., dimensions={0}, use_global_device_ids=true | all-gather | bytes 1239040 | tf_op jit(solution)/shard_map/all_gather | solution.py:261
  103.8 4.3 %shard_map.130 = (f32[176,176]{1,0:T(8,128)S(1)}, f32[176,176]{1,0:T(8,128)S(1)}, f32[2,176,176]{2,1,0:T(8,128)S(1)}, f32[176,352]{1,0:T(8,128)}) custom-call(s32[3]{0:T(128)S(1)} %pad_add_fusion.refs_0_, f32[16,88,176]{2,1,0:T(8,128)} %all-gather.2.refs_1_.refs_4_, f32[4,2,176,352]{3,2,1,0:T(8,128)} %bitcast.26, f32[8,176,384]{2,1,0:T(8,128)} %bitcast.25, ...), custom_call_target="tpu_custom_call" | custom-call | flops 261685248 | bytes 8000000 | tf_op jit(solution)/shard_map/pallas_call | solution.py:313
  108.2 0.0 reduce-scatter.2.cloned.1.call-start
  108.2 3.6 %collective-permute-start.6 = (f32[2,176,176]{2,1,0:T(8,128)S(1)}, f32[2,176,176]{2,1,0:T(8,128)S(1)}, u32[]{:S(2)}, u32[]{:S(2)}) collective-permute-start(f32[2,176,176]{2,1,0:T(8,128)S(1)} %get-tuple-element.38), channel_id=1, source_target_pairs={{0,32},{8,40},{16,48},{24,56},{32,0},{40,8},{48,16},{56,24},{64,96... | collective-permute-start | bytes 743432 | tf_op jit(solution)/shard_map/ppermute | solution.py:249
  111.8 5.7 %collective-permute-done.6 = f32[2,176,176]{2,1,0:T(8,128)S(1)} collective-permute-done((f32[2,176,176]{2,1,0:T(8,128)S(1)}, f32[2,176,176]{2,1,0:T(8,128)S(1)}, u32[]{:S(2)}, u32[]{:S(2)}) %collective-permute-start.6) | collective-permute-done | bytes 247840 | tf_op jit(solution)/shard_map/ppermute | solution.py:249
  117.6 27.2 %all-gather.4.refs_3_ = f32[8,176,176]{2,1,0:T(8,128)} all-gather(f32[2,176,176]{2,1,0:T(8,128)S(1)} %pad_maximum_fusion.1), channel_id=6, replica_groups={{0,8,16,24},{32,40,48,56},{64,72,80,88},{96,104,112,120},{128,136,144,1..., dimensions={0}, use_global_device_ids=true | all-gather | bytes 1239040 | tf_op jit(solution)/shard_map/all_gather | solution.py:261
  144.9 17.5 %all-gather.5.refs_4_ = f32[8,176,176]{2,1,0:T(8,128)} all-gather(f32[2,176,176]{2,1,0:T(8,128)S(1)} %pad_maximum_fusion.2), channel_id=7, replica_groups={{0,8,16,24},{32,40,48,56},{64,72,80,88},{96,104,112,120},{128,136,144,1..., dimensions={0}, use_global_device_ids=true | all-gather | bytes 1239040 | tf_op jit(solution)/shard_map/all_gather | solution.py:261
  162.4 6.2 %shard_map.131 = (f32[4,176,176]{2,1,0:T(8,128)S(1)}, f32[4,176,176]{2,1,0:T(8,128)S(1)}) custom-call(s32[3]{0:T(128)S(1)} %pad_add_fusion.refs_0_, f32[176,176]{1,0:T(8,128)S(1)} %get-tuple-element.36.refs_1_.refs_7_, f32[176,176]{1,0:T(8,128)S(1)} %get-tuple-element.37.refs_2_.refs_8_, f32[8,176,176]{2,1,0:T(8,128)} %all-gather.4.refs_3_, ...), custom_call_target="tpu_custom_call" | custom-call | flops 523370496 | bytes 8000000 | tf_op jit(solution)/shard_map/pallas_call | solution.py:313
  168.6 2.1 collective-permute-start.7
  170.7 2.2 collective-permute-done.7.refs_1_
  172.8 0.9 copy-done.10
  173.7 1.5 shard_map.132
  175.2 2.5 collective-permute-start.8
  177.7 8.2 %collective-permute-done.8.refs_9_.refs_1_ = f32[176,176]{1,0:T(8,128)S(1)} collective-permute-done((f32[176,176]{1,0:T(8,128)S(1)}, f32[176,176]{1,0:T(8,128)S(1)}, u32[]{:S(2)}, u32[]{:S(2)}) %collective-permute-start.8) | collective-permute-done | bytes 123936 | tf_op jit(solution)/shard_map/ppermute | solution.py:258
  185.9 7.0 %shard_map.133 = f32[8,176,396]{2,1,0:T(8,128)} custom-call(s32[3]{0:T(128)S(1)} %pad_add_fusion.refs_0_, f32[4,176,352]{2,1,0:T(8,128)S(1)} %bitcast.17, f32[44,176]{1,0:T(8,128)S(1)} %bitcast.20, f32[176,88]{1,0:T(8,128)S(1)} %get-tuple-element.33.refs_3_, f32[16,88,176]{2,1,0:T(8,128)} %all-gather.2.refs_1_.refs_4_, f32[4,2,176,352]{3,2,1,0:T(8,128)} %bitcast.28, ...), custom_call_target="tpu_custom_call" | custom-call | flops 523370496 | bytes 8000000 | tf_op jit(solution)/shard_map/pallas_call | solution.py:313
  192.9 3.1 %collective-permute-start.9 = (f32[176,176]{1,0:T(8,128)S(1)}, f32[176,176]{1,0:T(8,128)S(1)}, u32[]{:S(2)}, u32[]{:S(2)}) collective-permute-start(f32[176,176]{1,0:T(8,128)S(1)} %get-tuple-element.43), channel_id=1, source_target_pairs={{0,6},{1,7},{2,0},{3,1},{4,2},{5,3},{6,4},{7,5},{8,14},{9,15},{10,... | collective-permute-start | bytes 371720 | tf_op jit(solution)/shard_map/ppermute | solution.py:258
  196.0 4.5 %collective-permute-start.10 = (f32[176,176]{1,0:T(8,128)S(1)}, f32[176,176]{1,0:T(8,128)S(1)}, u32[]{:S(2)}, u32[]{:S(2)}) collective-permute-start(f32[176,176]{1,0:T(8,128)S(1)} %get-tuple-element.44), channel_id=1, source_target_pairs={{0,4},{1,5},{2,6},{3,7},{4,0},{5,1},{6,2},{7,3},{8,12},{9,13},{10,... | collective-permute-start | bytes 371720 | tf_op jit(solution)/shard_map/ppermute | solution.py:258
  200.5 2.5 collective-permute-done.9.refs_2_
  203.0 3.7 %collective-permute-done.10.refs_3_ = f32[176,176]{1,0:T(8,128)S(1)} collective-permute-done((f32[176,176]{1,0:T(8,128)S(1)}, f32[176,176]{1,0:T(8,128)S(1)}, u32[]{:S(2)}, u32[]{:S(2)}) %collective-permute-start.10) | collective-permute-done | bytes 123936 | tf_op jit(solution)/shard_map/ppermute | solution.py:258
  206.7 0.7 shard_map.134
  207.5 3.4 %collective-permute-start.11 = (f32[176,176]{1,0:T(8,128)S(1)}, f32[176,176]{1,0:T(8,128)S(1)}, u32[]{:S(2)}, u32[]{:S(2)}) collective-permute-start(f32[176,176]{1,0:T(8,128)S(1)} %get-tuple-element.46), channel_id=1, source_target_pairs={{0,32},{8,40},{16,48},{24,56},{32,0},{40,8},{48,16},{56,24},{64,96... | collective-permute-start | bytes 371720 | tf_op jit(solution)/shard_map/ppermute | solution.py:249
  210.9 3.9 %collective-permute-done.11 = f32[176,176]{1,0:T(8,128)S(1)} collective-permute-done((f32[176,176]{1,0:T(8,128)S(1)}, f32[176,176]{1,0:T(8,128)S(1)}, u32[]{:S(2)}, u32[]{:S(2)}) %collective-permute-start.11) | collective-permute-done | bytes 123936 | tf_op jit(solution)/shard_map/ppermute | solution.py:249
  214.9 17.4 %all-gather.6.refs_1_ = f32[8,176,176]{2,1,0:T(8,128)} all-gather(f32[2,176,176]{2,1,0:T(8,128)S(1)} %pad_maximum_fusion.3), channel_id=8, replica_groups={{0,8,16,24},{32,40,48,56},{64,72,80,88},{96,104,112,120},{128,136,144,1..., dimensions={0}, use_global_device_ids=true | all-gather | bytes 1239040 | tf_op jit(solution)/shard_map/all_gather | solution.py:261
  232.3 8.6 %shard_map.135 = (f32[176,352]{1,0:T(8,128)}, f32[4,176,352]{2,1,0:T(8,128)S(1)}, f32[4,176,352]{2,1,0:T(8,128)}) custom-call(s32[3]{0:T(128)S(1)} %pad_add_fusion.refs_0_, f32[8,176,176]{2,1,0:T(8,128)} %all-gather.6.refs_1_, f32[8,176,352]{2,1,0:T(8,128)} %bitcast.32, f32[4,2,176,352]{3,2,1,0:T(8,128)} %bitcast.30, f32[4,2,176,352]{3,2,1,0:T(8,128)} %bitcast.31, ...), custom_call_target="tpu_custom_call" | custom-call | flops 1046740992 | bytes 8000000 | tf_op jit(solution)/shard_map/pallas_call | solution.py:313
  240.9 1.9 collective-permute-start.12
  242.8 2.7 collective-permute-done.12.refs_1_
  245.5 1.0 copy-done.9
  246.5 2.6 shard_map.136
  249.1 2.8 %collective-permute-start.13 = (f32[176,352]{1,0:T(8,128)S(1)}, f32[176,352]{1,0:T(8,128)S(1)}, u32[]{:S(2)}, u32[]{:S(2)}) collective-permute-start(f32[176,352]{1,0:T(8,128)S(1)} %get-tuple-element.53), channel_id=1, source_target_pairs={{0,2},{1,3},{2,4},{3,5},{4,6},{5,7},{6,0},{7,1},{8,10},{9,11},{10,... | collective-permute-start | bytes 743432 | tf_op jit(solution)/shard_map/ppermute | solution.py:258
  252.0 3.0 %collective-permute-start.14 = (f32[176,352]{1,0:T(8,128)S(1)}, f32[176,352]{1,0:T(8,128)S(1)}, u32[]{:S(2)}, u32[]{:S(2)}) collective-permute-start(f32[176,352]{1,0:T(8,128)S(1)} %get-tuple-element.54), channel_id=1, source_target_pairs={{0,6},{1,7},{2,0},{3,1},{4,2},{5,3},{6,4},{7,5},{8,14},{9,15},{10,... | collective-permute-start | bytes 743432 | tf_op jit(solution)/shard_map/ppermute | solution.py:258
  255.0 3.0 %collective-permute-start.15 = (f32[176,352]{1,0:T(8,128)S(1)}, f32[176,352]{1,0:T(8,128)S(1)}, u32[]{:S(2)}, u32[]{:S(2)}) collective-permute-start(f32[176,352]{1,0:T(8,128)S(1)} %get-tuple-element.55), channel_id=1, source_target_pairs={{0,4},{1,5},{2,6},{3,7},{4,0},{5,1},{6,2},{7,3},{8,12},{9,13},{10,... | collective-permute-start | bytes 743432 | tf_op jit(solution)/shard_map/ppermute | solution.py:258
  258.0 1.5 collective-permute-done.13.refs_1_
  259.5 9.6 %collective-permute-done.14.refs_2_ = f32[176,352]{1,0:T(8,128)S(1)} collective-permute-done((f32[176,352]{1,0:T(8,128)S(1)}, f32[176,352]{1,0:T(8,128)S(1)}, u32[]{:S(2)}, u32[]{:S(2)}) %collective-permute-start.14) | collective-permute-done | bytes 247840 | tf_op jit(solution)/shard_map/ppermute | solution.py:258
  269.1 0.9 shard_map.137
  270.0 0.0 reduce-scatter.2.cloned.1.call-done
  270.1 0.9 slice.34
  271.0 0.7 copy.15
  271.7 1.8 fusion
  273.5 1.7 slice.37
  (34 shorter events, 0.3 us)
Async XLA Ops:
  7.2 41.3 %all-gather.14.cloned.1.call-start = ((), (), s32[]{:S(2)}) async-start(), calls=%async_computation.2 | async-start | bytes 2433024 | tf_op jit(solution)/shard_map/all_gather | solution.py:343
  8.9 94.9 %all-gather.16.cloned.1.call-start = ((), (), s32[]{:S(2)}) async-start(), calls=%async_computation.3 | async-start | bytes 2703360 | tf_op jit(solution)/shard_map/all_gather | solution.py:261
  9.0 11.4 %collective-permute-start = (f32[44,176]{1,0:T(8,128)}, f32[44,176]{1,0:T(8,128)S(1)}, u32[]{:S(2)}, u32[]{:S(2)}) collective-permute-start(f32[44,176]{1,0:T(8,128)} %bitcast.18), channel_id=1, source_target_pairs={{0,128},{8,136},{16,144},{24,152},{32,160},{40,168},{48,176},{56,1... | collective-permute-start | bytes 92936 | tf_op jit(solution)/shard_map/ppermute | solution.py:249
  20.4 0.9 copy-start.5
  21.2 0.8 copy-start.7
  22.4 12.1 %collective-permute-start.1 = (f32[88,352]{1,0:T(8,128)S(1)}, f32[88,352]{1,0:T(8,128)S(1)}, u32[]{:S(2)}, u32[]{:S(2)}) collective-permute-start(f32[88,352]{1,0:T(8,128)S(1)} %shard_map.126.refs_0_), channel_id=1, source_target_pairs={{0,64},{8,72},{16,80},{24,88},{32,96},{40,104},{48,112},{56,120},{... | collective-permute-start | bytes 371720 | tf_op jit(solution)/shard_map/ppermute | solution.py:249
  34.4 0.9 copy-start.3
  35.8 12.7 %collective-permute-start.2 = (f32[88,1056]{1,0:T(8,128)S(1)}, f32[88,1056]{1,0:T(8,128)S(1)}, u32[]{:S(2)}, u32[]{:S(2)}) collective-permute-start(f32[88,1056]{1,0:T(8,128)S(1)} %shard_map.127.refs_1_), channel_id=1, source_target_pairs={{0,32},{8,40},{16,48},{24,56},{32,0},{40,8},{48,16},{56,24},{64,96... | collective-permute-start | bytes 1115144 | tf_op jit(solution)/shard_map/ppermute | solution.py:249
  50.9 16.3 %copy-start.1 = (f32[176,352]{1,0:T(8,128)S(1)}, f32[176,352]{1,0:T(8,128)}, u32[]{:S(2)}) copy-start(f32[176,352]{1,0:T(8,128)} %refs_4_.1) | copy-start | bytes 743428
  50.9 16.3 %copy-start.2 = (f32[176,352]{1,0:T(8,128)S(1)}, f32[176,352]{1,0:T(8,128)}, u32[]{:S(2)}) copy-start(f32[176,352]{1,0:T(8,128)} %refs_5_.1) | copy-start | bytes 743428
  50.9 181.4 %all-gather.20.cloned.1.call-start = ((), (), s32[]{:S(2)}) async-start(), calls=%async_computation.5 | async-start | bytes 2703360 | tf_op jit(solution)/shard_map/all_gather | solution.py:261
  69.7 162.6 %all-gather.18.cloned.1.call-start = ((), (), s32[]{:S(2)}) async-start(), calls=%async_computation.4 | async-start | bytes 2433024 | tf_op jit(solution)/shard_map/all_gather | solution.py:404
  69.8 10.1 %collective-permute-start.5 = (f32[88,176]{1,0:T(8,128)S(1)}, f32[88,176]{1,0:T(8,128)S(1)}, u32[]{:S(2)}, u32[]{:S(2)}) collective-permute-start(f32[88,176]{1,0:T(8,128)S(1)} %get-tuple-element.34), channel_id=1, source_target_pairs={{0,96},{8,104},{16,112},{24,120},{32,64},{40,72},{48,80},{56,88},{... | collective-permute-start | bytes 185864 | tf_op jit(solution)/shard_map/ppermute | solution.py:249
  75.3 7.1 %collective-permute-start.4 = (f32[88,176]{1,0:T(8,128)S(1)}, f32[88,176]{1,0:T(8,128)S(1)}, u32[]{:S(2)}, u32[]{:S(2)}) collective-permute-start(f32[88,176]{1,0:T(8,128)S(1)} %get-tuple-element.34), channel_id=1, source_target_pairs={{0,32},{8,40},{16,48},{24,56},{32,0},{40,8},{48,16},{56,24},{64,96... | collective-permute-start | bytes 185864 | tf_op jit(solution)/shard_map/ppermute | solution.py:249
  77.3 7.3 %collective-permute-start.3 = (f32[88,176]{1,0:T(8,128)S(1)}, f32[88,176]{1,0:T(8,128)S(1)}, u32[]{:S(2)}, u32[]{:S(2)}) collective-permute-start(f32[88,176]{1,0:T(8,128)S(1)} %get-tuple-element.34), channel_id=1, source_target_pairs={{0,64},{8,72},{16,80},{24,88},{32,96},{40,104},{48,112},{56,120},{... | collective-permute-start | bytes 185864 | tf_op jit(solution)/shard_map/ppermute | solution.py:249
  108.2 161.9 %reduce-scatter.2.cloned.1.call-start = ((), (), s32[]{:S(2)}) async-start(), calls=%async_computation.1 | async-start | bytes 3244032 | tf_op jit(solution)/shard_map/reduce_scatter | solution.py:440
  108.2 9.3 %collective-permute-start.6 = (f32[2,176,176]{2,1,0:T(8,128)S(1)}, f32[2,176,176]{2,1,0:T(8,128)S(1)}, u32[]{:S(2)}, u32[]{:S(2)}) collective-permute-start(f32[2,176,176]{2,1,0:T(8,128)S(1)} %get-tuple-element.38), channel_id=1, source_target_pairs={{0,32},{8,40},{16,48},{24,56},{32,0},{40,8},{48,16},{56,24},{64,96... | collective-permute-start | bytes 743432 | tf_op jit(solution)/shard_map/ppermute | solution.py:249
  117.6 44.8 %copy-start.4 = (f32[176,176]{1,0:T(8,128)S(1)}, f32[176,176]{1,0:T(8,128)}, u32[]{:S(2)}) copy-start(f32[176,176]{1,0:T(8,128)} %refs_6_.2) | copy-start | bytes 371716
  168.6 17.3 %copy-start = (f32[704,352]{1,0:T(8,128)S(1)}, f32[704,352]{1,0:T(8,128)}, u32[]{:S(2)}) copy-start(f32[704,352]{1,0:T(8,128)} %all-gather.1) | copy-start | bytes 2973700
  168.6 17.3 %copy-start.6 = (f32[176,88]{1,0:T(8,128)S(1)}, f32[176,88]{1,0:T(8,128)}, u32[]{:S(2)}) copy-start(f32[176,88]{1,0:T(8,128)} %refs_6_.3) | copy-start | bytes 185860
  168.6 17.3 %copy-start.8 = (f32[176,44]{0,1:T(8,128)S(1)}, f32[176,44]{0,1:T(8,128)}, u32[]{:S(2)}) copy-start(f32[176,44]{0,1:T(8,128)} %param.7) | copy-start | bytes 92932
  168.6 4.2 %collective-permute-start.7 = (f32[4,176,176]{2,1,0:T(8,128)S(1)}, f32[4,176,176]{2,1,0:T(8,128)S(1)}, u32[]{:S(2)}, u32[]{:S(2)}) collective-permute-start(f32[4,176,176]{2,1,0:T(8,128)S(1)} %get-tuple-element.40), channel_id=1, source_target_pairs={{0,1},{1,0},{2,3},{3,2},{4,5},{5,4},{6,7},{7,6},{8,9},{9,8},{10,11... | collective-permute-start | bytes 1486856 | tf_op jit(solution)/shard_map/ppermute | solution.py:252
  172.8 0.9 copy-start.10
  175.2 10.7 %collective-permute-start.8 = (f32[176,176]{1,0:T(8,128)S(1)}, f32[176,176]{1,0:T(8,128)S(1)}, u32[]{:S(2)}, u32[]{:S(2)}) collective-permute-start(f32[176,176]{1,0:T(8,128)S(1)} %get-tuple-element.41), channel_id=1, source_target_pairs={{0,2},{1,3},{2,4},{3,5},{4,6},{5,7},{6,0},{7,1},{8,10},{9,11},{10,... | collective-permute-start | bytes 371720 | tf_op jit(solution)/shard_map/ppermute | solution.py:258
  192.9 10.1 %collective-permute-start.9 = (f32[176,176]{1,0:T(8,128)S(1)}, f32[176,176]{1,0:T(8,128)S(1)}, u32[]{:S(2)}, u32[]{:S(2)}) collective-permute-start(f32[176,176]{1,0:T(8,128)S(1)} %get-tuple-element.43), channel_id=1, source_target_pairs={{0,6},{1,7},{2,0},{3,1},{4,2},{5,3},{6,4},{7,5},{8,14},{9,15},{10,... | collective-permute-start | bytes 371720 | tf_op jit(solution)/shard_map/ppermute | solution.py:258
  196.0 10.7 %collective-permute-start.10 = (f32[176,176]{1,0:T(8,128)S(1)}, f32[176,176]{1,0:T(8,128)S(1)}, u32[]{:S(2)}, u32[]{:S(2)}) collective-permute-start(f32[176,176]{1,0:T(8,128)S(1)} %get-tuple-element.44), channel_id=1, source_target_pairs={{0,4},{1,5},{2,6},{3,7},{4,0},{5,1},{6,2},{7,3},{8,12},{9,13},{10,... | collective-permute-start | bytes 371720 | tf_op jit(solution)/shard_map/ppermute | solution.py:258
  207.5 7.4 %collective-permute-start.11 = (f32[176,176]{1,0:T(8,128)S(1)}, f32[176,176]{1,0:T(8,128)S(1)}, u32[]{:S(2)}, u32[]{:S(2)}) collective-permute-start(f32[176,176]{1,0:T(8,128)S(1)} %get-tuple-element.46), channel_id=1, source_target_pairs={{0,32},{8,40},{16,48},{24,56},{32,0},{40,8},{48,16},{56,24},{64,96... | collective-permute-start | bytes 371720 | tf_op jit(solution)/shard_map/ppermute | solution.py:249
  240.9 4.6 %collective-permute-start.12 = (f32[4,176,352]{2,1,0:T(8,128)S(1)}, f32[4,176,352]{2,1,0:T(8,128)S(1)}, u32[]{:S(2)}, u32[]{:S(2)}) collective-permute-start(f32[4,176,352]{2,1,0:T(8,128)S(1)} %get-tuple-element.51), channel_id=1, source_target_pairs={{0,1},{1,0},{2,3},{3,2},{4,5},{5,4},{6,7},{7,6},{8,9},{9,8},{10,11... | collective-permute-start | bytes 2973704 | tf_op jit(solution)/shard_map/ppermute | solution.py:252
  245.5 1.0 copy-start.9
  249.1 10.4 %collective-permute-start.13 = (f32[176,352]{1,0:T(8,128)S(1)}, f32[176,352]{1,0:T(8,128)S(1)}, u32[]{:S(2)}, u32[]{:S(2)}) collective-permute-start(f32[176,352]{1,0:T(8,128)S(1)} %get-tuple-element.53), channel_id=1, source_target_pairs={{0,2},{1,3},{2,4},{3,5},{4,6},{5,7},{6,0},{7,1},{8,10},{9,11},{10,... | collective-permute-start | bytes 743432 | tf_op jit(solution)/shard_map/ppermute | solution.py:258
  252.0 17.1 %collective-permute-start.14 = (f32[176,352]{1,0:T(8,128)S(1)}, f32[176,352]{1,0:T(8,128)S(1)}, u32[]{:S(2)}, u32[]{:S(2)}) collective-permute-start(f32[176,352]{1,0:T(8,128)S(1)} %get-tuple-element.54), channel_id=1, source_target_pairs={{0,6},{1,7},{2,0},{3,1},{4,2},{5,3},{6,4},{7,5},{8,14},{9,15},{10,... | collective-permute-start | bytes 743432 | tf_op jit(solution)/shard_map/ppermute | solution.py:258
  255.0 14.1 %collective-permute-start.15 = (f32[176,352]{1,0:T(8,128)S(1)}, f32[176,352]{1,0:T(8,128)S(1)}, u32[]{:S(2)}, u32[]{:S(2)}) collective-permute-start(f32[176,352]{1,0:T(8,128)S(1)} %get-tuple-element.55), channel_id=1, source_target_pairs={{0,4},{1,5},{2,6},{3,7},{4,0},{5,1},{6,2},{7,3},{8,12},{9,13},{10,... | collective-permute-start | bytes 743432 | tf_op jit(solution)/shard_map/ppermute | solution.py:258
Sparse Core Ops, SparseCore 0:
  10.7 36.2 all-gather.13
  51.0 42.2 all-gather.15
  95.5 55.6 all-gather.19
  153.7 32.8 all-gather.17
  193.0 40.9 reduce-scatter.1

commit v5 on v4

--- a/solution.py
+++ b/solution.py
@@ -142,8 +142,8 @@
     return copies
 
 
-def top_product(rows, columns, p4_ref, f4_ref, out_ref, turned_ref, last_ref, sems):
-    copies = copied([(p4_ref, last_ref.at[0]), (f4_ref, last_ref.at[1])], sems)
+def top_product(rows, columns, p4_ref, out_ref, turned_ref, last_ref, sems):
+    copies = copied([(p4_ref, last_ref)], sems)
     left = rows.ready()
     total = times_columns(4, None, lambda y: left[y], columns.ready(), out_ref.shape[1])
     out_ref[...] = total
@@ -152,9 +152,7 @@
         copy.wait()
 
 
-def next_products(where_ref, a_rows, f2_rows, columns, p4_ref, *refs):
-    b_ref, g_ref, turned_ref, last_ref, sems = refs
-    copies = copied([(p4_ref, last_ref)], sems)
+def next_products(where_ref, a_rows, f2_rows, columns, b_ref, g_ref, turned_ref):
     count, z = b_ref.shape[1], where_ref[2]
     a, f2, right = a_rows.ready(), f2_rows.ready(), columns.ready()
     b = times_columns(2, None, lambda y: f2[y], right, count)
@@ -163,8 +161,6 @@
     )
     b_ref[...], g_ref[...] = b, g
     turned_ref[0], turned_ref[1] = b.T, g.T
-    for copy in copies:
-        copy.wait()
 
 
 def pieces_of(ref, y, planes, z):
@@ -176,7 +172,9 @@
     return jnp.concatenate(pieces, 0)
 
 
-def third_terms(where_ref, b_ref, g_ref, b_rows, g_rows, f3_rows, f3, other_ref, mine_ref):
+def third_terms(where_ref, b_ref, g_ref, b_rows, g_rows, f3_rows, f3, p4_ref, f4_ref, *refs):
+    other_ref, mine_ref, last_ref, sems = refs
+    copies = copied([(p4_ref, last_ref.at[0]), (f4_ref, last_ref.at[1])], sems)
     z = where_ref[2]
     turned = [
         lambda y: pieces_of(b_rows.ready(), y, 2, z),
@@ -185,10 +183,11 @@
     ]
     factors = [split(b_ref[...]), split(g_ref[...]), split(f3.ready()[...])]
     share_terms(where_ref, 2, turned, factors, other_ref, mine_ref)
-
-
-def early_terms(where_ref, f1_rows, f1, a, a_rows, f2_rows, f2, b, g, arrived_ref, out_ref):
-    del arrived_ref
+    for copy in copies:
+        copy.wait()
+
+
+def early_terms(where_ref, f1_rows, f1, a, a_rows, f2_rows, f2, b, g, out_ref):
     z, inner = where_ref[2], a.ready()[...]
     factors = [split(jnp.concatenate([f1.ready()[...].T, -inner], 1))]
     first = factors[0][0].shape[1]
@@ -204,6 +203,14 @@
     ]
     for block, rows, value in sums(4, turned, factors):
         out_ref[block, rows, first:] = value
+
+
+def cut(early_ref, turned_ref, *out_refs):
+    first, at = turned_ref.shape[0], turned_ref.shape[0]
+    turned_ref[...] = early_ref[:, :first].T
+    for out_ref in out_refs:
+        out_ref[...] = early_ref[:, at : at + out_ref.shape[1]]
+        at += out_ref.shape[1]
 
 
 def last_terms(where_ref, parent, columns, p_rows, f_rows, own, *refs):
@@ -330,7 +337,7 @@
         parts = [pieces[0]] + [shift_x(pieces[d], d) for d in (1, 3, 2)]
         outs = [piece, stack(piece.shape[::-1])]
         outs = call(finish, outs, 1_000_000, *[near_by(part) for part in parts])
-        return *outs, parts[1]
+        return outs
 
     def plane_gather(parts):
         gathered = y_gather(jnp.stack(parts))
@@ -376,39 +383,34 @@
 
     work = 6 * share * share * XS * width
     count = panel_two.shape[1]
-    inner, turned, last = call(
+    inner, turned, p4 = call(
         top_product,
-        [stack((share, count)), stack((count, share)), stack((2, share, width))],
+        [stack((share, count)), stack((count, share)), tile],
         work // 4,
         staged(f1_rows),
         staged(panels, *lanes, slice(256, 384)),
         in_hbm(panel_four),
-        in_hbm(factor_four),
         hbm_outs=(2,),
-        semaphores=2,
-    )
-    last_rows = y_gather(last)
+        semaphores=1,
+    )
+    last_panel = lax.all_gather(p4, "front", axis=0)
     a_rows = plane_gather([turned] + [from_plane(turned, d) for d in (2, 1, 3)])
-    b, g, turned, p4 = call(
+    b, g, turned = call(
         next_products,
-        [stack((share, share))] * 2 + [stack((2, share, share)), tile],
+        [stack((share, share))] * 2 + [stack((2, share, share))],
         work,
         where,
         staged(a_rows),
         staged(rows, slice(None), 0),
         staged(panels, *lanes, slice(0, 256)),
-        in_hbm(panel_four),
-        hbm_outs=(3,),
-        semaphores=1,
-    )
-    last_panel = lax.all_gather(p4, "front", axis=0)
+    )
     got = from_plane(turned, 1)
     b_rows, g_rows = (plane_gather([turned[i], got[i]]) for i in range(2))
 
     half_sums = stack((XS, share, share))
-    other, mine = call(
+    other, mine, last = call(
         third_terms,
-        [half_sums, half_sums],
+        [half_sums, half_sums, stack((2, share, width))],
         2 * work,
         where,
         near_by(b),
@@ -417,8 +419,13 @@
         staged(g_rows),
         staged(rows, slice(None), 1),
         staged(factor_three),
-    )
-    cov_three, turned, arrived = front_total(other, mine)
+        in_hbm(panel_four),
+        in_hbm(factor_four),
+        hbm_outs=(2,),
+        semaphores=2,
+    )
+    last_rows = y_gather(last)
+    cov_three, turned = front_total(other, mine)
 
     widths = [top_factor.shape[1], count, count, share]
     (early,) = call(
@@ -434,14 +441,12 @@
         staged(factor_two),
         staged(b),
         staged(g),
-        near_by(arrived),
-    )
+    )
+    early, turned = lax.optimization_barrier((early, turned))
     early = early.reshape(fronts * share, -1)
     early = lax.psum_scatter(early, "front", scatter_dimension=0, tiled=True)
-    at = [sum(widths[:i]) for i in range(len(widths))]
-    cov_one, cross_two, cov_two, cross_three = (
-        early[:, i : i + w] for i, w in zip(at, widths)
-    )
+    cuts = [stack((widths[0], share))] + [stack((share, w)) for w in widths[1:]]
+    cov_one, cross_two, cov_two, cross_three = call(cut, cuts, 1_000_000, near_by(early))
 
     parent_rows = plane_gather([turned, from_plane(turned, 1)])
     cross_four, other, mine = call(
@@ -455,8 +460,8 @@
         staged(last_rows, slice(None), 1),
         staged(factor_four),
     )
-    cov_four, *_ = front_total(other, mine)
-    return cov_one, cross_two, cov_two, cross_three, cov_three, cross_four, cov_four
+    cov_four, _ = front_total(other, mine)
+    return cov_one.T, cross_two, cov_two, cross_three, cov_three, cross_four, cov_four
 
 
 def solution(mesh):

time: 283 us -> 266 us (0.940)
  waiting for transfers between devices: 63.6 us -> 54.4 us
  blocking collectives: 97.5 us -> 88.4 us
  local copies, waits for them, and re-layouts: 9.7 us -> 6.63 us
    ppermute x6, waiting for transfers between devices: 25.5 us -> 15.8 us  [shift_x(): return lax.ppermute(value, 'front', pairs)]
    all_gather x5, blocking collectives: 97.5 us -> 88.4 us  [y_gather(): return lax.all_gather(value, 'leaf', axis=0, axis_index_groups=y_groups)]
    slice x3 -> x0, local copies, waits for them, and re-layouts: 4.41 us -> none  [local(): early[:, i:i + w]]
    pallas_call x12 -> x13, Pallas kernels: 37.5 us -> 39.1 us  [call(): pl.pallas_call(body, out_shape=out_shape, grid=(1,), in_specs=specs, out_...]
    unnamed x23 -> x24, local copies, waits for them, and re-layouts: 5.24 us -> 6.58 us
  transfers between devices with their start and end apart: 21 -> 21, of which waited for: 14 -> 12; matrix products, arithmetic and copies ran while one was open for 0% -> 0% of each run, Pallas kernels for 12% -> 14%
where the time goes in v5:
time: 266 us; the launch traced here: 262 us
  blocking collectives  88.4 us (33%)
  starting transfers between devices  57.4 us (22%)
  waiting for transfers between devices  54.4 us (20%)
  Pallas kernels  39.1 us (15%)
  between operations  14.2 us (5%)
  local copies, waits for them, and re-layouts  6.63 us (2%)
    all_gather x5, blocking collectives, y_gather(): return lax.all_gather(value, 'leaf', axis=0, axis_index_groups=y_groups)  88.4 us
    pallas_call x13, Pallas kernels, call(): pl.pallas_call(body, out_shape=out_shape, grid=(1,), in_specs=specs, out_...  39.1 us
    ppermute x8, starting transfers between devices, from_plane(): return lax.ppermute(value, 'leaf', pairs)  34.9 us
    ppermute x8, waiting for transfers between devices, from_plane(): return lax.ppermute(value, 'leaf', pairs)  33.5 us
    ppermute x6, starting transfers between devices, shift_x(): return lax.ppermute(value, 'front', pairs)  18.4 us
    ppermute x6, waiting for transfers between devices, shift_x(): return lax.ppermute(value, 'front', pairs)  15.8 us
    unnamed x24, local copies, waits for them, and re-layouts  6.58 us
  transfers between devices with their start and end apart: 21, of which 12 were waited for; matrix products, arithmetic and copies ran while one was open for 0% of the time, Pallas kernels for 14%

profile of v5, /device:TPU:6, one launch (start us, length us, event | category | flops | bytes accessed | tf_op | source)
XLA Modules:
  0.0 262.1 jit_solution(15626061617486169406)
XLA Ops:
  7.2 0.0 all-gather.14.cloned.1.call-start
  7.2 1.7 select_maximum_fusion
  8.9 0.0 all-gather.16.cloned.1.call-start
  9.0 9.1 %collective-permute-start = (f32[44,176]{1,0:T(8,128)}, f32[44,176]{1,0:T(8,128)S(1)}, u32[]{:S(2)}, u32[]{:S(2)}) collective-permute-start(f32[44,176]{1,0:T(8,128)} %bitcast.19), channel_id=1, source_target_pairs={{0,128},{8,136},{16,144},{24,152},{32,160},{40,168},{48,176},{56,1... | collective-permute-start | bytes 92936 | tf_op jit(solution)/shard_map/ppermute | solution.py:256
  18.1 2.3 collective-permute-done.refs_2_
  20.4 0.9 copy-done.6
  21.3 0.8 copy-done.8
  22.0 0.3 shard_map.126.refs_0_
  22.4 5.4 %collective-permute-start.1 = (f32[88,352]{1,0:T(8,128)S(1)}, f32[88,352]{1,0:T(8,128)S(1)}, u32[]{:S(2)}, u32[]{:S(2)}) collective-permute-start(f32[88,352]{1,0:T(8,128)S(1)} %shard_map.126.refs_0_), channel_id=1, source_target_pairs={{0,64},{8,72},{16,80},{24,88},{32,96},{40,104},{48,112},{56,120},{... | collective-permute-start | bytes 371720 | tf_op jit(solution)/shard_map/ppermute | solution.py:256
  27.8 6.6 %collective-permute-done.1.refs_1_ = f32[88,352]{1,0:T(8,128)S(1)} collective-permute-done((f32[88,352]{1,0:T(8,128)S(1)}, f32[88,352]{1,0:T(8,128)S(1)}, u32[]{:S(2)}, u32[]{:S(2)}) %collective-permute-start.1) | collective-permute-done | bytes 123936 | tf_op jit(solution)/shard_map/ppermute | solution.py:256
  34.5 0.9 copy-done.2
  35.4 0.4 shard_map.127.refs_1_
  35.8 2.6 %collective-permute-start.2 = (f32[88,1056]{1,0:T(8,128)S(1)}, f32[88,1056]{1,0:T(8,128)S(1)}, u32[]{:S(2)}, u32[]{:S(2)}) collective-permute-start(f32[88,1056]{1,0:T(8,128)S(1)} %shard_map.127.refs_1_), channel_id=1, source_target_pairs={{0,32},{8,40},{16,48},{24,56},{32,0},{40,8},{48,16},{56,24},{64,96... | collective-permute-start | bytes 1115144 | tf_op jit(solution)/shard_map/ppermute | solution.py:256
  38.5 0.1 pad_add_fusion.refs_0_
  38.6 9.9 %collective-permute-done.2.refs_2_ = f32[88,1056]{1,0:T(8,128)S(1)} collective-permute-done((f32[88,1056]{1,0:T(8,128)S(1)}, f32[88,1056]{1,0:T(8,128)S(1)}, u32[]{:S(2)}, u32[]{:S(2)}) %collective-permute-start.2) | collective-permute-done | bytes 371744 | tf_op jit(solution)/shard_map/ppermute | solution.py:256
  48.5 2.4 shard_map.128
  50.9 0.0 all-gather.16.cloned.1.call-update
  50.9 0.0 all-gather.18.cloned.1.call-start
  50.9 15.1 %all-gather.1 = f32[704,352]{1,0:T(8,128)S(1)} all-gather(f32[176,352]{1,0:T(8,128)S(1)} %get-tuple-element.38), channel_id=3, replica_groups={{0,8,16,24},{32,40,48,56},{64,72,80,88},{96,104,112,120},{128,136,144,1..., dimensions={0}, use_global_device_ids=true | all-gather | bytes 1239040 | tf_op jit(solution)/shard_map/all_gather | solution.py:268
  66.1 2.2 shard_map.129
  68.3 0.0 all-gather.18.cloned.1.call-update
  68.3 0.0 all-gather.20.cloned.1.call-start
  68.3 6.3 %collective-permute-start.5 = (f32[88,176]{1,0:T(8,128)S(1)}, f32[88,176]{1,0:T(8,128)S(1)}, u32[]{:S(2)}, u32[]{:S(2)}) collective-permute-start(f32[88,176]{1,0:T(8,128)S(1)} %get-tuple-element.40), channel_id=1, source_target_pairs={{0,96},{8,104},{16,112},{24,120},{32,64},{40,72},{48,80},{56,88},{... | collective-permute-start | bytes 185864 | tf_op jit(solution)/shard_map/ppermute | solution.py:256
  74.6 1.9 collective-permute-start.4
  76.5 2.5 collective-permute-start.3
  79.0 2.1 collective-permute-done.4
  81.1 2.7 %collective-permute-done.3 = f32[88,176]{1,0:T(8,128)S(1)} collective-permute-done((f32[88,176]{1,0:T(8,128)S(1)}, f32[88,176]{1,0:T(8,128)S(1)}, u32[]{:S(2)}, u32[]{:S(2)}) %collective-permute-start.3) | collective-permute-done | bytes 61984 | tf_op jit(solution)/shard_map/ppermute | solution.py:256
  83.9 20.0 %all-gather.2.refs_1_.refs_4_ = f32[16,88,176]{2,1,0:T(8,128)} all-gather(f32[4,88,176]{2,1,0:T(8,128)S(1)} %pad_maximum_fusion), channel_id=4, replica_groups={{0,8,16,24},{32,40,48,56},{64,72,80,88},{96,104,112,120},{128,136,144,1..., dimensions={0}, use_global_device_ids=true | all-gather | bytes 1239040 | tf_op jit(solution)/shard_map/all_gather | solution.py:268
  103.9 4.1 %shard_map.130 = (f32[176,176]{1,0:T(8,128)S(1)}, f32[176,176]{1,0:T(8,128)S(1)}, f32[2,176,176]{2,1,0:T(8,128)S(1)}) custom-call(s32[3]{0:T(128)S(1)} %pad_add_fusion.refs_0_, f32[16,88,176]{2,1,0:T(8,128)} %all-gather.2.refs_1_.refs_4_, f32[4,2,176,352]{3,2,1,0:T(8,128)} %bitcast.27, f32[8,176,384]{2,1,0:T(8,128)} %bitcast.26), custom_call_target="tpu_custom_call" | custom-call | flops 261685248 | bytes 8000000 | tf_op jit(solution)/shard_map/pallas_call | solution.py:320
  108.0 3.6 %collective-permute-start.6 = (f32[2,176,176]{2,1,0:T(8,128)S(1)}, f32[2,176,176]{2,1,0:T(8,128)S(1)}, u32[]{:S(2)}, u32[]{:S(2)}) collective-permute-start(f32[2,176,176]{2,1,0:T(8,128)S(1)} %get-tuple-element.44), channel_id=1, source_target_pairs={{0,32},{8,40},{16,48},{24,56},{32,0},{40,8},{48,16},{56,24},{64,96... | collective-permute-start | bytes 743432 | tf_op jit(solution)/shard_map/ppermute | solution.py:256
  111.7 5.7 %collective-permute-done.6 = f32[2,176,176]{2,1,0:T(8,128)S(1)} collective-permute-done((f32[2,176,176]{2,1,0:T(8,128)S(1)}, f32[2,176,176]{2,1,0:T(8,128)S(1)}, u32[]{:S(2)}, u32[]{:S(2)}) %collective-permute-start.6) | collective-permute-done | bytes 247840 | tf_op jit(solution)/shard_map/ppermute | solution.py:256
  117.5 17.8 %all-gather.4.refs_3_ = f32[8,176,176]{2,1,0:T(8,128)} all-gather(f32[2,176,176]{2,1,0:T(8,128)S(1)} %pad_maximum_fusion.1), channel_id=6, replica_groups={{0,8,16,24},{32,40,48,56},{64,72,80,88},{96,104,112,120},{128,136,144,1..., dimensions={0}, use_global_device_ids=true | all-gather | bytes 1239040 | tf_op jit(solution)/shard_map/all_gather | solution.py:268
  135.3 15.8 %all-gather.5.refs_4_ = f32[8,176,176]{2,1,0:T(8,128)} all-gather(f32[2,176,176]{2,1,0:T(8,128)S(1)} %pad_maximum_fusion.2), channel_id=7, replica_groups={{0,8,16,24},{32,40,48,56},{64,72,80,88},{96,104,112,120},{128,136,144,1..., dimensions={0}, use_global_device_ids=true | all-gather | bytes 1239040 | tf_op jit(solution)/shard_map/all_gather | solution.py:268
  151.1 7.5 %shard_map.132 = (f32[4,176,176]{2,1,0:T(8,128)}, f32[4,176,176]{2,1,0:T(8,128)}, f32[2,176,352]{2,1,0:T(8,128)}) custom-call(s32[3]{0:T(128)S(1)} %pad_add_fusion.refs_0_, f32[176,176]{1,0:T(8,128)S(1)} %get-tuple-element.42.refs_7_.refs_1_, f32[176,176]{1,0:T(8,128)S(1)} %get-tuple-element.43.refs_8_.refs_2_, f32[8,176,176]{2,1,0:T(8,128)} %all-gather.4.refs_3_, ...), custom_call_target="tpu_custom_call" | custom-call | flops 523370496 | bytes 8000000 | tf_op jit(solution)/shard_map/pallas_call | solution.py:320
  158.7 0.0 all-gather.20.cloned.1.call-update
  158.7 0.0 reduce-scatter.2.cloned.1.call-start
  158.7 1.9 collective-permute-start.7
  160.7 2.4 collective-permute-done.7.refs_1_
  163.0 0.9 copy-done.11
  163.9 1.1 copy-done.4
  165.0 1.5 shard_map.133
  166.5 2.1 collective-permute-start.8
  168.6 3.7 %collective-permute-start.9 = (f32[176,176]{1,0:T(8,128)S(1)}, f32[176,176]{1,0:T(8,128)S(1)}, u32[]{:S(2)}, u32[]{:S(2)}) collective-permute-start(f32[176,176]{1,0:T(8,128)S(1)} %get-tuple-element.49), channel_id=1, source_target_pairs={{0,6},{1,7},{2,0},{3,1},{4,2},{5,3},{6,4},{7,5},{8,14},{9,15},{10,... | collective-permute-start | bytes 371720 | tf_op jit(solution)/shard_map/ppermute | solution.py:265
  172.3 3.3 %collective-permute-start.10 = (f32[176,176]{1,0:T(8,128)S(1)}, f32[176,176]{1,0:T(8,128)S(1)}, u32[]{:S(2)}, u32[]{:S(2)}) collective-permute-start(f32[176,176]{1,0:T(8,128)S(1)} %get-tuple-element.50), channel_id=1, source_target_pairs={{0,4},{1,5},{2,6},{3,7},{4,0},{5,1},{6,2},{7,3},{8,12},{9,13},{10,... | collective-permute-start | bytes 371720 | tf_op jit(solution)/shard_map/ppermute | solution.py:265
  175.7 7.0 %shard_map.131 = f32[8,176,396]{2,1,0:T(8,128)} custom-call(s32[3]{0:T(128)S(1)} %pad_add_fusion.refs_0_, f32[4,176,352]{2,1,0:T(8,128)S(1)} %bitcast.18, f32[44,176]{1,0:T(8,128)S(1)} %bitcast.21, f32[176,88]{1,0:T(8,128)S(1)} %get-tuple-element.39.refs_3_, f32[16,88,176]{2,1,0:T(8,128)} %all-gather.2.refs_1_.refs_4_, f32[4,2,176,352]{3,2,1,0:T(8,128)} %bitcast.29, ...), custom_call_target="tpu_custom_call" | custom-call | flops 523370496 | bytes 8000000 | tf_op jit(solution)/shard_map/pallas_call | solution.py:320
  182.7 0.7 shard_map.134
  183.5 3.5 %collective-permute-start.11 = (f32[176,176]{1,0:T(8,128)S(1)}, f32[176,176]{1,0:T(8,128)S(1)}, u32[]{:S(2)}, u32[]{:S(2)}) collective-permute-start(f32[176,176]{1,0:T(8,128)S(1)} %get-tuple-element.58), channel_id=1, source_target_pairs={{0,32},{8,40},{16,48},{24,56},{32,0},{40,8},{48,16},{56,24},{64,96... | collective-permute-start | bytes 371720 | tf_op jit(solution)/shard_map/ppermute | solution.py:256
  187.0 4.1 %collective-permute-done.11 = f32[176,176]{1,0:T(8,128)S(1)} collective-permute-done((f32[176,176]{1,0:T(8,128)S(1)}, f32[176,176]{1,0:T(8,128)S(1)}, u32[]{:S(2)}, u32[]{:S(2)}) %collective-permute-start.11) | collective-permute-done | bytes 123936 | tf_op jit(solution)/shard_map/ppermute | solution.py:256
  191.2 19.6 %all-gather.6.refs_1_ = f32[8,176,176]{2,1,0:T(8,128)} all-gather(f32[2,176,176]{2,1,0:T(8,128)S(1)} %pad_maximum_fusion.3), channel_id=8, replica_groups={{0,8,16,24},{32,40,48,56},{64,72,80,88},{96,104,112,120},{128,136,144,1..., dimensions={0}, use_global_device_ids=true | all-gather | bytes 1239040 | tf_op jit(solution)/shard_map/all_gather | solution.py:268
  210.8 8.5 %shard_map.136 = (f32[176,352]{1,0:T(8,128)}, f32[4,176,352]{2,1,0:T(8,128)S(1)}, f32[4,176,352]{2,1,0:T(8,128)}) custom-call(s32[3]{0:T(128)S(1)} %pad_add_fusion.refs_0_, f32[8,176,176]{2,1,0:T(8,128)} %all-gather.6.refs_1_, f32[8,176,352]{2,1,0:T(8,128)} %bitcast.33, f32[4,2,176,352]{3,2,1,0:T(8,128)} %bitcast.31, f32[4,2,176,352]{3,2,1,0:T(8,128)} %bitcast.32, ...), custom_call_target="tpu_custom_call" | custom-call | flops 1046740992 | bytes 8000000 | tf_op jit(solution)/shard_map/pallas_call | solution.py:320
  219.3 1.9 collective-permute-start.12
  221.3 2.7 %collective-permute-done.12.refs_1_ = f32[4,176,352]{2,1,0:T(8,128)S(1)} collective-permute-done((f32[4,176,352]{2,1,0:T(8,128)S(1)}, f32[4,176,352]{2,1,0:T(8,128)S(1)}, u32[]{:S(2)}, u32[]{:S(2)}) %collective-permute-start.12) | collective-permute-done | bytes 991264 | tf_op jit(solution)/shard_map/ppermute | solution.py:259
  223.9 1.0 copy-done.10
  224.9 2.6 %shard_map.137 = (f32[176,352]{1,0:T(8,128)S(1)}, f32[176,352]{1,0:T(8,128)S(1)}, f32[176,352]{1,0:T(8,128)S(1)}, f32[176,352]{1,0:T(8,128)S(1)}) custom-call(f32[4,176,352]{2,1,0:T(8,128)} %get-tuple-element.62.refs_0_, f32[4,176,352]{2,1,0:T(8,128)} %copy-done.10), custom_call_target="tpu_custom_call" | custom-call | flops 1000000 | bytes 8000000 | tf_op jit(solution)/shard_map/pallas_call | solution.py:320
  227.6 2.5 collective-permute-start.13
  230.0 3.4 %collective-permute-start.14 = (f32[176,352]{1,0:T(8,128)S(1)}, f32[176,352]{1,0:T(8,128)S(1)}, u32[]{:S(2)}, u32[]{:S(2)}) collective-permute-start(f32[176,352]{1,0:T(8,128)S(1)} %get-tuple-element.66), channel_id=1, source_target_pairs={{0,6},{1,7},{2,0},{3,1},{4,2},{5,3},{6,4},{7,5},{8,14},{9,15},{10,... | collective-permute-start | bytes 743432 | tf_op jit(solution)/shard_map/ppermute | solution.py:265
  233.4 3.4 %collective-permute-start.15 = (f32[176,352]{1,0:T(8,128)S(1)}, f32[176,352]{1,0:T(8,128)S(1)}, u32[]{:S(2)}, u32[]{:S(2)}) collective-permute-start(f32[176,352]{1,0:T(8,128)S(1)} %get-tuple-element.67), channel_id=1, source_target_pairs={{0,4},{1,5},{2,6},{3,7},{4,0},{5,1},{6,2},{7,3},{8,12},{9,13},{10,... | collective-permute-start | bytes 743432 | tf_op jit(solution)/shard_map/ppermute | solution.py:265
  236.8 4.8 %collective-permute-done.13.refs_1_ = f32[176,352]{1,0:T(8,128)S(1)} collective-permute-done((f32[176,352]{1,0:T(8,128)S(1)}, f32[176,352]{1,0:T(8,128)S(1)}, u32[]{:S(2)}, u32[]{:S(2)}) %collective-permute-start.13) | collective-permute-done | bytes 247840 | tf_op jit(solution)/shard_map/ppermute | solution.py:265
  241.6 2.5 collective-permute-done.14.refs_2_
  244.2 8.5 %collective-permute-done.15.refs_3_ = f32[176,352]{1,0:T(8,128)S(1)} collective-permute-done((f32[176,352]{1,0:T(8,128)S(1)}, f32[176,352]{1,0:T(8,128)S(1)}, u32[]{:S(2)}, u32[]{:S(2)}) %collective-permute-start.15) | collective-permute-done | bytes 247840 | tf_op jit(solution)/shard_map/ppermute | solution.py:265
  252.6 0.9 shard_map.138
  253.6 0.0 reduce-scatter.2.cloned.1.call-done.refs_0_
  253.6 1.0 copy-done.5
  254.6 0.9 shard_map.135
  (33 shorter events, 0.3 us)
Async XLA Ops:
  7.2 41.3 %all-gather.14.cloned.1.call-start = ((), (), s32[]{:S(2)}) async-start(), calls=%async_computation.2 | async-start | bytes 2433024 | tf_op jit(solution)/shard_map/all_gather | solution.py:350
  8.9 95.0 %all-gather.16.cloned.1.call-start = ((), (), s32[]{:S(2)}) async-start(), calls=%async_computation.3 | async-start | bytes 2703360 | tf_op jit(solution)/shard_map/all_gather | solution.py:268
  9.0 11.4 %collective-permute-start = (f32[44,176]{1,0:T(8,128)}, f32[44,176]{1,0:T(8,128)S(1)}, u32[]{:S(2)}, u32[]{:S(2)}) collective-permute-start(f32[44,176]{1,0:T(8,128)} %bitcast.19), channel_id=1, source_target_pairs={{0,128},{8,136},{16,144},{24,152},{32,160},{40,168},{48,176},{56,1... | collective-permute-start | bytes 92936 | tf_op jit(solution)/shard_map/ppermute | solution.py:256
  20.4 0.9 copy-start.6
  21.3 0.8 copy-start.8
  22.4 12.1 %collective-permute-start.1 = (f32[88,352]{1,0:T(8,128)S(1)}, f32[88,352]{1,0:T(8,128)S(1)}, u32[]{:S(2)}, u32[]{:S(2)}) collective-permute-start(f32[88,352]{1,0:T(8,128)S(1)} %shard_map.126.refs_0_), channel_id=1, source_target_pairs={{0,64},{8,72},{16,80},{24,88},{32,96},{40,104},{48,112},{56,120},{... | collective-permute-start | bytes 371720 | tf_op jit(solution)/shard_map/ppermute | solution.py:256
  34.4 0.9 copy-start.2
  35.8 12.7 %collective-permute-start.2 = (f32[88,1056]{1,0:T(8,128)S(1)}, f32[88,1056]{1,0:T(8,128)S(1)}, u32[]{:S(2)}, u32[]{:S(2)}) collective-permute-start(f32[88,1056]{1,0:T(8,128)S(1)} %shard_map.127.refs_1_), channel_id=1, source_target_pairs={{0,32},{8,40},{16,48},{24,56},{32,0},{40,8},{48,16},{56,24},{64,96... | collective-permute-start | bytes 1115144 | tf_op jit(solution)/shard_map/ppermute | solution.py:256
  50.9 15.2 %copy-start.1 = (f32[176,352]{1,0:T(8,128)S(1)}, f32[176,352]{1,0:T(8,128)}, u32[]{:S(2)}) copy-start(f32[176,352]{1,0:T(8,128)} %refs_7_.1) | copy-start | bytes 743428
  50.9 159.9 %all-gather.18.cloned.1.call-start = ((), (), s32[]{:S(2)}) async-start(), calls=%async_computation.4 | async-start | bytes 2433024 | tf_op jit(solution)/shard_map/all_gather | solution.py:396
  68.3 142.5 %all-gather.20.cloned.1.call-start = ((), (), s32[]{:S(2)}) async-start(), calls=%async_computation.5 | async-start | bytes 2703360 | tf_op jit(solution)/shard_map/all_gather | solution.py:268
  68.3 10.7 %collective-permute-start.5 = (f32[88,176]{1,0:T(8,128)S(1)}, f32[88,176]{1,0:T(8,128)S(1)}, u32[]{:S(2)}, u32[]{:S(2)}) collective-permute-start(f32[88,176]{1,0:T(8,128)S(1)} %get-tuple-element.40), channel_id=1, source_target_pairs={{0,96},{8,104},{16,112},{24,120},{32,64},{40,72},{48,80},{56,88},{... | collective-permute-start | bytes 185864 | tf_op jit(solution)/shard_map/ppermute | solution.py:256
  74.6 6.5 %collective-permute-start.4 = (f32[88,176]{1,0:T(8,128)S(1)}, f32[88,176]{1,0:T(8,128)S(1)}, u32[]{:S(2)}, u32[]{:S(2)}) collective-permute-start(f32[88,176]{1,0:T(8,128)S(1)} %get-tuple-element.40), channel_id=1, source_target_pairs={{0,32},{8,40},{16,48},{24,56},{32,0},{40,8},{48,16},{56,24},{64,96... | collective-permute-start | bytes 185864 | tf_op jit(solution)/shard_map/ppermute | solution.py:256
  76.5 7.3 %collective-permute-start.3 = (f32[88,176]{1,0:T(8,128)S(1)}, f32[88,176]{1,0:T(8,128)S(1)}, u32[]{:S(2)}, u32[]{:S(2)}) collective-permute-start(f32[88,176]{1,0:T(8,128)S(1)} %get-tuple-element.40), channel_id=1, source_target_pairs={{0,64},{8,72},{16,80},{24,88},{32,96},{40,104},{48,112},{56,120},{... | collective-permute-start | bytes 185864 | tf_op jit(solution)/shard_map/ppermute | solution.py:256
  108.0 9.3 %collective-permute-start.6 = (f32[2,176,176]{2,1,0:T(8,128)S(1)}, f32[2,176,176]{2,1,0:T(8,128)S(1)}, u32[]{:S(2)}, u32[]{:S(2)}) collective-permute-start(f32[2,176,176]{2,1,0:T(8,128)S(1)} %get-tuple-element.44), channel_id=1, source_target_pairs={{0,32},{8,40},{16,48},{24,56},{32,0},{40,8},{48,16},{56,24},{64,96... | collective-permute-start | bytes 743432 | tf_op jit(solution)/shard_map/ppermute | solution.py:256
  117.4 33.7 %copy-start = (f32[176,352]{1,0:T(8,128)S(1)}, f32[176,352]{1,0:T(8,128)}, u32[]{:S(2)}) copy-start(f32[176,352]{1,0:T(8,128)} %refs_5_.1) | copy-start | bytes 743428
  117.5 33.7 %copy-start.3 = (f32[176,176]{1,0:T(8,128)S(1)}, f32[176,176]{1,0:T(8,128)}, u32[]{:S(2)}) copy-start(f32[176,176]{1,0:T(8,128)} %refs_6_.3) | copy-start | bytes 371716
  158.6 17.1 %copy-start.7 = (f32[176,88]{1,0:T(8,128)S(1)}, f32[176,88]{1,0:T(8,128)}, u32[]{:S(2)}) copy-start(f32[176,88]{1,0:T(8,128)} %refs_6_.2) | copy-start | bytes 185860
  158.6 17.1 %copy-start.9 = (f32[176,44]{0,1:T(8,128)S(1)}, f32[176,44]{0,1:T(8,128)}, u32[]{:S(2)}) copy-start(f32[176,44]{0,1:T(8,128)} %param.7) | copy-start | bytes 92932
  158.7 94.9 %reduce-scatter.2.cloned.1.call-start = ((), (), s32[]{:S(2)}) async-start(), calls=%async_computation.1 | async-start | bytes 3244032 | tf_op jit(solution)/shard_map/reduce_scatter | solution.py:447
  158.7 4.3 %collective-permute-start.7 = (f32[4,176,176]{2,1,0:T(8,128)}, f32[4,176,176]{2,1,0:T(8,128)S(1)}, u32[]{:S(2)}, u32[]{:S(2)}) collective-permute-start(f32[4,176,176]{2,1,0:T(8,128)} %get-tuple-element.46), channel_id=1, source_target_pairs={{0,1},{1,0},{2,3},{3,2},{4,5},{5,4},{6,7},{7,6},{8,9},{9,8},{10,11... | collective-permute-start | bytes 1486856 | tf_op jit(solution)/shard_map/ppermute | solution.py:259
  163.0 0.9 copy-start.11
  163.9 1.1 copy-start.4
  166.5 16.2 %collective-permute-start.8 = (f32[176,176]{1,0:T(8,128)S(1)}, f32[176,176]{1,0:T(8,128)S(1)}, u32[]{:S(2)}, u32[]{:S(2)}) collective-permute-start(f32[176,176]{1,0:T(8,128)S(1)} %get-tuple-element.48), channel_id=1, source_target_pairs={{0,2},{1,3},{2,4},{3,5},{4,6},{5,7},{6,0},{7,1},{8,10},{9,11},{10,... | collective-permute-start | bytes 371720 | tf_op jit(solution)/shard_map/ppermute | solution.py:265
  168.6 14.1 %collective-permute-start.9 = (f32[176,176]{1,0:T(8,128)S(1)}, f32[176,176]{1,0:T(8,128)S(1)}, u32[]{:S(2)}, u32[]{:S(2)}) collective-permute-start(f32[176,176]{1,0:T(8,128)S(1)} %get-tuple-element.49), channel_id=1, source_target_pairs={{0,6},{1,7},{2,0},{3,1},{4,2},{5,3},{6,4},{7,5},{8,14},{9,15},{10,... | collective-permute-start | bytes 371720 | tf_op jit(solution)/shard_map/ppermute | solution.py:265
  172.3 10.4 %collective-permute-start.10 = (f32[176,176]{1,0:T(8,128)S(1)}, f32[176,176]{1,0:T(8,128)S(1)}, u32[]{:S(2)}, u32[]{:S(2)}) collective-permute-start(f32[176,176]{1,0:T(8,128)S(1)} %get-tuple-element.50), channel_id=1, source_target_pairs={{0,4},{1,5},{2,6},{3,7},{4,0},{5,1},{6,2},{7,3},{8,12},{9,13},{10,... | collective-permute-start | bytes 371720 | tf_op jit(solution)/shard_map/ppermute | solution.py:265
  183.5 7.6 %collective-permute-start.11 = (f32[176,176]{1,0:T(8,128)S(1)}, f32[176,176]{1,0:T(8,128)S(1)}, u32[]{:S(2)}, u32[]{:S(2)}) collective-permute-start(f32[176,176]{1,0:T(8,128)S(1)} %get-tuple-element.58), channel_id=1, source_target_pairs={{0,32},{8,40},{16,48},{24,56},{32,0},{40,8},{48,16},{56,24},{64,96... | collective-permute-start | bytes 371720 | tf_op jit(solution)/shard_map/ppermute | solution.py:256
  219.3 4.6 %collective-permute-start.12 = (f32[4,176,352]{2,1,0:T(8,128)S(1)}, f32[4,176,352]{2,1,0:T(8,128)S(1)}, u32[]{:S(2)}, u32[]{:S(2)}) collective-permute-start(f32[4,176,352]{2,1,0:T(8,128)S(1)} %get-tuple-element.63), channel_id=1, source_target_pairs={{0,1},{1,0},{2,3},{3,2},{4,5},{5,4},{6,7},{7,6},{8,9},{9,8},{10,11... | collective-permute-start | bytes 2973704 | tf_op jit(solution)/shard_map/ppermute | solution.py:259
  223.9 1.0 copy-start.10
  227.6 14.1 %collective-permute-start.13 = (f32[176,352]{1,0:T(8,128)S(1)}, f32[176,352]{1,0:T(8,128)S(1)}, u32[]{:S(2)}, u32[]{:S(2)}) collective-permute-start(f32[176,352]{1,0:T(8,128)S(1)} %get-tuple-element.65), channel_id=1, source_target_pairs={{0,2},{1,3},{2,4},{3,5},{4,6},{5,7},{6,0},{7,1},{8,10},{9,11},{10,... | collective-permute-start | bytes 743432 | tf_op jit(solution)/shard_map/ppermute | solution.py:265
  230.0 14.1 %collective-permute-start.14 = (f32[176,352]{1,0:T(8,128)S(1)}, f32[176,352]{1,0:T(8,128)S(1)}, u32[]{:S(2)}, u32[]{:S(2)}) collective-permute-start(f32[176,352]{1,0:T(8,128)S(1)} %get-tuple-element.66), channel_id=1, source_target_pairs={{0,6},{1,7},{2,0},{3,1},{4,2},{5,3},{6,4},{7,5},{8,14},{9,15},{10,... | collective-permute-start | bytes 743432 | tf_op jit(solution)/shard_map/ppermute | solution.py:265
  233.4 19.2 %collective-permute-start.15 = (f32[176,352]{1,0:T(8,128)S(1)}, f32[176,352]{1,0:T(8,128)S(1)}, u32[]{:S(2)}, u32[]{:S(2)}) collective-permute-start(f32[176,352]{1,0:T(8,128)S(1)} %get-tuple-element.67), channel_id=1, source_target_pairs={{0,4},{1,5},{2,6},{3,7},{4,0},{5,1},{6,2},{7,3},{8,12},{9,13},{10,... | collective-permute-start | bytes 743432 | tf_op jit(solution)/shard_map/ppermute | solution.py:265
  253.6 1.0 copy-start.5
Sparse Core Ops, SparseCore 0:
  10.7 36.2 all-gather.13
  51.0 43.4 all-gather.15
  97.2 35.3 all-gather.17
  158.8 42.5 all-gather.19
  204.1 47.9 reduce-scatter.1

commit v6 on v5

--- a/solution.py
+++ b/solution.py
@@ -95,21 +95,6 @@
                 column = (plane * Y + y) * width + part
                 value = total[plane * width + part : plane * width + part + step]
                 yield column // 176, slice(column % 176, column % 176 + step), value
-
-
-def share_terms(where_ref, planes, turned, factors, other_ref, mine_ref):
-    x, core = where_ref[0], where_ref[1]
-    for block, rows, value in sums(planes, turned, factors):
-        at = (block // CORES - x) % XS
-        same = core == (block % CORES)
-
-        @pl.when(same)
-        def _():
-            mine_ref[at, rows, :] = value
-
-        @pl.when(jnp.logical_not(same))
-        def _():
-            other_ref[at, rows, :] = value
 
 
 def times_columns(planes, distances, left, columns_ref, count):
@@ -132,24 +117,11 @@
     return total
 
 
-def copied(pairs, sems):
-    copies = [
-        pltpu.make_async_copy(source, target, sems.at[index])
-        for index, (source, target) in enumerate(pairs)
-    ]
-    for copy in copies:
-        copy.start()
-    return copies
-
-
-def top_product(rows, columns, p4_ref, out_ref, turned_ref, last_ref, sems):
-    copies = copied([(p4_ref, last_ref)], sems)
+def top_product(rows, columns, out_ref, turned_ref):
     left = rows.ready()
     total = times_columns(4, None, lambda y: left[y], columns.ready(), out_ref.shape[1])
     out_ref[...] = total
     turned_ref[...] = total.T
-    for copy in copies:
-        copy.wait()
 
 
 def next_products(where_ref, a_rows, f2_rows, columns, b_ref, g_ref, turned_ref):
@@ -172,19 +144,19 @@
     return jnp.concatenate(pieces, 0)
 
 
-def third_terms(where_ref, b_ref, g_ref, b_rows, g_rows, f3_rows, f3, p4_ref, f4_ref, *refs):
-    other_ref, mine_ref, last_ref, sems = refs
-    copies = copied([(p4_ref, last_ref.at[0]), (f4_ref, last_ref.at[1])], sems)
-    z = where_ref[2]
-    turned = [
-        lambda y: pieces_of(b_rows.ready(), y, 2, z),
-        lambda y: pieces_of(g_rows.ready(), y, 2, z),
-        lambda y: f3_rows.ready()[y].T,
-    ]
+def third_terms(flip, where_ref, b_ref, g_ref, b_rows, g_rows, f3_rows, f3, out_ref):
+    x, half, z = where_ref[0], where_ref[1] ^ flip, where_ref[2]
     factors = [split(b_ref[...]), split(g_ref[...]), split(f3.ready()[...])]
-    share_terms(where_ref, 2, turned, factors, other_ref, mine_ref)
-    for copy in copies:
-        copy.wait()
+    for i in range(2):
+        y = 2 * i + half
+        turned = [
+            pieces_of(b_rows.ready(), y, 2, z),
+            pieces_of(g_rows.ready(), y, 2, z),
+            f3_rows.ready()[y].T,
+        ]
+        total = sum(product(split(t), factor) for t, factor in zip(turned, factors))
+        for plane in range(2):
+            out_ref[(plane * 2 + i - x) % XS] = total[plane * 176 : plane * 176 + 176]
 
 
 def early_terms(where_ref, f1_rows, f1, a, a_rows, f2_rows, f2, b, g, out_ref):
@@ -213,22 +185,34 @@
         at += out_ref.shape[1]
 
 
-def last_terms(where_ref, parent, columns, p_rows, f_rows, own, *refs):
-    cross_ref, other_ref, mine_ref = refs
-    count = cross_ref.shape[1]
-
+def last_half(flip, where_ref, p_rows, f_rows, factors, out_ref):
+    x, half = where_ref[0], where_ref[1] ^ flip
+    for y in range(Y):
+        total = 0.0
+        for rows, factor in zip((p_rows, f_rows), factors):
+            tile = rows.ready()[y]
+            tile = jnp.where(half == 0, tile[:, :176], tile[:, 176:])
+            total += product(split(tile.T), factor)
+        out_ref[(y - x) % XS] = total
+
+
+def last_other(where_ref, parent, columns, p_rows, f_rows, own, cross_ref, other_ref):
     def left(y):
         return parent.ready()[2 * y : 2 * y + 2].reshape(352, 176).T
 
+    count = cross_ref.shape[1]
     total = times_columns(1, where_ref[2] % 2, left, columns.ready(), count)
     cross_ref[...] = -total
-    turned = [lambda y: p_rows.ready()[y].T, lambda y: f_rows.ready()[y].T]
     factors = [split(total), split(own.ready()[...])]
-    share_terms(where_ref, 1, turned, factors, other_ref, mine_ref)
-
-
-def add_pieces(mine, got_ref, *out_refs):
-    mine_ref = mine.ready()
+    last_half(1, where_ref, p_rows, f_rows, factors, other_ref)
+
+
+def last_mine(where_ref, cross_ref, p_rows, f_rows, own, mine_ref):
+    factors = [split(-cross_ref[...]), split(own.ready()[...])]
+    last_half(0, where_ref, p_rows, f_rows, factors, mine_ref)
+
+
+def add_pieces(mine_ref, got_ref, *out_refs):
     for step, out_ref in enumerate(out_refs):
         out_ref[...] = mine_ref[step] + got_ref[step]
 
@@ -333,7 +317,7 @@
     def front_total(other, mine):
         got = from_core(other)
         piece = stack(mine.shape[1:])
-        pieces = call(add_pieces, [piece] * XS, 1_000_000, staged(mine), near_by(got))
+        pieces = call(add_pieces, [piece] * XS, 1_000_000, near_by(mine), near_by(got))
         parts = [pieces[0]] + [shift_x(pieces[d], d) for d in (1, 3, 2)]
         outs = [piece, stack(piece.shape[::-1])]
         outs = call(finish, outs, 1_000_000, *[near_by(part) for part in parts])
@@ -383,16 +367,14 @@
 
     work = 6 * share * share * XS * width
     count = panel_two.shape[1]
-    inner, turned, p4 = call(
+    inner, turned = call(
         top_product,
-        [stack((share, count)), stack((count, share)), tile],
+        [stack((share, count)), stack((count, share))],
         work // 4,
         staged(f1_rows),
         staged(panels, *lanes, slice(256, 384)),
-        in_hbm(panel_four),
-        hbm_outs=(2,),
-        semaphores=1,
-    )
+    )
+    p4, inner = lax.optimization_barrier((panel_four, inner))
     last_panel = lax.all_gather(p4, "front", axis=0)
     a_rows = plane_gather([turned] + [from_plane(turned, d) for d in (2, 1, 3)])
     b, g, turned = call(
@@ -404,14 +386,13 @@
         staged(rows, slice(None), 0),
         staged(panels, *lanes, slice(0, 256)),
     )
+    last, b = lax.optimization_barrier((jnp.stack([panel_four, factor_four]), b))
+    last_rows = y_gather(last)
     got = from_plane(turned, 1)
     b_rows, g_rows = (plane_gather([turned[i], got[i]]) for i in range(2))
 
     half_sums = stack((XS, share, share))
-    other, mine, last = call(
-        third_terms,
-        [half_sums, half_sums, stack((2, share, width))],
-        2 * work,
+    third = [
         where,
         near_by(b),
         near_by(g),
@@ -419,12 +400,11 @@
         staged(g_rows),
         staged(rows, slice(None), 1),
         staged(factor_three),
-        in_hbm(panel_four),
-        in_hbm(factor_four),
-        hbm_outs=(2,),
-        semaphores=2,
-    )
-    last_rows = y_gather(last)
+    ]
+    other, mine = (
+        call(functools.partial(third_terms, flip), [half_sums], work, *third)[0]
+        for flip in (1, 0)
+    )
     cov_three, turned = front_total(other, mine)
 
     widths = [top_factor.shape[1], count, count, share]
@@ -449,17 +429,21 @@
     cov_one, cross_two, cov_two, cross_three = call(cut, cuts, 1_000_000, near_by(early))
 
     parent_rows = plane_gather([turned, from_plane(turned, 1)])
-    cross_four, other, mine = call(
-        last_terms,
-        [tile, tiles, tiles],
-        4 * work,
+    last = [
+        staged(last_rows, slice(None), 0),
+        staged(last_rows, slice(None), 1),
+        staged(factor_four),
+    ]
+    cross_four, other = call(
+        last_other,
+        [tile, tiles],
+        2 * work,
         where,
         staged(parent_rows),
         staged(last_panel),
-        staged(last_rows, slice(None), 0),
-        staged(last_rows, slice(None), 1),
-        staged(factor_four),
-    )
+        *last,
+    )
+    (mine,) = call(last_mine, [tiles], work, where, near_by(cross_four), *last)
     cov_four, _ = front_total(other, mine)
     return cov_one.T, cross_two, cov_two, cross_three, cov_three, cross_four, cov_four
 

time: 266 us -> 255 us (0.959); the launches traced: 262 us -> 254 us
  waiting for transfers between devices: 54.4 us -> 48.7 us
  blocking collectives: 88.4 us -> 85.2 us
    ppermute x2, waiting for transfers between devices: 5.04 us -> 0.01 us  [from_core(): return lax.ppermute(value, 'front', [(i, i ^ 1) for i in range(fronts)])]
    all_gather x5, blocking collectives: 88.4 us -> 85.2 us  [y_gather(): return lax.all_gather(value, 'leaf', axis=0, axis_index_groups=y_groups)]
    ppermute x6, waiting for transfers between devices: 15.8 us -> 12.7 us  [shift_x(): return lax.ppermute(value, 'front', pairs)]
    unnamed x24 -> x26, local copies, waits for them, and re-layouts: 6.58 us -> 7.44 us
    pallas_call x13 -> x15, Pallas kernels: 39.1 us -> 39.5 us  [call(): pl.pallas_call(body, out_shape=out_shape, grid=(1,), in_specs=specs, out_...]
  transfers between devices with their start and end apart: 21 -> 21, of which waited for: 12 -> 9; matrix products, arithmetic and copies ran while one was open for 0% -> 0% of each run, Pallas kernels for 14% -> 14%
where the time goes in v6:
time: 255 us; the launch traced here: 254 us
  blocking collectives  85.2 us (33%)
  starting transfers between devices  56.4 us (22%)
  waiting for transfers between devices  48.7 us (19%)
  Pallas kernels  39.5 us (15%)
  between operations  14.2 us (6%)
  local copies, waits for them, and re-layouts  7.49 us (3%)
  other arithmetic  2.75 us (1%)
    all_gather x5, blocking collectives, y_gather(): return lax.all_gather(value, 'leaf', axis=0, axis_index_groups=y_groups)  85.2 us
    pallas_call x15, Pallas kernels, call(): pl.pallas_call(body, out_shape=out_shape, grid=(1,), in_specs=specs, out_...  39.5 us
    ppermute x8, waiting for transfers between devices, from_plane(): return lax.ppermute(value, 'leaf', pairs)  35.8 us
    ppermute x8, starting transfers between devices, from_plane(): return lax.ppermute(value, 'leaf', pairs)  33.3 us
    ppermute x6, starting transfers between devices, shift_x(): return lax.ppermute(value, 'front', pairs)  19.1 us
    ppermute x6, waiting for transfers between devices, shift_x(): return lax.ppermute(value, 'front', pairs)  12.7 us
    unnamed x26, local copies, waits for them, and re-layouts  7.44 us
  transfers between devices with their start and end apart: 21, of which 9 were waited for; matrix products, arithmetic and copies ran while one was open for 0% of the time, Pallas kernels for 14%

profile of v6, /device:TPU:6, one launch (start us, length us, event | category | flops | bytes accessed | tf_op | source)
XLA Modules:
  0.0 254.4 jit_solution(3852533981257223043)
XLA Ops:
  7.2 0.0 all-gather.14.cloned.1.call-start
  7.2 1.7 select_maximum_fusion
  8.9 0.0 all-gather.16.cloned.1.call-start
  9.0 9.1 %collective-permute-start = (f32[44,176]{1,0:T(8,128)}, f32[44,176]{1,0:T(8,128)S(1)}, u32[]{:S(2)}, u32[]{:S(2)}) collective-permute-start(f32[44,176]{1,0:T(8,128)} %bitcast.22), channel_id=1, source_target_pairs={{0,128},{8,136},{16,144},{24,152},{32,160},{40,168},{48,176},{56,1... | collective-permute-start | bytes 92936 | tf_op jit(solution)/shard_map/ppermute | solution.py:240
  18.1 2.3 collective-permute-done.refs_2_
  20.4 0.9 copy-done.5
  21.3 0.8 copy-done.8
  22.0 0.3 shard_map.126.refs_0_
  22.4 5.4 %collective-permute-start.1 = (f32[88,352]{1,0:T(8,128)S(1)}, f32[88,352]{1,0:T(8,128)S(1)}, u32[]{:S(2)}, u32[]{:S(2)}) collective-permute-start(f32[88,352]{1,0:T(8,128)S(1)} %shard_map.126.refs_0_), channel_id=1, source_target_pairs={{0,64},{8,72},{16,80},{24,88},{32,96},{40,104},{48,112},{56,120},{... | collective-permute-start | bytes 371720 | tf_op jit(solution)/shard_map/ppermute | solution.py:240
  27.8 6.6 %collective-permute-done.1.refs_1_ = f32[88,352]{1,0:T(8,128)S(1)} collective-permute-done((f32[88,352]{1,0:T(8,128)S(1)}, f32[88,352]{1,0:T(8,128)S(1)}, u32[]{:S(2)}, u32[]{:S(2)}) %collective-permute-start.1) | collective-permute-done | bytes 123936 | tf_op jit(solution)/shard_map/ppermute | solution.py:240
  34.5 0.9 copy-done.2
  35.4 0.4 shard_map.127.refs_1_
  35.8 2.6 %collective-permute-start.2 = (f32[88,1056]{1,0:T(8,128)S(1)}, f32[88,1056]{1,0:T(8,128)S(1)}, u32[]{:S(2)}, u32[]{:S(2)}) collective-permute-start(f32[88,1056]{1,0:T(8,128)S(1)} %shard_map.127.refs_1_), channel_id=1, source_target_pairs={{0,32},{8,40},{16,48},{24,56},{32,0},{40,8},{48,16},{56,24},{64,96... | collective-permute-start | bytes 1115144 | tf_op jit(solution)/shard_map/ppermute | solution.py:240
  38.5 0.1 pad_add_fusion.refs_0_
  38.6 9.9 %collective-permute-done.2.refs_2_ = f32[88,1056]{1,0:T(8,128)S(1)} collective-permute-done((f32[88,1056]{1,0:T(8,128)S(1)}, f32[88,1056]{1,0:T(8,128)S(1)}, u32[]{:S(2)}, u32[]{:S(2)}) %collective-permute-start.2) | collective-permute-done | bytes 371744 | tf_op jit(solution)/shard_map/ppermute | solution.py:240
  48.5 2.4 shard_map.128
  50.9 0.0 all-gather.16.cloned.1.call-update
  50.9 0.0 all-gather.18.cloned.1.call-start
  50.9 15.1 %all-gather.1 = f32[704,352]{1,0:T(8,128)S(1)} all-gather(f32[176,352]{1,0:T(8,128)S(1)} %get-tuple-element.37), channel_id=3, replica_groups={{0,8,16,24},{32,40,48,56},{64,72,80,88},{96,104,112,120},{128,136,144,1..., dimensions={0}, use_global_device_ids=true | all-gather | bytes 1239040 | tf_op jit(solution)/shard_map/all_gather | solution.py:252
  66.1 2.1 shard_map.129
  68.2 0.0 all-gather.18.cloned.1.call-update
  68.2 0.0 all-gather.20.cloned.1.call-start
  68.3 4.9 %collective-permute-start.3 = (f32[88,176]{1,0:T(8,128)S(1)}, f32[88,176]{1,0:T(8,128)S(1)}, u32[]{:S(2)}, u32[]{:S(2)}) collective-permute-start(f32[88,176]{1,0:T(8,128)S(1)} %get-tuple-element.40), channel_id=1, source_target_pairs={{0,64},{8,72},{16,80},{24,88},{32,96},{40,104},{48,112},{56,120},{... | collective-permute-start | bytes 185864 | tf_op jit(solution)/shard_map/ppermute | solution.py:240
  73.1 3.9 %collective-permute-start.4 = (f32[88,176]{1,0:T(8,128)S(1)}, f32[88,176]{1,0:T(8,128)S(1)}, u32[]{:S(2)}, u32[]{:S(2)}) collective-permute-start(f32[88,176]{1,0:T(8,128)S(1)} %get-tuple-element.40), channel_id=1, source_target_pairs={{0,32},{8,40},{16,48},{24,56},{32,0},{40,8},{48,16},{56,24},{64,96... | collective-permute-start | bytes 185864 | tf_op jit(solution)/shard_map/ppermute | solution.py:240
  77.0 1.9 collective-permute-start.5
  79.0 0.9 pad_maximum_fusion
  79.9 5.4 %collective-permute-done.5 = f32[88,176]{1,0:T(8,128)S(1)} collective-permute-done((f32[88,176]{1,0:T(8,128)S(1)}, f32[88,176]{1,0:T(8,128)S(1)}, u32[]{:S(2)}, u32[]{:S(2)}) %collective-permute-start.5) | collective-permute-done | bytes 61984 | tf_op jit(solution)/shard_map/ppermute | solution.py:240
  85.3 18.8 %all-gather.2.refs_1_.refs_4_ = f32[16,88,176]{2,1,0:T(8,128)} all-gather(f32[4,88,176]{2,1,0:T(8,128)S(1)} %pad_maximum_fusion.1), channel_id=4, replica_groups={{0,8,16,24},{32,40,48,56},{64,72,80,88},{96,104,112,120},{128,136,144,1..., dimensions={0}, use_global_device_ids=true | all-gather | bytes 1239040 | tf_op jit(solution)/shard_map/all_gather | solution.py:252
  104.1 4.1 %shard_map.130 = (f32[176,176]{1,0:T(8,128)S(1)}, f32[176,176]{1,0:T(8,128)S(1)}, f32[2,176,176]{2,1,0:T(8,128)S(1)}) custom-call(s32[3]{0:T(128)S(1)} %pad_add_fusion.refs_0_, f32[16,88,176]{2,1,0:T(8,128)} %all-gather.2.refs_1_.refs_4_, f32[4,2,176,352]{3,2,1,0:T(8,128)} %bitcast.31, f32[8,176,384]{2,1,0:T(8,128)} %bitcast.37), custom_call_target="tpu_custom_call" | custom-call | flops 261685248 | bytes 8000000 | tf_op jit(solution)/shard_map/pallas_call | solution.py:304
  108.3 0.0 reduce-scatter.2.cloned.1.call-start
  108.3 2.8 %collective-permute-start.6 = (f32[2,176,176]{2,1,0:T(8,128)S(1)}, f32[2,176,176]{2,1,0:T(8,128)S(1)}, u32[]{:S(2)}, u32[]{:S(2)}) collective-permute-start(f32[2,176,176]{2,1,0:T(8,128)S(1)} %get-tuple-element.45), channel_id=1, source_target_pairs={{0,32},{8,40},{16,48},{24,56},{32,0},{40,8},{48,16},{56,24},{64,96... | collective-permute-start | bytes 743432 | tf_op jit(solution)/shard_map/ppermute | solution.py:240
  111.2 6.4 %collective-permute-done.6 = f32[2,176,176]{2,1,0:T(8,128)S(1)} collective-permute-done((f32[2,176,176]{2,1,0:T(8,128)S(1)}, f32[2,176,176]{2,1,0:T(8,128)S(1)}, u32[]{:S(2)}, u32[]{:S(2)}) %collective-permute-start.6) | collective-permute-done | bytes 247840 | tf_op jit(solution)/shard_map/ppermute | solution.py:240
  117.7 17.8 %all-gather.5.refs_4_ = f32[8,176,176]{2,1,0:T(8,128)} all-gather(f32[2,176,176]{2,1,0:T(8,128)S(1)} %pad_maximum_fusion.3), channel_id=7, replica_groups={{0,8,16,24},{32,40,48,56},{64,72,80,88},{96,104,112,120},{128,136,144,1..., dimensions={0}, use_global_device_ids=true | all-gather | bytes 1239040 | tf_op jit(solution)/shard_map/all_gather | solution.py:252
  135.5 15.8 %all-gather.4.refs_3_ = f32[8,176,176]{2,1,0:T(8,128)} all-gather(f32[2,176,176]{2,1,0:T(8,128)S(1)} %pad_maximum_fusion.2), channel_id=6, replica_groups={{0,8,16,24},{32,40,48,56},{64,72,80,88},{96,104,112,120},{128,136,144,1..., dimensions={0}, use_global_device_ids=true | all-gather | bytes 1239040 | tf_op jit(solution)/shard_map/all_gather | solution.py:252
  151.4 3.9 %shard_map.133 = f32[4,176,176]{2,1,0:T(8,128)S(1)} custom-call(s32[3]{0:T(128)S(1)} %pad_add_fusion.refs_0_, f32[176,176]{1,0:T(8,128)S(1)} %get-tuple-element.43.refs_7_.refs_1_, f32[176,176]{1,0:T(8,128)S(1)} %get-tuple-element.44.refs_8_.refs_2_, f32[8,176,176]{2,1,0:T(8,128)} %all-gather.4.refs_3_, f32[8,176,176]{2,1,0:T(8,128)} %all-gather.5.refs_4_, ...), custom_call_target="tpu_custom_call" | custom-call | flops 261685248 | bytes 8000000 | tf_op jit(solution)/shard_map/pallas_call | solution.py:304
  155.3 1.9 collective-permute-start.7
  157.3 3.8 %shard_map.132.refs_0_ = f32[4,176,176]{2,1,0:T(8,128)S(1)} custom-call(s32[3]{0:T(128)S(1)} %pad_add_fusion.refs_0_, f32[176,176]{1,0:T(8,128)S(1)} %get-tuple-element.43.refs_7_.refs_1_, f32[176,176]{1,0:T(8,128)S(1)} %get-tuple-element.44.refs_8_.refs_2_, f32[8,176,176]{2,1,0:T(8,128)} %all-gather.4.refs_3_, f32[8,176,176]{2,1,0:T(8,128)} %all-gather.5.refs_4_, ...), custom_call_target="tpu_custom_call" | custom-call | flops 261685248 | bytes 8000000 | tf_op jit(solution)/shard_map/pallas_call | solution.py:304
  161.1 0.9 copy-done.12
  162.0 1.2 shard_map.134
  163.2 3.5 %collective-permute-start.10 = (f32[176,176]{1,0:T(8,128)S(1)}, f32[176,176]{1,0:T(8,128)S(1)}, u32[]{:S(2)}, u32[]{:S(2)}) collective-permute-start(f32[176,176]{1,0:T(8,128)S(1)} %get-tuple-element.49), channel_id=1, source_target_pairs={{0,4},{1,5},{2,6},{3,7},{4,0},{5,1},{6,2},{7,3},{8,12},{9,13},{10,... | collective-permute-start | bytes 371720 | tf_op jit(solution)/shard_map/ppermute | solution.py:249
  166.6 3.9 %collective-permute-start.8 = (f32[176,176]{1,0:T(8,128)S(1)}, f32[176,176]{1,0:T(8,128)S(1)}, u32[]{:S(2)}, u32[]{:S(2)}) collective-permute-start(f32[176,176]{1,0:T(8,128)S(1)} %get-tuple-element.47), channel_id=1, source_target_pairs={{0,2},{1,3},{2,4},{3,5},{4,6},{5,7},{6,0},{7,1},{8,10},{9,11},{10,... | collective-permute-start | bytes 371720 | tf_op jit(solution)/shard_map/ppermute | solution.py:249
  170.6 1.9 collective-permute-start.9
  172.5 6.9 %shard_map.131 = f32[8,176,396]{2,1,0:T(8,128)} custom-call(s32[3]{0:T(128)S(1)} %pad_add_fusion.refs_0_, f32[4,176,352]{2,1,0:T(8,128)S(1)} %bitcast.20, f32[44,176]{1,0:T(8,128)S(1)} %bitcast.24, f32[176,88]{1,0:T(8,128)S(1)} %get-tuple-element.39.refs_3_, f32[16,88,176]{2,1,0:T(8,128)} %all-gather.2.refs_1_.refs_4_, f32[4,2,176,352]{3,2,1,0:T(8,128)} %bitcast.34, ...), custom_call_target="tpu_custom_call" | custom-call | flops 523370496 | bytes 8000000 | tf_op jit(solution)/shard_map/pallas_call | solution.py:304
  179.5 0.6 collective-permute-done.9.refs_2_
  180.1 0.7 shard_map.135
  180.9 2.6 %collective-permute-start.11 = (f32[176,176]{1,0:T(8,128)S(1)}, f32[176,176]{1,0:T(8,128)S(1)}, u32[]{:S(2)}, u32[]{:S(2)}) collective-permute-start(f32[176,176]{1,0:T(8,128)S(1)} %get-tuple-element.57), channel_id=1, source_target_pairs={{0,32},{8,40},{16,48},{24,56},{32,0},{40,8},{48,16},{56,24},{64,96... | collective-permute-start | bytes 371720 | tf_op jit(solution)/shard_map/ppermute | solution.py:240
  183.4 5.1 %collective-permute-done.11 = f32[176,176]{1,0:T(8,128)S(1)} collective-permute-done((f32[176,176]{1,0:T(8,128)S(1)}, f32[176,176]{1,0:T(8,128)S(1)}, u32[]{:S(2)}, u32[]{:S(2)}) %collective-permute-start.11) | collective-permute-done | bytes 123936 | tf_op jit(solution)/shard_map/ppermute | solution.py:240
  188.6 17.7 %all-gather.6.refs_1_ = f32[8,176,176]{2,1,0:T(8,128)} all-gather(f32[2,176,176]{2,1,0:T(8,128)S(1)} %pad_maximum_fusion.4), channel_id=8, replica_groups={{0,8,16,24},{32,40,48,56},{64,72,80,88},{96,104,112,120},{128,136,144,1..., dimensions={0}, use_global_device_ids=true | all-gather | bytes 1239040 | tf_op jit(solution)/shard_map/all_gather | solution.py:252
  206.3 6.2 %shard_map.137 = (f32[176,352]{1,0:T(8,128)}, f32[4,176,352]{2,1,0:T(8,128)S(1)}) custom-call(s32[3]{0:T(128)S(1)} %pad_add_fusion.refs_0_, f32[8,176,176]{2,1,0:T(8,128)} %all-gather.6.refs_1_, f32[8,176,352]{2,1,0:T(8,128)} %bitcast.39, f32[4,2,176,352]{3,2,1,0:T(8,128)} %bitcast.27, f32[4,2,176,352]{3,2,1,0:T(8,128)} %bitcast.28, f32[176,352]{1,0:T(8,128)S(1)} %copy-done.1), custom_call_target="tpu_custom_call" | custom-call | flops 523370496 | bytes 8000000 | tf_op jit(solution)/shard_map/pallas_call | solution.py:304
  212.5 1.9 collective-permute-start.12
  214.4 0.9 copy-done.7
  215.4 3.9 %shard_map.138.refs_0_ = f32[4,176,352]{2,1,0:T(8,128)S(1)} custom-call(s32[3]{0:T(128)S(1)} %pad_add_fusion.refs_0_, f32[176,352]{1,0:T(8,128)S(1)} %copy-done.7, f32[4,2,176,352]{3,2,1,0:T(8,128)} %bitcast.29, f32[4,2,176,352]{3,2,1,0:T(8,128)} %bitcast.30, f32[176,352]{1,0:T(8,128)S(1)} %copy-done.1), custom_call_target="tpu_custom_call" | custom-call | flops 261685248 | bytes 8000000 | tf_op jit(solution)/shard_map/pallas_call | solution.py:304
  219.3 1.0 copy-done
  220.2 1.0 copy-done.10
  221.3 1.7 shard_map.139
  222.9 4.5 %collective-permute-start.13 = (f32[176,352]{1,0:T(8,128)S(1)}, f32[176,352]{1,0:T(8,128)S(1)}, u32[]{:S(2)}, u32[]{:S(2)}) collective-permute-start(f32[176,352]{1,0:T(8,128)S(1)} %get-tuple-element.63), channel_id=1, source_target_pairs={{0,2},{1,3},{2,4},{3,5},{4,6},{5,7},{6,0},{7,1},{8,10},{9,11},{10,... | collective-permute-start | bytes 743432 | tf_op jit(solution)/shard_map/ppermute | solution.py:249
  227.4 1.9 collective-permute-start.14
  229.4 3.4 %collective-permute-start.15 = (f32[176,352]{1,0:T(8,128)S(1)}, f32[176,352]{1,0:T(8,128)S(1)}, u32[]{:S(2)}, u32[]{:S(2)}) collective-permute-start(f32[176,352]{1,0:T(8,128)S(1)} %get-tuple-element.65), channel_id=1, source_target_pairs={{0,4},{1,5},{2,6},{3,7},{4,0},{5,1},{6,2},{7,3},{8,12},{9,13},{10,... | collective-permute-start | bytes 743432 | tf_op jit(solution)/shard_map/ppermute | solution.py:249
  232.7 1.0 collective-permute-done.13.refs_1_
  233.8 11.1 %collective-permute-done.14.refs_2_ = f32[176,352]{1,0:T(8,128)S(1)} collective-permute-done((f32[176,352]{1,0:T(8,128)S(1)}, f32[176,352]{1,0:T(8,128)S(1)}, u32[]{:S(2)}, u32[]{:S(2)}) %collective-permute-start.14) | collective-permute-done | bytes 247840 | tf_op jit(solution)/shard_map/ppermute | solution.py:249
  244.9 0.9 shard_map.140
  245.9 0.0 reduce-scatter.2.cloned.1.call-done.refs_0_
  245.9 1.0 copy-done.4
  246.9 0.9 shard_map.136
  (38 shorter events, 0.3 us)
Async XLA Ops:
  7.2 41.3 %all-gather.14.cloned.1.call-start = ((), (), s32[]{:S(2)}) async-start(), calls=%async_computation.2 | async-start | bytes 2433024 | tf_op jit(solution)/shard_map/all_gather | solution.py:334
  8.9 95.2 %all-gather.16.cloned.1.call-start = ((), (), s32[]{:S(2)}) async-start(), calls=%async_computation.3 | async-start | bytes 2703360 | tf_op jit(solution)/shard_map/all_gather | solution.py:252
  9.0 11.4 %collective-permute-start = (f32[44,176]{1,0:T(8,128)}, f32[44,176]{1,0:T(8,128)S(1)}, u32[]{:S(2)}, u32[]{:S(2)}) collective-permute-start(f32[44,176]{1,0:T(8,128)} %bitcast.22), channel_id=1, source_target_pairs={{0,128},{8,136},{16,144},{24,152},{32,160},{40,168},{48,176},{56,1... | collective-permute-start | bytes 92936 | tf_op jit(solution)/shard_map/ppermute | solution.py:240
  20.4 0.9 copy-start.5
  21.2 0.8 copy-start.8
  22.4 12.1 %collective-permute-start.1 = (f32[88,352]{1,0:T(8,128)S(1)}, f32[88,352]{1,0:T(8,128)S(1)}, u32[]{:S(2)}, u32[]{:S(2)}) collective-permute-start(f32[88,352]{1,0:T(8,128)S(1)} %shard_map.126.refs_0_), channel_id=1, source_target_pairs={{0,64},{8,72},{16,80},{24,88},{32,96},{40,104},{48,112},{56,120},{... | collective-permute-start | bytes 371720 | tf_op jit(solution)/shard_map/ppermute | solution.py:240
  34.4 0.9 copy-start.2
  35.8 12.7 %collective-permute-start.2 = (f32[88,1056]{1,0:T(8,128)S(1)}, f32[88,1056]{1,0:T(8,128)S(1)}, u32[]{:S(2)}, u32[]{:S(2)}) collective-permute-start(f32[88,1056]{1,0:T(8,128)S(1)} %shard_map.127.refs_1_), channel_id=1, source_target_pairs={{0,32},{8,40},{16,48},{24,56},{32,0},{40,8},{48,16},{56,24},{64,96... | collective-permute-start | bytes 1115144 | tf_op jit(solution)/shard_map/ppermute | solution.py:240
  50.9 155.4 %all-gather.18.cloned.1.call-start = ((), (), s32[]{:S(2)}) async-start(), calls=%async_computation.4 | async-start | bytes 2433024 | tf_op jit(solution)/shard_map/all_gather | solution.py:378
  66.1 12.9 %copy-start.1 = (f32[176,352]{1,0:T(8,128)S(1)}, f32[176,352]{1,0:T(8,128)}, u32[]{:S(2)}) copy-start(f32[176,352]{1,0:T(8,128)} %refs_4_.1) | copy-start | bytes 743428
  66.1 12.9 %copy-start.11 = (f32[176,352]{1,0:T(8,128)S(1)}, f32[176,352]{1,0:T(8,128)}, u32[]{:S(2)}) copy-start(f32[176,352]{1,0:T(8,128)} %param.10) | copy-start | bytes 743428
  68.2 138.1 %all-gather.20.cloned.1.call-start = ((), (), s32[]{:S(2)}) async-start(), calls=%async_computation.5 | async-start | bytes 2703360 | tf_op jit(solution)/shard_map/all_gather | solution.py:252
  68.3 11.6 %collective-permute-start.3 = (f32[88,176]{1,0:T(8,128)S(1)}, f32[88,176]{1,0:T(8,128)S(1)}, u32[]{:S(2)}, u32[]{:S(2)}) collective-permute-start(f32[88,176]{1,0:T(8,128)S(1)} %get-tuple-element.40), channel_id=1, source_target_pairs={{0,64},{8,72},{16,80},{24,88},{32,96},{40,104},{48,112},{56,120},{... | collective-permute-start | bytes 185864 | tf_op jit(solution)/shard_map/ppermute | solution.py:240
  73.1 6.8 %collective-permute-start.4 = (f32[88,176]{1,0:T(8,128)S(1)}, f32[88,176]{1,0:T(8,128)S(1)}, u32[]{:S(2)}, u32[]{:S(2)}) collective-permute-start(f32[88,176]{1,0:T(8,128)S(1)} %get-tuple-element.40), channel_id=1, source_target_pairs={{0,32},{8,40},{16,48},{24,56},{32,0},{40,8},{48,16},{56,24},{64,96... | collective-permute-start | bytes 185864 | tf_op jit(solution)/shard_map/ppermute | solution.py:240
  77.0 8.2 %collective-permute-start.5 = (f32[88,176]{1,0:T(8,128)S(1)}, f32[88,176]{1,0:T(8,128)S(1)}, u32[]{:S(2)}, u32[]{:S(2)}) collective-permute-start(f32[88,176]{1,0:T(8,128)S(1)} %get-tuple-element.40), channel_id=1, source_target_pairs={{0,96},{8,104},{16,112},{24,120},{32,64},{40,72},{48,80},{56,88},{... | collective-permute-start | bytes 185864 | tf_op jit(solution)/shard_map/ppermute | solution.py:240
  108.3 137.6 %reduce-scatter.2.cloned.1.call-start = ((), (), s32[]{:S(2)}) async-start(), calls=%async_computation.1 | async-start | bytes 3244032 | tf_op jit(solution)/shard_map/reduce_scatter | solution.py:427
  108.3 9.3 %collective-permute-start.6 = (f32[2,176,176]{2,1,0:T(8,128)S(1)}, f32[2,176,176]{2,1,0:T(8,128)S(1)}, u32[]{:S(2)}, u32[]{:S(2)}) collective-permute-start(f32[2,176,176]{2,1,0:T(8,128)S(1)} %get-tuple-element.45), channel_id=1, source_target_pairs={{0,32},{8,40},{16,48},{24,56},{32,0},{40,8},{48,16},{56,24},{64,96... | collective-permute-start | bytes 743432 | tf_op jit(solution)/shard_map/ppermute | solution.py:240
  117.7 33.7 %copy-start.3 = (f32[176,176]{1,0:T(8,128)S(1)}, f32[176,176]{1,0:T(8,128)}, u32[]{:S(2)}) copy-start(f32[176,176]{1,0:T(8,128)} %refs_6_.5) | copy-start | bytes 371716
  155.3 5.7 %collective-permute-start.7 = (f32[4,176,176]{2,1,0:T(8,128)S(1)}, f32[4,176,176]{2,1,0:T(8,128)S(1)}, u32[]{:S(2)}, u32[]{:S(2)}) collective-permute-start(f32[4,176,176]{2,1,0:T(8,128)S(1)} %shard_map.133), channel_id=1, source_target_pairs={{0,1},{1,0},{2,3},{3,2},{4,5},{5,4},{6,7},{7,6},{8,9},{9,8},{10,11... | collective-permute-start | bytes 1486856 | tf_op jit(solution)/shard_map/ppermute | solution.py:243
  161.0 11.5 %copy-start.6 = (f32[176,88]{1,0:T(8,128)S(1)}, f32[176,88]{1,0:T(8,128)}, u32[]{:S(2)}) copy-start(f32[176,88]{1,0:T(8,128)} %refs_6_.3) | copy-start | bytes 185860
  161.0 11.5 %copy-start.9 = (f32[176,44]{0,1:T(8,128)S(1)}, f32[176,44]{0,1:T(8,128)}, u32[]{:S(2)}) copy-start(f32[176,44]{0,1:T(8,128)} %param.7) | copy-start | bytes 92932
  161.1 0.9 copy-start.12
  163.2 16.3 %collective-permute-start.10 = (f32[176,176]{1,0:T(8,128)S(1)}, f32[176,176]{1,0:T(8,128)S(1)}, u32[]{:S(2)}, u32[]{:S(2)}) collective-permute-start(f32[176,176]{1,0:T(8,128)S(1)} %get-tuple-element.49), channel_id=1, source_target_pairs={{0,4},{1,5},{2,6},{3,7},{4,0},{5,1},{6,2},{7,3},{8,12},{9,13},{10,... | collective-permute-start | bytes 371720 | tf_op jit(solution)/shard_map/ppermute | solution.py:249
  166.6 12.9 %collective-permute-start.8 = (f32[176,176]{1,0:T(8,128)S(1)}, f32[176,176]{1,0:T(8,128)S(1)}, u32[]{:S(2)}, u32[]{:S(2)}) collective-permute-start(f32[176,176]{1,0:T(8,128)S(1)} %get-tuple-element.47), channel_id=1, source_target_pairs={{0,2},{1,3},{2,4},{3,5},{4,6},{5,7},{6,0},{7,1},{8,10},{9,11},{10,... | collective-permute-start | bytes 371720 | tf_op jit(solution)/shard_map/ppermute | solution.py:249
  170.6 9.5 %collective-permute-start.9 = (f32[176,176]{1,0:T(8,128)S(1)}, f32[176,176]{1,0:T(8,128)S(1)}, u32[]{:S(2)}, u32[]{:S(2)}) collective-permute-start(f32[176,176]{1,0:T(8,128)S(1)} %get-tuple-element.48), channel_id=1, source_target_pairs={{0,6},{1,7},{2,0},{3,1},{4,2},{5,3},{6,4},{7,5},{8,14},{9,15},{10,... | collective-permute-start | bytes 371720 | tf_op jit(solution)/shard_map/ppermute | solution.py:249
  180.9 7.7 %collective-permute-start.11 = (f32[176,176]{1,0:T(8,128)S(1)}, f32[176,176]{1,0:T(8,128)S(1)}, u32[]{:S(2)}, u32[]{:S(2)}) collective-permute-start(f32[176,176]{1,0:T(8,128)S(1)} %get-tuple-element.57), channel_id=1, source_target_pairs={{0,32},{8,40},{16,48},{24,56},{32,0},{40,8},{48,16},{56,24},{64,96... | collective-permute-start | bytes 371720 | tf_op jit(solution)/shard_map/ppermute | solution.py:240
  212.5 7.8 %collective-permute-start.12 = (f32[4,176,352]{2,1,0:T(8,128)S(1)}, f32[4,176,352]{2,1,0:T(8,128)S(1)}, u32[]{:S(2)}, u32[]{:S(2)}) collective-permute-start(f32[4,176,352]{2,1,0:T(8,128)S(1)} %get-tuple-element.61), channel_id=1, source_target_pairs={{0,1},{1,0},{2,3},{3,2},{4,5},{5,4},{6,7},{7,6},{8,9},{9,8},{10,11... | collective-permute-start | bytes 2973704 | tf_op jit(solution)/shard_map/ppermute | solution.py:243
  214.4 1.0 copy-start.7
  219.2 1.0 copy-start
  220.2 1.0 copy-start.10
  222.9 10.8 %collective-permute-start.13 = (f32[176,352]{1,0:T(8,128)S(1)}, f32[176,352]{1,0:T(8,128)S(1)}, u32[]{:S(2)}, u32[]{:S(2)}) collective-permute-start(f32[176,352]{1,0:T(8,128)S(1)} %get-tuple-element.63), channel_id=1, source_target_pairs={{0,2},{1,3},{2,4},{3,5},{4,6},{5,7},{6,0},{7,1},{8,10},{9,11},{10,... | collective-permute-start | bytes 743432 | tf_op jit(solution)/shard_map/ppermute | solution.py:249
  227.4 17.5 %collective-permute-start.14 = (f32[176,352]{1,0:T(8,128)S(1)}, f32[176,352]{1,0:T(8,128)S(1)}, u32[]{:S(2)}, u32[]{:S(2)}) collective-permute-start(f32[176,352]{1,0:T(8,128)S(1)} %get-tuple-element.64), channel_id=1, source_target_pairs={{0,6},{1,7},{2,0},{3,1},{4,2},{5,3},{6,4},{7,5},{8,14},{9,15},{10,... | collective-permute-start | bytes 743432 | tf_op jit(solution)/shard_map/ppermute | solution.py:249
  229.4 15.5 %collective-permute-start.15 = (f32[176,352]{1,0:T(8,128)S(1)}, f32[176,352]{1,0:T(8,128)S(1)}, u32[]{:S(2)}, u32[]{:S(2)}) collective-permute-start(f32[176,352]{1,0:T(8,128)S(1)} %get-tuple-element.65), channel_id=1, source_target_pairs={{0,4},{1,5},{2,6},{3,7},{4,0},{5,1},{6,2},{7,3},{8,12},{9,13},{10,... | collective-permute-start | bytes 743432 | tf_op jit(solution)/shard_map/ppermute | solution.py:249
  245.9 1.0 copy-start.4
Sparse Core Ops, SparseCore 0:
  10.7 36.2 all-gather.13
  51.0 42.3 all-gather.15
  95.5 35.8 all-gather.17
  133.4 40.5 all-gather.19
  181.0 39.0 reduce-scatter.1

commit v7 on v6

--- a/solution.py
+++ b/solution.py
@@ -11,6 +11,7 @@
 XS = 4
 CORES = 2
 VMEM_BYTES = 52 * 1024 * 1024
+VMEM_SMALL = 16 * 1024 * 1024
 
 
 class Staged:
@@ -277,6 +278,8 @@
             if kind == "staged":
                 scratch.append(pltpu.VMEM(rest[1].shape, rest[1].dtype))
         count = len(scratch)
+        near_only = all(kind in ("near", "smem") for kind, *_ in inputs)
+        limit = VMEM_SMALL if near_only else VMEM_BYTES
         scratch.append(pltpu.SemaphoreType.DMA((count + 1,)))
         if semaphores:
             scratch.append(pltpu.SemaphoreType.DMA((semaphores,)))
@@ -308,7 +311,7 @@
             in_specs=specs,
             out_specs=out_specs,
             scratch_shapes=scratch,
-            compiler_params=pltpu.CompilerParams(vmem_limit_bytes=VMEM_BYTES),
+            compiler_params=pltpu.CompilerParams(vmem_limit_bytes=limit),
             cost_estimate=pl.CostEstimate(
                 flops=flops, bytes_accessed=8_000_000, transcendentals=0
             ),

time: 255 us -> 250 us (0.980)
  local copies, waits for them, and re-layouts: 7.49 us -> 4.61 us
  Pallas kernels: 39.5 us -> 36.8 us
    unnamed x26 -> x20, local copies, waits for them, and re-layouts: 7.44 us -> 4.56 us
    pallas_call x15, Pallas kernels: 39.5 us -> 36.8 us  [call(): pl.pallas_call(body, out_shape=out_shape, grid=(1,), in_specs=specs, out_...]
  transfers between devices with their start and end apart: 21 -> 21, of which waited for: 9 -> 9; matrix products, arithmetic and copies ran while one was open for 0% -> 0% of each run, Pallas kernels for 14% -> 13%
where the time goes in v7:
time: 250 us; the launch traced here: 249 us
  blocking collectives  85.1 us (34%)
  starting transfers between devices  56.6 us (23%)
  waiting for transfers between devices  48.7 us (19%)
  Pallas kernels  36.8 us (15%)
  between operations  14.2 us (6%)
  local copies, waits for them, and re-layouts  4.61 us (2%)
  other arithmetic  2.73 us (1%)
    all_gather x5, blocking collectives, y_gather(): return lax.all_gather(value, 'leaf', axis=0, axis_index_groups=y_groups)  85.1 us
    pallas_call x15, Pallas kernels, call(): pl.pallas_call(body, out_shape=out_shape, grid=(1,), in_specs=specs, out_...  36.8 us
    ppermute x8, waiting for transfers between devices, from_plane(): return lax.ppermute(value, 'leaf', pairs)  35.8 us
    ppermute x8, starting transfers between devices, from_plane(): return lax.ppermute(value, 'leaf', pairs)  33.3 us
    ppermute x6, starting transfers between devices, shift_x(): return lax.ppermute(value, 'front', pairs)  19.3 us
    ppermute x6, waiting for transfers between devices, shift_x(): return lax.ppermute(value, 'front', pairs)  12.7 us
  transfers between devices with their start and end apart: 21, of which 9 were waited for; matrix products, arithmetic and copies ran while one was open for 0% of the time, Pallas kernels for 13%

profile of v7, /device:TPU:6, one launch (start us, length us, event | category | flops | bytes accessed | tf_op | source)
XLA Modules:
  0.0 248.8 jit_solution(1869839351137376847)
XLA Ops:
  7.2 0.0 all-gather.14.cloned.1.call-start
  7.2 1.7 select_maximum_fusion
  8.9 0.0 all-gather.14.cloned.1.call-update
  8.9 0.0 all-gather.16.cloned.1.call-start
  9.0 9.1 %collective-permute-start = (f32[44,176]{1,0:T(8,128)}, f32[44,176]{1,0:T(8,128)S(1)}, u32[]{:S(2)}, u32[]{:S(2)}) collective-permute-start(f32[44,176]{1,0:T(8,128)} %bitcast.22), channel_id=1, source_target_pairs={{0,128},{8,136},{16,144},{24,152},{32,160},{40,168},{48,176},{56,1... | collective-permute-start | bytes 92936 | tf_op jit(solution)/shard_map/ppermute | solution.py:241
  18.1 2.3 collective-permute-done.refs_2_
  20.4 0.9 copy-done.4
  21.3 0.8 copy-done.7
  22.0 0.3 shard_map.126.refs_0_
  22.4 5.4 %collective-permute-start.1 = (f32[88,352]{1,0:T(8,128)S(1)}, f32[88,352]{1,0:T(8,128)S(1)}, u32[]{:S(2)}, u32[]{:S(2)}) collective-permute-start(f32[88,352]{1,0:T(8,128)S(1)} %shard_map.126.refs_0_), channel_id=1, source_target_pairs={{0,64},{8,72},{16,80},{24,88},{32,96},{40,104},{48,112},{56,120},{... | collective-permute-start | bytes 371720 | tf_op jit(solution)/shard_map/ppermute | solution.py:241
  27.8 6.6 %collective-permute-done.1.refs_1_ = f32[88,352]{1,0:T(8,128)S(1)} collective-permute-done((f32[88,352]{1,0:T(8,128)S(1)}, f32[88,352]{1,0:T(8,128)S(1)}, u32[]{:S(2)}, u32[]{:S(2)}) %collective-permute-start.1) | collective-permute-done | bytes 123936 | tf_op jit(solution)/shard_map/ppermute | solution.py:241
  34.5 0.9 copy-done.1
  35.4 0.4 shard_map.127.refs_1_
  35.8 2.6 %collective-permute-start.2 = (f32[88,1056]{1,0:T(8,128)S(1)}, f32[88,1056]{1,0:T(8,128)S(1)}, u32[]{:S(2)}, u32[]{:S(2)}) collective-permute-start(f32[88,1056]{1,0:T(8,128)S(1)} %shard_map.127.refs_1_), channel_id=1, source_target_pairs={{0,32},{8,40},{16,48},{24,56},{32,0},{40,8},{48,16},{56,24},{64,96... | collective-permute-start | bytes 1115144 | tf_op jit(solution)/shard_map/ppermute | solution.py:241
  38.5 0.1 pad_add_fusion.refs_0_
  38.6 9.9 %collective-permute-done.2.refs_2_ = f32[88,1056]{1,0:T(8,128)S(1)} collective-permute-done((f32[88,1056]{1,0:T(8,128)S(1)}, f32[88,1056]{1,0:T(8,128)S(1)}, u32[]{:S(2)}, u32[]{:S(2)}) %collective-permute-start.2) | collective-permute-done | bytes 371744 | tf_op jit(solution)/shard_map/ppermute | solution.py:241
  48.5 2.4 shard_map.128
  50.9 0.0 all-gather.16.cloned.1.call-update
  50.9 0.0 all-gather.18.cloned.1.call-start
  50.9 15.1 %all-gather.1 = f32[704,352]{1,0:T(8,128)S(1)} all-gather(f32[176,352]{1,0:T(8,128)S(1)} %get-tuple-element.37), channel_id=3, replica_groups={{0,8,16,24},{32,40,48,56},{64,72,80,88},{96,104,112,120},{128,136,144,1..., dimensions={0}, use_global_device_ids=true | all-gather | bytes 1239040 | tf_op jit(solution)/shard_map/all_gather | solution.py:253
  66.1 2.1 shard_map.129
  68.2 0.0 all-gather.18.cloned.1.call-update
  68.2 0.0 all-gather.20.cloned.1.call-start
  68.3 4.9 %collective-permute-start.3 = (f32[88,176]{1,0:T(8,128)S(1)}, f32[88,176]{1,0:T(8,128)S(1)}, u32[]{:S(2)}, u32[]{:S(2)}) collective-permute-start(f32[88,176]{1,0:T(8,128)S(1)} %get-tuple-element.40), channel_id=1, source_target_pairs={{0,64},{8,72},{16,80},{24,88},{32,96},{40,104},{48,112},{56,120},{... | collective-permute-start | bytes 185864 | tf_op jit(solution)/shard_map/ppermute | solution.py:241
  73.1 3.9 %collective-permute-start.4 = (f32[88,176]{1,0:T(8,128)S(1)}, f32[88,176]{1,0:T(8,128)S(1)}, u32[]{:S(2)}, u32[]{:S(2)}) collective-permute-start(f32[88,176]{1,0:T(8,128)S(1)} %get-tuple-element.40), channel_id=1, source_target_pairs={{0,32},{8,40},{16,48},{24,56},{32,0},{40,8},{48,16},{56,24},{64,96... | collective-permute-start | bytes 185864 | tf_op jit(solution)/shard_map/ppermute | solution.py:241
  77.1 1.9 collective-permute-start.5
  79.0 0.9 pad_maximum_fusion
  79.9 5.4 %collective-permute-done.5 = f32[88,176]{1,0:T(8,128)S(1)} collective-permute-done((f32[88,176]{1,0:T(8,128)S(1)}, f32[88,176]{1,0:T(8,128)S(1)}, u32[]{:S(2)}, u32[]{:S(2)}) %collective-permute-start.5) | collective-permute-done | bytes 61984 | tf_op jit(solution)/shard_map/ppermute | solution.py:241
  85.3 18.8 %all-gather.2.refs_1_.refs_4_ = f32[16,88,176]{2,1,0:T(8,128)} all-gather(f32[4,88,176]{2,1,0:T(8,128)S(1)} %pad_maximum_fusion.1), channel_id=4, replica_groups={{0,8,16,24},{32,40,48,56},{64,72,80,88},{96,104,112,120},{128,136,144,1..., dimensions={0}, use_global_device_ids=true | all-gather | bytes 1239040 | tf_op jit(solution)/shard_map/all_gather | solution.py:253
  104.1 4.1 %shard_map.130 = (f32[176,176]{1,0:T(8,128)S(1)}, f32[176,176]{1,0:T(8,128)S(1)}, f32[2,176,176]{2,1,0:T(8,128)S(1)}) custom-call(s32[3]{0:T(128)S(1)} %pad_add_fusion.refs_0_, f32[16,88,176]{2,1,0:T(8,128)} %all-gather.2.refs_1_.refs_4_, f32[4,2,176,352]{3,2,1,0:T(8,128)} %bitcast.31, f32[8,176,384]{2,1,0:T(8,128)} %bitcast.37), custom_call_target="tpu_custom_call" | custom-call | flops 261685248 | bytes 8000000 | tf_op jit(solution)/shard_map/pallas_call | solution.py:307
  108.2 0.0 all-gather.20.cloned.1.call-update
  108.3 0.0 reduce-scatter.2.cloned.1.call-start
  108.3 2.8 %collective-permute-start.6 = (f32[2,176,176]{2,1,0:T(8,128)S(1)}, f32[2,176,176]{2,1,0:T(8,128)S(1)}, u32[]{:S(2)}, u32[]{:S(2)}) collective-permute-start(f32[2,176,176]{2,1,0:T(8,128)S(1)} %get-tuple-element.45), channel_id=1, source_target_pairs={{0,32},{8,40},{16,48},{24,56},{32,0},{40,8},{48,16},{56,24},{64,96... | collective-permute-start | bytes 743432 | tf_op jit(solution)/shard_map/ppermute | solution.py:241
  111.2 6.4 %collective-permute-done.6 = f32[2,176,176]{2,1,0:T(8,128)S(1)} collective-permute-done((f32[2,176,176]{2,1,0:T(8,128)S(1)}, f32[2,176,176]{2,1,0:T(8,128)S(1)}, u32[]{:S(2)}, u32[]{:S(2)}) %collective-permute-start.6) | collective-permute-done | bytes 247840 | tf_op jit(solution)/shard_map/ppermute | solution.py:241
  117.7 17.8 %all-gather.5.refs_4_ = f32[8,176,176]{2,1,0:T(8,128)} all-gather(f32[2,176,176]{2,1,0:T(8,128)S(1)} %pad_maximum_fusion.3), channel_id=7, replica_groups={{0,8,16,24},{32,40,48,56},{64,72,80,88},{96,104,112,120},{128,136,144,1..., dimensions={0}, use_global_device_ids=true | all-gather | bytes 1239040 | tf_op jit(solution)/shard_map/all_gather | solution.py:253
  135.6 15.8 %all-gather.4.refs_3_ = f32[8,176,176]{2,1,0:T(8,128)} all-gather(f32[2,176,176]{2,1,0:T(8,128)S(1)} %pad_maximum_fusion.2), channel_id=6, replica_groups={{0,8,16,24},{32,40,48,56},{64,72,80,88},{96,104,112,120},{128,136,144,1..., dimensions={0}, use_global_device_ids=true | all-gather | bytes 1239040 | tf_op jit(solution)/shard_map/all_gather | solution.py:253
  151.4 3.9 %shard_map.133 = f32[4,176,176]{2,1,0:T(8,128)S(1)} custom-call(s32[3]{0:T(128)S(1)} %pad_add_fusion.refs_0_, f32[176,176]{1,0:T(8,128)S(1)} %get-tuple-element.43.refs_7_.refs_1_, f32[176,176]{1,0:T(8,128)S(1)} %get-tuple-element.44.refs_8_.refs_2_, f32[8,176,176]{2,1,0:T(8,128)} %all-gather.4.refs_3_, f32[8,176,176]{2,1,0:T(8,128)} %all-gather.5.refs_4_, ...), custom_call_target="tpu_custom_call" | custom-call | flops 261685248 | bytes 8000000 | tf_op jit(solution)/shard_map/pallas_call | solution.py:307
  155.3 1.9 collective-permute-start.7
  157.3 3.8 %shard_map.132.refs_0_ = f32[4,176,176]{2,1,0:T(8,128)S(1)} custom-call(s32[3]{0:T(128)S(1)} %pad_add_fusion.refs_0_, f32[176,176]{1,0:T(8,128)S(1)} %get-tuple-element.43.refs_7_.refs_1_, f32[176,176]{1,0:T(8,128)S(1)} %get-tuple-element.44.refs_8_.refs_2_, f32[8,176,176]{2,1,0:T(8,128)} %all-gather.4.refs_3_, f32[8,176,176]{2,1,0:T(8,128)} %all-gather.5.refs_4_, ...), custom_call_target="tpu_custom_call" | custom-call | flops 261685248 | bytes 8000000 | tf_op jit(solution)/shard_map/pallas_call | solution.py:307
  161.1 0.1 shard_map.134
  161.2 3.5 %collective-permute-start.10 = (f32[176,176]{1,0:T(8,128)S(1)}, f32[176,176]{1,0:T(8,128)S(1)}, u32[]{:S(2)}, u32[]{:S(2)}) collective-permute-start(f32[176,176]{1,0:T(8,128)S(1)} %get-tuple-element.49), channel_id=1, source_target_pairs={{0,4},{1,5},{2,6},{3,7},{4,0},{5,1},{6,2},{7,3},{8,12},{9,13},{10,... | collective-permute-start | bytes 371720 | tf_op jit(solution)/shard_map/ppermute | solution.py:250
  164.7 4.0 %collective-permute-start.8 = (f32[176,176]{1,0:T(8,128)S(1)}, f32[176,176]{1,0:T(8,128)S(1)}, u32[]{:S(2)}, u32[]{:S(2)}) collective-permute-start(f32[176,176]{1,0:T(8,128)S(1)} %get-tuple-element.47), channel_id=1, source_target_pairs={{0,2},{1,3},{2,4},{3,5},{4,6},{5,7},{6,0},{7,1},{8,10},{9,11},{10,... | collective-permute-start | bytes 371720 | tf_op jit(solution)/shard_map/ppermute | solution.py:250
  168.6 1.9 collective-permute-start.9
  170.6 6.9 %shard_map.131 = f32[8,176,396]{2,1,0:T(8,128)} custom-call(s32[3]{0:T(128)S(1)} %pad_add_fusion.refs_0_, f32[4,176,352]{2,1,0:T(8,128)S(1)} %bitcast.20, f32[44,176]{1,0:T(8,128)S(1)} %bitcast.24, f32[176,88]{1,0:T(8,128)S(1)} %get-tuple-element.39.refs_3_, f32[16,88,176]{2,1,0:T(8,128)} %all-gather.2.refs_1_.refs_4_, f32[4,2,176,352]{3,2,1,0:T(8,128)} %bitcast.34, ...), custom_call_target="tpu_custom_call" | custom-call | flops 523370496 | bytes 8000000 | tf_op jit(solution)/shard_map/pallas_call | solution.py:307
  177.5 0.6 collective-permute-done.9.refs_2_
  178.1 0.7 shard_map.135
  178.8 0.0 reduce-scatter.2.cloned.1.call-update
  178.9 2.6 %collective-permute-start.11 = (f32[176,176]{1,0:T(8,128)S(1)}, f32[176,176]{1,0:T(8,128)S(1)}, u32[]{:S(2)}, u32[]{:S(2)}) collective-permute-start(f32[176,176]{1,0:T(8,128)S(1)} %get-tuple-element.57), channel_id=1, source_target_pairs={{0,32},{8,40},{16,48},{24,56},{32,0},{40,8},{48,16},{56,24},{64,96... | collective-permute-start | bytes 371720 | tf_op jit(solution)/shard_map/ppermute | solution.py:241
  181.5 5.1 %collective-permute-done.11 = f32[176,176]{1,0:T(8,128)S(1)} collective-permute-done((f32[176,176]{1,0:T(8,128)S(1)}, f32[176,176]{1,0:T(8,128)S(1)}, u32[]{:S(2)}, u32[]{:S(2)}) %collective-permute-start.11) | collective-permute-done | bytes 123936 | tf_op jit(solution)/shard_map/ppermute | solution.py:241
  186.6 17.5 %all-gather.6.refs_1_ = f32[8,176,176]{2,1,0:T(8,128)} all-gather(f32[2,176,176]{2,1,0:T(8,128)S(1)} %pad_maximum_fusion.4), channel_id=8, replica_groups={{0,8,16,24},{32,40,48,56},{64,72,80,88},{96,104,112,120},{128,136,144,1..., dimensions={0}, use_global_device_ids=true | all-gather | bytes 1239040 | tf_op jit(solution)/shard_map/all_gather | solution.py:253
  204.2 6.2 %shard_map.137 = (f32[176,352]{1,0:T(8,128)}, f32[4,176,352]{2,1,0:T(8,128)S(1)}) custom-call(s32[3]{0:T(128)S(1)} %pad_add_fusion.refs_0_, f32[8,176,176]{2,1,0:T(8,128)} %all-gather.6.refs_1_, f32[8,176,352]{2,1,0:T(8,128)} %bitcast.39, f32[4,2,176,352]{3,2,1,0:T(8,128)} %bitcast.27, f32[4,2,176,352]{3,2,1,0:T(8,128)} %bitcast.28, f32[176,352]{1,0:T(8,128)S(1)} %copy-done), custom_call_target="tpu_custom_call" | custom-call | flops 523370496 | bytes 8000000 | tf_op jit(solution)/shard_map/pallas_call | solution.py:307
  210.3 1.9 collective-permute-start.12
  212.3 0.9 copy-done.6
  213.2 3.9 %shard_map.138.refs_0_ = f32[4,176,352]{2,1,0:T(8,128)S(1)} custom-call(s32[3]{0:T(128)S(1)} %pad_add_fusion.refs_0_, f32[176,352]{1,0:T(8,128)S(1)} %copy-done.6, f32[4,2,176,352]{3,2,1,0:T(8,128)} %bitcast.29, f32[4,2,176,352]{3,2,1,0:T(8,128)} %bitcast.30, f32[176,352]{1,0:T(8,128)S(1)} %copy-done), custom_call_target="tpu_custom_call" | custom-call | flops 261685248 | bytes 8000000 | tf_op jit(solution)/shard_map/pallas_call | solution.py:307
  217.1 0.1 shard_map.139
  217.3 4.6 %collective-permute-start.13 = (f32[176,352]{1,0:T(8,128)S(1)}, f32[176,352]{1,0:T(8,128)S(1)}, u32[]{:S(2)}, u32[]{:S(2)}) collective-permute-start(f32[176,352]{1,0:T(8,128)S(1)} %get-tuple-element.63), channel_id=1, source_target_pairs={{0,2},{1,3},{2,4},{3,5},{4,6},{5,7},{6,0},{7,1},{8,10},{9,11},{10,... | collective-permute-start | bytes 743432 | tf_op jit(solution)/shard_map/ppermute | solution.py:250
  221.9 1.9 collective-permute-start.14
  223.8 3.4 %collective-permute-start.15 = (f32[176,352]{1,0:T(8,128)S(1)}, f32[176,352]{1,0:T(8,128)S(1)}, u32[]{:S(2)}, u32[]{:S(2)}) collective-permute-start(f32[176,352]{1,0:T(8,128)S(1)} %get-tuple-element.65), channel_id=1, source_target_pairs={{0,4},{1,5},{2,6},{3,7},{4,0},{5,1},{6,2},{7,3},{8,12},{9,13},{10,... | collective-permute-start | bytes 743432 | tf_op jit(solution)/shard_map/ppermute | solution.py:250
  227.2 1.1 collective-permute-done.13.refs_1_
  228.3 11.1 %collective-permute-done.14.refs_2_ = f32[176,352]{1,0:T(8,128)S(1)} collective-permute-done((f32[176,352]{1,0:T(8,128)S(1)}, f32[176,352]{1,0:T(8,128)S(1)}, u32[]{:S(2)}, u32[]{:S(2)}) %collective-permute-start.14) | collective-permute-done | bytes 247840 | tf_op jit(solution)/shard_map/ppermute | solution.py:250
  239.4 0.9 shard_map.140
  240.3 0.0 reduce-scatter.2.cloned.1.call-done.refs_0_
  240.4 1.0 copy-done.3
  241.3 0.9 shard_map.136
  (32 shorter events, 0.2 us)
Async XLA Ops:
  7.2 41.3 %all-gather.14.cloned.1.call-start = ((), (), s32[]{:S(2)}) async-start(), calls=%async_computation.2 | async-start | bytes 2433024 | tf_op jit(solution)/shard_map/all_gather | solution.py:337
  8.9 95.2 %all-gather.16.cloned.1.call-start = ((), (), s32[]{:S(2)}) async-start(), calls=%async_computation.3 | async-start | bytes 2703360 | tf_op jit(solution)/shard_map/all_gather | solution.py:253
  9.0 11.4 %collective-permute-start = (f32[44,176]{1,0:T(8,128)}, f32[44,176]{1,0:T(8,128)S(1)}, u32[]{:S(2)}, u32[]{:S(2)}) collective-permute-start(f32[44,176]{1,0:T(8,128)} %bitcast.22), channel_id=1, source_target_pairs={{0,128},{8,136},{16,144},{24,152},{32,160},{40,168},{48,176},{56,1... | collective-permute-start | bytes 92936 | tf_op jit(solution)/shard_map/ppermute | solution.py:241
  20.4 0.9 copy-start.4
  21.2 0.8 copy-start.7
  22.4 12.1 %collective-permute-start.1 = (f32[88,352]{1,0:T(8,128)S(1)}, f32[88,352]{1,0:T(8,128)S(1)}, u32[]{:S(2)}, u32[]{:S(2)}) collective-permute-start(f32[88,352]{1,0:T(8,128)S(1)} %shard_map.126.refs_0_), channel_id=1, source_target_pairs={{0,64},{8,72},{16,80},{24,88},{32,96},{40,104},{48,112},{56,120},{... | collective-permute-start | bytes 371720 | tf_op jit(solution)/shard_map/ppermute | solution.py:241
  34.4 0.9 copy-start.1
  35.8 12.7 %collective-permute-start.2 = (f32[88,1056]{1,0:T(8,128)S(1)}, f32[88,1056]{1,0:T(8,128)S(1)}, u32[]{:S(2)}, u32[]{:S(2)}) collective-permute-start(f32[88,1056]{1,0:T(8,128)S(1)} %shard_map.127.refs_1_), channel_id=1, source_target_pairs={{0,32},{8,40},{16,48},{24,56},{32,0},{40,8},{48,16},{56,24},{64,96... | collective-permute-start | bytes 1115144 | tf_op jit(solution)/shard_map/ppermute | solution.py:241
  50.9 153.3 %all-gather.18.cloned.1.call-start = ((), (), s32[]{:S(2)}) async-start(), calls=%async_computation.4 | async-start | bytes 2433024 | tf_op jit(solution)/shard_map/all_gather | solution.py:381
  66.1 12.9 %copy-start = (f32[176,352]{1,0:T(8,128)S(1)}, f32[176,352]{1,0:T(8,128)}, u32[]{:S(2)}) copy-start(f32[176,352]{1,0:T(8,128)} %refs_4_.1) | copy-start | bytes 743428
  66.1 12.9 %copy-start.9 = (f32[176,352]{1,0:T(8,128)S(1)}, f32[176,352]{1,0:T(8,128)}, u32[]{:S(2)}) copy-start(f32[176,352]{1,0:T(8,128)} %param.10) | copy-start | bytes 743428
  68.2 135.9 %all-gather.20.cloned.1.call-start = ((), (), s32[]{:S(2)}) async-start(), calls=%async_computation.5 | async-start | bytes 2703360 | tf_op jit(solution)/shard_map/all_gather | solution.py:253
  68.3 11.6 %collective-permute-start.3 = (f32[88,176]{1,0:T(8,128)S(1)}, f32[88,176]{1,0:T(8,128)S(1)}, u32[]{:S(2)}, u32[]{:S(2)}) collective-permute-start(f32[88,176]{1,0:T(8,128)S(1)} %get-tuple-element.40), channel_id=1, source_target_pairs={{0,64},{8,72},{16,80},{24,88},{32,96},{40,104},{48,112},{56,120},{... | collective-permute-start | bytes 185864 | tf_op jit(solution)/shard_map/ppermute | solution.py:241
  73.1 6.7 %collective-permute-start.4 = (f32[88,176]{1,0:T(8,128)S(1)}, f32[88,176]{1,0:T(8,128)S(1)}, u32[]{:S(2)}, u32[]{:S(2)}) collective-permute-start(f32[88,176]{1,0:T(8,128)S(1)} %get-tuple-element.40), channel_id=1, source_target_pairs={{0,32},{8,40},{16,48},{24,56},{32,0},{40,8},{48,16},{56,24},{64,96... | collective-permute-start | bytes 185864 | tf_op jit(solution)/shard_map/ppermute | solution.py:241
  77.1 8.2 %collective-permute-start.5 = (f32[88,176]{1,0:T(8,128)S(1)}, f32[88,176]{1,0:T(8,128)S(1)}, u32[]{:S(2)}, u32[]{:S(2)}) collective-permute-start(f32[88,176]{1,0:T(8,128)S(1)} %get-tuple-element.40), channel_id=1, source_target_pairs={{0,96},{8,104},{16,112},{24,120},{32,64},{40,72},{48,80},{56,88},{... | collective-permute-start | bytes 185864 | tf_op jit(solution)/shard_map/ppermute | solution.py:241
  108.3 132.1 %reduce-scatter.2.cloned.1.call-start = ((), (), s32[]{:S(2)}) async-start(), calls=%async_computation.1 | async-start | bytes 3244032 | tf_op jit(solution)/shard_map/reduce_scatter | solution.py:430
  108.3 9.3 %collective-permute-start.6 = (f32[2,176,176]{2,1,0:T(8,128)S(1)}, f32[2,176,176]{2,1,0:T(8,128)S(1)}, u32[]{:S(2)}, u32[]{:S(2)}) collective-permute-start(f32[2,176,176]{2,1,0:T(8,128)S(1)} %get-tuple-element.45), channel_id=1, source_target_pairs={{0,32},{8,40},{16,48},{24,56},{32,0},{40,8},{48,16},{56,24},{64,96... | collective-permute-start | bytes 743432 | tf_op jit(solution)/shard_map/ppermute | solution.py:241
  117.7 33.7 %copy-start.2 = (f32[176,176]{1,0:T(8,128)S(1)}, f32[176,176]{1,0:T(8,128)}, u32[]{:S(2)}) copy-start(f32[176,176]{1,0:T(8,128)} %refs_6_.5) | copy-start | bytes 371716
  155.3 5.7 %collective-permute-start.7 = (f32[4,176,176]{2,1,0:T(8,128)S(1)}, f32[4,176,176]{2,1,0:T(8,128)S(1)}, u32[]{:S(2)}, u32[]{:S(2)}) collective-permute-start(f32[4,176,176]{2,1,0:T(8,128)S(1)} %shard_map.133), channel_id=1, source_target_pairs={{0,1},{1,0},{2,3},{3,2},{4,5},{5,4},{6,7},{7,6},{8,9},{9,8},{10,11... | collective-permute-start | bytes 1486856 | tf_op jit(solution)/shard_map/ppermute | solution.py:244
  161.0 9.5 %copy-start.5 = (f32[176,88]{1,0:T(8,128)S(1)}, f32[176,88]{1,0:T(8,128)}, u32[]{:S(2)}) copy-start(f32[176,88]{1,0:T(8,128)} %refs_6_.3) | copy-start | bytes 185860
  161.1 9.5 %copy-start.8 = (f32[176,44]{0,1:T(8,128)S(1)}, f32[176,44]{0,1:T(8,128)}, u32[]{:S(2)}) copy-start(f32[176,44]{0,1:T(8,128)} %param.7) | copy-start | bytes 92932
  161.2 16.4 %collective-permute-start.10 = (f32[176,176]{1,0:T(8,128)S(1)}, f32[176,176]{1,0:T(8,128)S(1)}, u32[]{:S(2)}, u32[]{:S(2)}) collective-permute-start(f32[176,176]{1,0:T(8,128)S(1)} %get-tuple-element.49), channel_id=1, source_target_pairs={{0,4},{1,5},{2,6},{3,7},{4,0},{5,1},{6,2},{7,3},{8,12},{9,13},{10,... | collective-permute-start | bytes 371720 | tf_op jit(solution)/shard_map/ppermute | solution.py:250
  164.7 12.9 %collective-permute-start.8 = (f32[176,176]{1,0:T(8,128)S(1)}, f32[176,176]{1,0:T(8,128)S(1)}, u32[]{:S(2)}, u32[]{:S(2)}) collective-permute-start(f32[176,176]{1,0:T(8,128)S(1)} %get-tuple-element.47), channel_id=1, source_target_pairs={{0,2},{1,3},{2,4},{3,5},{4,6},{5,7},{6,0},{7,1},{8,10},{9,11},{10,... | collective-permute-start | bytes 371720 | tf_op jit(solution)/shard_map/ppermute | solution.py:250
  168.6 9.5 %collective-permute-start.9 = (f32[176,176]{1,0:T(8,128)S(1)}, f32[176,176]{1,0:T(8,128)S(1)}, u32[]{:S(2)}, u32[]{:S(2)}) collective-permute-start(f32[176,176]{1,0:T(8,128)S(1)} %get-tuple-element.48), channel_id=1, source_target_pairs={{0,6},{1,7},{2,0},{3,1},{4,2},{5,3},{6,4},{7,5},{8,14},{9,15},{10,... | collective-permute-start | bytes 371720 | tf_op jit(solution)/shard_map/ppermute | solution.py:250
  178.9 7.7 %collective-permute-start.11 = (f32[176,176]{1,0:T(8,128)S(1)}, f32[176,176]{1,0:T(8,128)S(1)}, u32[]{:S(2)}, u32[]{:S(2)}) collective-permute-start(f32[176,176]{1,0:T(8,128)S(1)} %get-tuple-element.57), channel_id=1, source_target_pairs={{0,32},{8,40},{16,48},{24,56},{32,0},{40,8},{48,16},{56,24},{64,96... | collective-permute-start | bytes 371720 | tf_op jit(solution)/shard_map/ppermute | solution.py:241
  210.3 6.8 %collective-permute-start.12 = (f32[4,176,352]{2,1,0:T(8,128)S(1)}, f32[4,176,352]{2,1,0:T(8,128)S(1)}, u32[]{:S(2)}, u32[]{:S(2)}) collective-permute-start(f32[4,176,352]{2,1,0:T(8,128)S(1)} %get-tuple-element.61), channel_id=1, source_target_pairs={{0,1},{1,0},{2,3},{3,2},{4,5},{5,4},{6,7},{7,6},{8,9},{9,8},{10,11... | collective-permute-start | bytes 2973704 | tf_op jit(solution)/shard_map/ppermute | solution.py:244
  212.3 1.0 copy-start.6
  217.3 11.0 %collective-permute-start.13 = (f32[176,352]{1,0:T(8,128)S(1)}, f32[176,352]{1,0:T(8,128)S(1)}, u32[]{:S(2)}, u32[]{:S(2)}) collective-permute-start(f32[176,352]{1,0:T(8,128)S(1)} %get-tuple-element.63), channel_id=1, source_target_pairs={{0,2},{1,3},{2,4},{3,5},{4,6},{5,7},{6,0},{7,1},{8,10},{9,11},{10,... | collective-permute-start | bytes 743432 | tf_op jit(solution)/shard_map/ppermute | solution.py:250
  221.9 17.5 %collective-permute-start.14 = (f32[176,352]{1,0:T(8,128)S(1)}, f32[176,352]{1,0:T(8,128)S(1)}, u32[]{:S(2)}, u32[]{:S(2)}) collective-permute-start(f32[176,352]{1,0:T(8,128)S(1)} %get-tuple-element.64), channel_id=1, source_target_pairs={{0,6},{1,7},{2,0},{3,1},{4,2},{5,3},{6,4},{7,5},{8,14},{9,15},{10,... | collective-permute-start | bytes 743432 | tf_op jit(solution)/shard_map/ppermute | solution.py:250
  223.8 15.6 %collective-permute-start.15 = (f32[176,352]{1,0:T(8,128)S(1)}, f32[176,352]{1,0:T(8,128)S(1)}, u32[]{:S(2)}, u32[]{:S(2)}) collective-permute-start(f32[176,352]{1,0:T(8,128)S(1)} %get-tuple-element.65), channel_id=1, source_target_pairs={{0,4},{1,5},{2,6},{3,7},{4,0},{5,1},{6,2},{7,3},{8,12},{9,13},{10,... | collective-permute-start | bytes 743432 | tf_op jit(solution)/shard_map/ppermute | solution.py:250
  240.3 1.0 copy-start.3
Sparse Core Ops, SparseCore 0:
  10.7 36.2 all-gather.13
  51.0 42.3 all-gather.15
  95.5 35.9 all-gather.17
  133.5 40.5 all-gather.19
  179.0 39.0 reduce-scatter.1
